TPU v7x, 32 devices: a whole 2x2x4 slice. The times are simulated.
32 devices in a mesh: user: 16 (over z, y, core), item: 2 (over x).
Axes of the slice: x: 2, y: 2, z: 4, core: 2. Of those that a mesh axis runs over, the one named last changes fastest.
Arguments:
- tile_vals: bfloat16 [16, 2, 128, 128, 128], P('user', 'item'), may hold values from -6 to 6
- tile_row: int32 [16, 2, 128], P('user', 'item'), may hold values from 0 to 15, as said below
- tile_col: int32 [16, 2, 128], P('user', 'item'), may hold values from 0 to 15
- tile_count: int32 [16, 2], P('user', 'item'), may hold values from 16 to 128, as said below
- fac_a: bfloat16 [64, 32768], P(None, 'user'), may hold values from -2.5 to 2.5
- fac_b: bfloat16 [64, 4096], P(None, ('item', 'user')), may hold values from -2.5 to 2.5
- omega: bfloat16 [64, 4096], P(None, ('item', 'user')), may hold values from -6 to 6
Outputs:
- user_dir: float32 [64, 32768], P(None, 'user')
- item_dir: float32 [64, 4096], P(None, ('item', 'user'))
- row_loss: float32 [16, 2, 128, 128], P('user', 'item')
Inputs may be any that keep to these rules, and one draw needn't show every extreme that they name: `tile_count`: slot s of a device is used when s is under its count. Counts tend to grow with the user index, and some device of the last user index has all 128 slots used. The slots of one device name distinct (tile_row, tile_col) pairs.
All inputs are finite; a program needn't handle non-finite values.
Results may differ from a plain program's by a relative error of at most 0.0055.
Values may be sent and summed in bfloat16 or wider, within the bound.
No kernel may reach another device: no remote copies, remote signals or barrier semaphores. Data moves between devices by JAX's collectives and lax.ppermute only.
A program may use at most 64 MiB of HBM per device.

v0:
```python
import math

import jax
import jax.numpy as jnp
from jax import lax
from jax.sharding import PartitionSpec as P

ITERS = 2


def tiles_of(mat, tile):
    return mat.reshape(mat.shape[0], -1, tile).transpose(1, 0, 2)


def untile(stack):
    return stack.transpose(1, 0, 2).reshape(stack.shape[1], -1)


def gram_of(mat):
    return jnp.dot(mat, mat.T, precision=lax.Precision.HIGHEST)


def orthonormal(mat, gram):
    chol = jnp.linalg.cholesky(gram)
    inverse = lax.linalg.triangular_solve(
        chol, jnp.eye(gram.shape[0], dtype=jnp.float32), left_side=True, lower=True
    )
    return jnp.dot(inverse, mat, precision=lax.Precision.HIGHEST)


def spread_add(total, index, part):
    onehot = (index[:, None] == jnp.arange(total.shape[0], dtype=jnp.int32)[None, :]).astype(
        jnp.float32
    )
    return total + jnp.einsum(
        "wu,wkr->ukr",
        onehot,
        part,
        precision=lax.Precision.HIGHEST,
        preferred_element_type=jnp.float32,
    )


def shards(tile_vals, tile_row, tile_col, tile_count, fac_a, fac_b, omega):
    ratings = tile_vals[0, 0]
    slot_rows = tile_row[0, 0]
    slot_cols = tile_col[0, 0]
    count = tile_count[0, 0]
    cap = ratings.shape[0]
    tile = ratings.shape[1]
    rank = fac_a.shape[0]
    users_dev = fac_a.shape[1]
    width = min(16, cap)
    blocks = (count + width - 1) // width
    valid = (jnp.arange(cap, dtype=jnp.int32) < count).astype(jnp.float32)
    b_block, q_full = (
        lax.all_gather(fac_b, "user", axis=1, tiled=True),
        lax.all_gather(omega, "user", axis=1, tiled=True),
    )
    a_tiles = tiles_of(fac_a, tile)
    b_tiles = tiles_of(b_block, tile)
    user_tiles = a_tiles.shape[0]
    item_tiles = b_tiles.shape[0]
    n_user = lax.axis_size("user")
    n_item = lax.axis_size("item")
    users = users_dev * n_user
    items = b_block.shape[1] * n_item

    def window(index):
        start = index * width
        rows_now = lax.dynamic_slice_in_dim(slot_rows, start, width)
        cols_now = lax.dynamic_slice_in_dim(slot_cols, start, width)
        kept = lax.dynamic_slice_in_dim(valid, start, width)
        return (start, rows_now, cols_now, kept)

    def predict(rows_now, cols_now):
        return jnp.einsum(
            "wkr,wki->wri", a_tiles[rows_now], b_tiles[cols_now], preferred_element_type=jnp.float32
        )

    def residual_step(index, buffer):
        start, rows_now, cols_now, kept = window(index)
        seen = lax.dynamic_slice_in_dim(ratings, start, width).astype(jnp.float32)
        fresh = ((predict(rows_now, cols_now) - seen) * kept[:, None, None]).astype(jnp.bfloat16)
        return lax.dynamic_update_slice_in_dim(buffer, fresh, start, 0)

    resid = lax.fori_loop(0, blocks, residual_step, jnp.zeros((cap, tile, tile), jnp.bfloat16))

    def user_side(q_mat):
        q_tiles = tiles_of(q_mat, tile)

        def user_step_fn(index, total):
            start, rows_now, cols_now, kept = window(index)
            piece = lax.dynamic_slice_in_dim(resid, start, width)
            part = jnp.einsum(
                "wki,wri->wkr", q_tiles[cols_now], piece, preferred_element_type=jnp.float32
            )
            return spread_add(total, rows_now, part * kept[:, None, None])

        total = lax.fori_loop(
            0, blocks, user_step_fn, jnp.zeros((user_tiles, rank, tile), jnp.float32)
        )
        return untile(total)

    def item_side(y_mat):
        y_tiles = tiles_of(y_mat, tile)

        def item_step_fn(index, total):
            start, rows_now, cols_now, kept = window(index)
            piece = lax.dynamic_slice_in_dim(resid, start, width)
            part = jnp.einsum(
                "wkr,wri->wki", y_tiles[rows_now], piece, preferred_element_type=jnp.float32
            )
            return spread_add(total, cols_now, part * kept[:, None, None])

        total = lax.fori_loop(
            0, blocks, item_step_fn, jnp.zeros((item_tiles, rank, tile), jnp.float32)
        )
        return untile(total)

    y_hat = None
    q_share = None
    for step in range(ITERS):
        y_part = user_side(q_full)
        y_sum = lax.psum(y_part, "item")
        gram = lax.psum(gram_of(y_sum), "user")
        y_hat = orthonormal(y_sum, gram).astype(jnp.bfloat16)
        z_part = item_side(y_hat)
        z_share = lax.psum_scatter(z_part, "user", scatter_dimension=1, tiled=True)
        gram = lax.psum(gram_of(z_share), ("user", "item"))
        q_share = orthonormal(z_share, gram).astype(jnp.bfloat16)
        q_full = lax.all_gather(q_share, "user", axis=1, tiled=True)
    y_last = tiles_of(y_hat, tile)
    q_last = tiles_of(q_full, tile)
    radius = math.sqrt(users * items / rank)

    def loss_step(index, buffer):
        start, rows_now, cols_now, kept = window(index)
        seen = lax.dynamic_slice_in_dim(ratings, start, width).astype(jnp.float32)
        atom = jnp.einsum(
            "wkr,wki->wri", y_last[rows_now], q_last[cols_now], preferred_element_type=jnp.float32
        )
        fresh = 0.5 * predict(rows_now, cols_now) - 0.5 * radius * atom - seen
        values = jnp.mean(fresh * fresh, axis=-1) * kept[:, None]
        return lax.dynamic_update_slice_in_dim(buffer, values, start, 0)

    losses = lax.fori_loop(0, blocks, loss_step, jnp.zeros((cap, tile), jnp.float32))
    user_dir = y_hat.astype(jnp.float32) * math.sqrt(users)
    item_dir = q_share.astype(jnp.float32) * math.sqrt(items)
    return (user_dir, item_dir, losses[None, None])


def solution(mesh):
    return jax.shard_map(
        shards,
        mesh=mesh,
        in_specs=(
            P("user", "item", None, None, None),
            P("user", "item", None),
            P("user", "item", None),
            P("user", "item"),
            P(None, "user"),
            P(None, ("item", "user")),
            P(None, ("item", "user")),
        ),
        out_specs=(P(None, "user"), P(None, ("item", "user")), P("user", "item", None, None)),
        check_vma=False,
    )
```

profile of v0, /device:TPU:29, one launch (start us, length us, event | category | flops | bytes accessed | tf_op | source)
XLA Modules:
  0.0 679.5 jit_solution(10981339302209044932)
XLA Ops:
  7.9 17.7 %all_gather.13 = bf16[64,2048]{1,0:T(8,128)(2,1)S(1)} all-gather(bf16[64,128]{1,0:T(8,128)(2,1)} %param.27), channel_id=1, replica_groups=mesh['user'=16,'item'=2] {'user'}, dimensions={1}, use_global_device_ids=true | all-gather | bytes 278528 | tf_op jit(solution)/shard_map/all_gather | solution.py:57
  26.8 3.0 broadcast_in_dim.42
  29.8 28.8 %while.60 = (s32[]{:T(128)}, bf16[128,128,128]{2,1,0:T(8,128)(2,1)}, s32[]{:T(128)}, s32[128]{0:T(128)S(1)}, bf16[16,64,128]{2,1,0:T(8,128)(2,1)S(1)}, /*index=5...) while((s32[]{:T(128)}, ...), condition=%wide.region_1.2_spmd, body=%wide.region_0.1_spmd.sunk | while | flops 34605156 | bytes 2630519 | solution.py:87
  34.8 2.2 fusion.119
  38.4 2.2 fusion.119
  56.4 2.2 fusion.119
  58.6 15.6 %all_gather.12 = bf16[64,2048]{1,0:T(8,128)(2,1)S(1)} all-gather(bf16[64,128]{1,0:T(8,128)(2,1)S(1)} %copy-done.3), channel_id=1, replica_groups=mesh['user'=16,'item'=2] {'user'}, dimensions={1}, use_global_device_ids=true | all-gather | bytes 278528 | tf_op jit(solution)/shard_map/all_gather | solution.py:58
  74.4 25.3 %while.61 = (s32[]{:T(128)}, f32[16,64,128]{2,0,1:T(8,128)S(1)}, s32[]{:T(128)}, s32[128]{0:T(128)S(1)}, s32[128]{0:T(128)S(1)}, /*index=5*/bf16[16,64,128]{2,1,...) while((s32[]{:T(128)}, f32[16,64,128]{2,0,1:T(8,128)S(1)}, ...), condition=%wide.region_3.4_spmd, body=%wide.region_2.3_spmd.sunk | while | flops 58983732 | bytes 3412787 | solution.py:100
  100.7 29.1 %all-reduce.3.cloned.1.call-done = f32[64,2048]{1,0:T(8,128)} async-done(((f32[64,2048]{1,0:T(8,128)}), f32[64,2048]{1,0:T(8,128)}) %all-reduce.3.cloned.1.call-update) | async-done | bytes 524304 | tf_op jit(solution)/shard_map/psum | solution.py:125
  131.6 57.0 %psum.43 = f32[64,64]{0,1:T(8,128)S(1)} all-reduce(f32[64,64]{0,1:T(8,128)S(1)} %fusion.60), channel_id=1, replica_groups=mesh['user'=16,'item'=2] {'user'}, use_global_device_ids=true, to_apply=%region_5.6 | all-reduce | flops 4096 | bytes 32768 | tf_op jit(solution)/shard_map/psum | solution.py:126
  188.7 5.8 cholesky.74
  195.9 4.9 custom-call.8
  202.8 23.8 %while.62 = (s32[]{:T(128)}, f32[16,64,128]{2,0,1:T(8,128)S(1)}, s32[]{:T(128)}, s32[128]{0:T(128)S(1)}, s32[128]{0:T(128)S(1)}, /*index=5*/bf16[16,64,128]{2,1,...) while((s32[]{:T(128)}, f32[16,64,128]{2,0,1:T(8,128)S(1)}, ...), condition=%wide.region_9.12_spmd, body=%wide.region_8.11_spmd.sunk | while | flops 58983732 | bytes 3412787 | solution.py:116
  227.6 51.8 %reduce-scatter.3.cloned.1.call-done = f32[64,128]{1,0:T(8,128)} async-done(((f32[64,2048]{1,0:T(8,128)}), f32[64,128]{1,0:T(8,128)}) %reduce-scatter.3.cloned.1.call-update) | async-done | bytes 32784 | tf_op jit(solution)/shard_map/reduce_scatter | solution.py:129
  280.5 41.1 %psum.44 = f32[64,64]{0,1:T(8,128)S(1)} all-reduce(f32[64,64]{0,1:T(8,128)S(1)} %fusion.61), channel_id=1, replica_groups=mesh['user'=16,'item'=2] {'user','item'}, use_global_device_ids=true, to_apply=%region_11.14 | all-reduce | flops 4096 | bytes 32768 | tf_op jit(solution)/shard_map/psum | solution.py:130
  321.6 5.8 cholesky.85
  328.8 4.9 custom-call.9
  334.9 19.2 %all_gather.14 = bf16[64,2048]{1,0:T(8,128)(2,1)S(1)} all-gather(bf16[64,128]{1,0:T(8,128)(2,1)S(1)} %convolution_convert_fusion.3), channel_id=1, replica_groups=mesh['user'=16,'item'=2] {'user'}, dimensions={1}, use_global_device_ids=true | all-gather | bytes 278528 | tf_op jit(solution)/shard_map/all_gather | solution.py:132
  354.2 25.5 %while.63 = (s32[]{:T(128)}, f32[16,64,128]{2,0,1:T(8,128)S(1)}, s32[]{:T(128)}, s32[128]{0:T(128)S(1)}, s32[128]{0:T(128)S(1)}, /*index=5*/bf16[16,64,128]{2,1,...) while((s32[]{:T(128)}, f32[16,64,128]{2,0,1:T(8,128)S(1)}, ...), condition=%wide.region_13.16_spmd, body=%wide.region_12.15_spmd.sunk | while | flops 58983732 | bytes 3412787 | solution.py:100
  380.8 29.5 %all-reduce.5.cloned.1.call-done = f32[64,2048]{1,0:T(8,128)} async-done(((f32[64,2048]{1,0:T(8,128)}), f32[64,2048]{1,0:T(8,128)}) %all-reduce.5.cloned.1.call-update) | async-done | bytes 524304 | tf_op jit(solution)/shard_map/psum | solution.py:125
  412.1 57.0 %psum.46 = f32[64,64]{0,1:T(8,128)S(1)} all-reduce(f32[64,64]{0,1:T(8,128)S(1)} %fusion.62), channel_id=1, replica_groups=mesh['user'=16,'item'=2] {'user'}, use_global_device_ids=true, to_apply=%region_15.18 | all-reduce | flops 4096 | bytes 32768 | tf_op jit(solution)/shard_map/psum | solution.py:126
  469.2 5.8 cholesky.96
  476.3 4.9 custom-call.10
  481.5 2.4 convert_multiply_fusion
  484.0 23.8 %while.64 = (s32[]{:T(128)}, f32[16,64,128]{2,0,1:T(8,128)S(1)}, s32[]{:T(128)}, s32[128]{0:T(128)S(1)}, s32[128]{0:T(128)S(1)}, /*index=5*/bf16[16,64,128]{2,1,...) while((s32[]{:T(128)}, f32[16,64,128]{2,0,1:T(8,128)S(1)}, ...), condition=%wide.region_17.20_spmd, body=%wide.region_16.19_spmd.sunk | while | flops 58983732 | bytes 3412787 | solution.py:116
  508.8 6.4 copy.24
  515.2 45.5 %reduce-scatter.5.cloned.1.call-done = f32[64,128]{1,0:T(8,128)} async-done(((f32[64,2048]{1,0:T(8,128)}), f32[64,128]{1,0:T(8,128)}) %reduce-scatter.5.cloned.1.call-update) | async-done | bytes 32784 | tf_op jit(solution)/shard_map/reduce_scatter | solution.py:129
  561.7 41.1 %psum.47 = f32[64,64]{0,1:T(8,128)S(1)} all-reduce(f32[64,64]{0,1:T(8,128)S(1)} %fusion.63), channel_id=1, replica_groups=mesh['user'=16,'item'=2] {'user','item'}, use_global_device_ids=true, to_apply=%region_19.0 | all-reduce | flops 4096 | bytes 32768 | tf_op jit(solution)/shard_map/psum | solution.py:130
  602.9 5.8 cholesky.107
  610.1 4.9 custom-call.11
  616.8 19.2 %all_gather.15 = bf16[64,2048]{1,0:T(8,128)(2,1)S(1)} all-gather(bf16[64,128]{1,0:T(8,128)(2,1)S(1)} %get-tuple-element.437), channel_id=1, replica_groups=mesh['user'=16,'item'=2] {'user'}, dimensions={1}, use_global_device_ids=true | all-gather | bytes 278528 | tf_op jit(solution)/shard_map/all_gather | solution.py:132
  636.0 36.3 %while.65 = (s32[]{:T(128)}, f32[128,128]{1,0:T(8,128)S(1)}, s32[]{:T(128)}, s32[128]{0:T(128)S(1)}, bf16[16,64,128]{2,1,0:T(8,128)(2,1)S(1)}, /*index=5*/s32[12...) while((s32[]{:T(128)}, f32[128,128]{1,0:T(8,128)S(1)}, ...), condition=%wide.region_22.25_spmd, body=%wide.region_20.0_spmd.sunk | while | flops 68946032 | bytes 5801419 | solution.py:147
  (432 shorter events, 177.3 us)
Async XLA Ops:
  7.2 22.6 %copy-start.1 = (s32[1,1,128]{2,1,0:T(1,128)S(1)}, s32[1,1,128]{2,1,0:T(1,128)}, u32[]{:S(2)}) copy-start(s32[1,1,128]{2,1,0:T(1,128)} %param.23) | copy-start | bytes 1540
  7.2 22.6 %copy-start.2 = (s32[1,1,128]{2,1,0:T(1,128)S(1)}, s32[1,1,128]{2,1,0:T(1,128)}, u32[]{:S(2)}) copy-start(s32[1,1,128]{2,1,0:T(1,128)} %param.24) | copy-start | bytes 1540
  7.2 122.7 %all-reduce.3.cloned.1.call-start = ((), (), s32[]{:S(2)}) async-start(), calls=%async_computation.2 | async-start | bytes 1048576 | tf_op jit(solution)/shard_map/psum | solution.py:125
  29.8 28.8 %copy-start.3 = (bf16[64,128]{1,0:T(8,128)(2,1)S(1)}, bf16[64,128]{1,0:T(8,128)(2,1)}, u32[]{:S(2)}) copy-start(bf16[64,128]{1,0:T(8,128)(2,1)} %param.28) | copy-start | bytes 49156
  100.7 178.8 %reduce-scatter.3.cloned.1.call-start = ((), (), s32[]{:S(2)}) async-start(), calls=%async_computation.3 | async-start | bytes 557056 | tf_op jit(solution)/shard_map/reduce_scatter | solution.py:129
  227.6 182.7 %all-reduce.5.cloned.1.call-start = ((), (), s32[]{:S(2)}) async-start(), calls=%async_computation.4 | async-start | bytes 1048576 | tf_op jit(solution)/shard_map/psum | solution.py:125
  380.7 180.0 %reduce-scatter.5.cloned.1.call-start = ((), (), s32[]{:S(2)}) async-start(), calls=%async_computation.5 | async-start | bytes 557056 | tf_op jit(solution)/shard_map/reduce_scatter | solution.py:129
  672.3 0.6 copy-start
Sparse Core Ops, SparseCore 0:
  100.8 29.0 all-reduce.2
  227.7 51.7 reduce-scatter.2
  380.8 29.4 all-reduce.4
  508.9 51.6 reduce-scatter.4
where the time goes:
time: 683 us; the launch traced here: 679 us
  blocking collectives  268 us (39%)
  waiting for transfers between devices  156 us (23%)
  matrix products  116 us (17%)
  local copies, waits for them, and re-layouts  69.1 us (10%)
  other arithmetic  53.8 us (8%)
  between operations  14.8 us (2%)
    psum x2, blocking collectives, shards(): gram = lax.psum(gram_of(y_sum), 'user')  114 us
    reduce_scatter x2, waiting for transfers between devices, shards(): z_share = lax.psum_scatter(z_part, 'user', scatter_dimension=1, tiled=True)  97.3 us
    psum x2, blocking collectives, shards(): gram = lax.psum(gram_of(z_share), ('user', 'item'))  82.2 us
    psum x2, waiting for transfers between devices, shards(): y_sum = lax.psum(y_part, 'item')  58.6 us
    all_gather x2, blocking collectives, shards(): q_full = lax.all_gather(q_share, 'user', axis=1, tiled=True)  38.4 us
    another operation x12, other arithmetic, orthonormal(): chol = jnp.linalg.cholesky(gram)  26.1 us
    dot_general x32, matrix products, spread_add(): jnp.einsum('wu,wkr->ukr', onehot, part, precision=lax.Precision.HIGHEST,...  25.2 us
    dot_general x16, matrix products, user_step_fn(): jnp.einsum('wki,wri->wkr', q_tiles[cols_now], piece, preferred_element_ty...  23.9 us
  transfers between devices with their start and end apart: 4, of which 4 were waited for; matrix products, arithmetic and copies ran while one was open for 1% of the time, Pallas kernels for 0%

commit v1 on v0

v1 whole, which is shorter than its diff:
```python
import functools
import math

import jax
import jax.numpy as jnp
from jax import lax
from jax.experimental import pallas as pl
from jax.experimental.pallas import tpu as pltpu
from jax.sharding import PartitionSpec as P

ITERS = 2
F32 = jnp.float32
BF16 = jnp.bfloat16
VMEM = pl.BlockSpec(memory_space=pltpu.VMEM)
SMEM = pl.BlockSpec(memory_space=pltpu.SMEM)
NT = (((1,), (1,)), ((), ()))
NN = (((1,), (0,)), ((), ()))


def params():
    return pltpu.CompilerParams(vmem_limit_bytes=16 * 1024 * 1024)


def xor_pairs(size, mask):
    return [(i, i ^ mask) for i in range(size)]


def bit_groups(size):
    bits = size.bit_length() - 1
    groups, at = [], 0
    while at < bits:
        width = 1 if at < 2 else min(2, bits - at)
        groups.append((at, width))
        at += width
    return groups


def position_of(index, size):
    place = index * 0
    for at, width in bit_groups(size):
        place = place * (1 << width) + ((index >> at) & ((1 << width) - 1))
    return place


def gather_blocks(held, axis, size, groups):
    for at, width in reversed(groups):
        got = [held]
        for k in range(1, 1 << width):
            got.append(lax.ppermute(held, axis, xor_pairs(size, k << at)))
        held = jnp.concatenate(got, axis=0)
    return held


def reduce_blocks(parts, axis, size):
    groups = bit_groups(size)
    for at, width in groups[:-1]:
        ways = 1 << width
        pieces = parts.reshape((ways, parts.shape[0] // ways) + parts.shape[1:])
        total = pieces[0].astype(F32)
        got = [
            lax.ppermute(pieces[k].astype(BF16), axis, xor_pairs(size, k << at))
            for k in range(1, ways)
        ]
        for piece in got:
            total = total + piece.astype(F32)
        parts = total
    at, width = groups[-1]
    mine = parts.astype(BF16)
    total = mine.astype(F32)
    got = [lax.ppermute(mine, axis, xor_pairs(size, k << at)) for k in range(1, 1 << width)]
    for k, piece in enumerate(got, 1):
        total = total + jnp.stack([piece[j ^ k] for j in range(1 << width)]).astype(F32)
    return total


def y_pass(q_cat, r_ref, y_ref):
    users = r_ref.shape[0]
    step = min(256, users)

    def body(i, carry):
        at = pl.multiple_of(i * step, step)
        y = lax.dot_general(
            q_cat, r_ref[pl.ds(at, step), :], NT, preferred_element_type=F32
        )
        y_ref[:, pl.ds(at, step)] = y.astype(y_ref.dtype)
        return carry

    lax.fori_loop(0, users // step, body, 0)


def cat_tiles(ref, rows):
    return jnp.concatenate([ref[t, rows, :] for t in range(ref.shape[0])], axis=1)


def first_kernel(count_ref, row_ref, pos_ref, vals_ref, at_ref, bq_ref, r_ref, y_ref):
    tile = vals_ref.shape[1]
    rank = bq_ref.shape[1] // 2
    users = r_ref.shape[0]
    count = count_ref[0]

    def clear(i, carry):
        r_ref[pl.ds(pl.multiple_of(i * tile, tile), tile), :] = jnp.zeros(
            (tile, r_ref.shape[1]), BF16
        )
        return carry

    lax.fori_loop(0, users // tile, clear, 0)
    group = 4

    def body(i, carry):
        for j in range(group):
            slot = i * group + j
            row = pl.multiple_of(row_ref[slot] * tile, tile)
            pos = pos_ref[slot]
            pred = lax.dot_general(
                at_ref[pl.ds(row, tile), :],
                bq_ref[pos, :rank, :],
                NN,
                preferred_element_type=F32,
            )
            kept = jnp.where(slot < count, 1.0, 0.0)
            resid = (pred - vals_ref[slot].astype(F32)) * kept
            r_ref[pl.ds(row, tile), pl.ds(pl.multiple_of(pos * tile, tile), tile)] = resid.astype(
                BF16
            )
        return carry

    lax.fori_loop(0, (count + group - 1) // group, body, 0)
    y_pass(cat_tiles(bq_ref, slice(rank, 2 * rank)), r_ref, y_ref)


def z_kernel(ya_ref, yb_ref, r_ref, z_ref):
    tile = z_ref.shape[2]
    y = (ya_ref[...].astype(F32) + yb_ref[...].astype(F32)).astype(BF16)
    wide = 2

    def body(i, carry):
        at = pl.multiple_of(i * tile * wide, tile * wide)
        z = lax.dot_general(y, r_ref[:, pl.ds(at, tile * wide)], NN, preferred_element_type=F32)
        for j in range(wide):
            z_ref[i * wide + j] = z[:, j * tile : (j + 1) * tile].astype(z_ref.dtype)
        return carry

    lax.fori_loop(0, z_ref.shape[0] // wide, body, 0)


def gram_kernel(z_ref, g_ref):
    z = cat_tiles(z_ref, slice(None))
    g_ref[...] = lax.dot_general(z, z, NT, preferred_element_type=F32)


def grams_kernel(old_ref, z_ref, g_ref):
    z = cat_tiles(z_ref, slice(None))
    old = cat_tiles(old_ref, slice(None))
    both = jnp.concatenate([z, old], axis=0)
    g_ref[...] = lax.dot_general(both, z, NT, preferred_element_type=F32)


def chol_inverse(grams):
    rank = grams[0].shape[0]
    wide = 8
    blocks = rank // wide
    rows = lax.broadcasted_iota(jnp.int32, (wide, 2 * rank), 0)
    lanes = lax.broadcasted_iota(jnp.int32, (wide, 2 * rank), 1)
    mats = []
    for g in grams:
        padded = jnp.concatenate([g, jnp.zeros_like(g)], axis=1)
        mats.append(
            [
                jnp.where(lanes == rows + (rank + i * wide), 1.0, padded[i * wide : (i + 1) * wide])
                for i in range(blocks)
            ]
        )
    for p in range(blocks):
        below = range(p, blocks)
        cols = [
            [
                {
                    i: jnp.broadcast_to(
                        mat[i][:, p * wide + k : p * wide + k + 1], (wide, 2 * rank)
                    )
                    for i in below
                }
                for k in range(wide)
            ]
            for mat in mats
        ]
        for k in range(wide):
            for mat, col in zip(mats, cols):
                inverse = 1.0 / col[k][p][k : k + 1, :]
                row = mat[p][k : k + 1, :] * inverse
                factor = {
                    i: jnp.where(rows > k, col[k][i], 0.0) if i == p else col[k][i] for i in below
                }
                heads = {q: col[q][p][k : k + 1, :] * inverse for q in range(k + 1, wide)}
                for i in below:
                    mat[i] = mat[i] - factor[i] * row
                    for q in range(k + 1, wide):
                        col[q][i] = col[q][i] - factor[i] * heads[q]
    result = []
    for mat in mats:
        out = []
        for i in range(blocks):
            diagonal = jnp.sum(
                jnp.where(lanes == rows + i * wide, mat[i], 0.0), axis=1, keepdims=True
            )
            out.append(mat[i][:, rank:] * lax.rsqrt(diagonal))
        result.append(jnp.concatenate(out, axis=0))
    return result


def two_parts(mat):
    high = mat.astype(BF16)
    return high, (mat - high.astype(F32)).astype(BF16)


def apply_inverse(inverse, mat):
    high, low = two_parts(inverse)
    return lax.dot_general(
        jnp.concatenate([high, low], axis=1),
        jnp.concatenate([mat, mat], axis=0),
        NN,
        preferred_element_type=F32,
    )


def apply_wide(inverse, mat):
    high, low = two_parts(inverse)
    part, rest = two_parts(mat)
    return lax.dot_general(
        jnp.concatenate([high, low, high], axis=1),
        jnp.concatenate([part, part, rest], axis=0),
        NN,
        preferred_element_type=F32,
    )


def y_kernel(z_ref, r_ref, y_ref):
    y_pass(cat_tiles(z_ref, slice(None)), r_ref, y_ref)


def scale_kernel(ga_ref, gb_ref, y_ref, inv_ref, out_ref):
    (inverse,) = chol_inverse([ga_ref[...] + gb_ref[...]])
    inv_ref[...] = inverse
    out_ref[...] = apply_wide(inverse, y_ref[...]).astype(BF16)


def last_kernel(
    radius,
    user_scale,
    item_scale,
    count_ref,
    row_ref,
    pos_ref,
    ga_ref,
    gb_ref,
    inv_ref,
    z_ref,
    share_ref,
    ya_ref,
    yb_ref,
    vals_ref,
    at_ref,
    bq_ref,
    user_ref,
    item_ref,
    loss_ref,
    left,
    right,
):
    tile = vals_ref.shape[1]
    rank = z_ref.shape[1]
    count = count_ref[0]
    gram = ga_ref[...] + gb_ref[...]
    y_gram = lax.dot_general(
        inv_ref[...], gram[rank:], NN, precision=lax.Precision.HIGHEST, preferred_element_type=F32
    )
    z_inv, y_inv = chol_inverse([gram[:rank], y_gram])
    for t in range(z_ref.shape[0]):
        q = apply_inverse(z_inv, z_ref[t]).astype(BF16)
        right[t, :rank] = bq_ref[t, :rank, :]
        right[t, rank : 2 * rank] = q
        right[t, 2 * rank : 3 * rank] = q
    for t in range(user_ref.shape[1] // tile):
        cols = slice(t * tile, (t + 1) * tile)
        y = ya_ref[:, cols].astype(F32) + yb_ref[:, cols].astype(F32)
        y_hat = apply_wide(y_inv, y)
        user_ref[:, cols] = y_hat * user_scale
        y_hat = y_hat.astype(BF16).astype(F32)
        turned = (y_hat * (-0.5 * radius)).T
        high, low = two_parts(turned)
        half = at_ref[cols, :].astype(F32) * 0.5
        left[cols, :] = jnp.concatenate([half.astype(BF16), high, low], axis=1)
    item_ref[...] = apply_wide(z_inv, share_ref[...]) * item_scale
    loss_ref[...] = jnp.zeros_like(loss_ref)
    group = 8
    ones = jnp.ones((group, tile), BF16)
    place = lax.broadcasted_iota(jnp.int32, (group, tile), 0)

    def body(i, carry):
        at = pl.multiple_of(i * group, group)
        total = jnp.zeros((group, tile), F32)
        for j in range(group):
            slot = at + j
            row = pl.multiple_of(row_ref[slot] * tile, tile)
            fresh = lax.dot_general(
                left[pl.ds(row, tile), :], right[pos_ref[slot]], NN, preferred_element_type=F32
            )
            fresh = fresh - vals_ref[slot].astype(F32)
            sums = lax.dot_general(
                ones, (fresh * fresh).astype(BF16), NT, preferred_element_type=F32
            )
            total = jnp.where((place == j) & (slot < count), sums, total)
        loss_ref[pl.ds(at, group), :] = total * (1.0 / tile)
        return carry

    lax.fori_loop(0, (count + group - 1) // group, body, 0)


def shards(tile_vals, tile_row, tile_col, tile_count, fac_a, fac_b, omega):
    ratings = tile_vals[0, 0]
    rows = tile_row[0, 0]
    cols = tile_col[0, 0]
    count = tile_count[0]
    cap, tile, _ = ratings.shape
    rank, users_dev = fac_a.shape
    share = fac_b.shape[1]
    n_user = lax.axis_size("user")
    n_item = lax.axis_size("item")
    items_dev = share * n_user
    item_tiles = items_dev // tile
    users, items = users_dev * n_user, items_dev * n_item
    radius = math.sqrt(users * items / rank)
    me = lax.axis_index("user").astype(jnp.int32)

    by_tile = share == tile
    slots = jnp.arange(n_user, dtype=jnp.int32)
    if by_tile:
        places = position_of(cols ^ me, n_user)
    else:
        places = cols
        order = position_of(slots ^ me, n_user)

    def to_tiles(blocks):
        if by_tile:
            return blocks
        blocks = blocks[order]
        wide = blocks.transpose(1, 0, 2).reshape(blocks.shape[1], item_tiles, tile)
        return wide.transpose(1, 0, 2)

    def to_blocks(tiles):
        if by_tile:
            return tiles
        wide = tiles.transpose(1, 0, 2).reshape(tiles.shape[1], n_user, share)
        return jnp.zeros((n_user, tiles.shape[1], share), tiles.dtype).at[order].set(
            wide.transpose(1, 0, 2)
        )

    def across(mine):
        bit = 1
        while True:
            other = lax.ppermute(mine, "item", xor_pairs(n_item, bit))
            bit *= 2
            if bit >= n_item:
                return mine, other
            mine = (mine.astype(F32) + other.astype(F32)).astype(mine.dtype)

    def reduced(parts):
        total = reduce_blocks(to_blocks(parts), "user", n_user)
        groups = bit_groups(n_user)[:-1]
        return to_tiles(gather_blocks(total.astype(BF16), "user", n_user, groups)), total[0]

    a_t = fac_a.T
    both = jnp.concatenate([fac_b, omega], axis=0)
    bq = to_tiles(gather_blocks(both[None], "user", n_user, bit_groups(n_user)))

    z_call = pl.pallas_call(
        z_kernel,
        out_shape=jax.ShapeDtypeStruct((item_tiles, rank, tile), BF16),
        in_specs=[VMEM] * 3,
        out_specs=VMEM,
        compiler_params=params(),
        name="z_pass",
    )
    resid, y_part = pl.pallas_call(
        first_kernel,
        out_shape=(
            jax.ShapeDtypeStruct((users_dev, items_dev), BF16),
            jax.ShapeDtypeStruct((rank, users_dev), BF16),
        ),
        in_specs=[SMEM] * 3 + [VMEM] * 3,
        out_specs=(VMEM, VMEM),
        compiler_params=params(),
        name="resid_y",
    )(count, rows, places, ratings, a_t, bq)
    old, _ = reduced(z_call(*across(y_part), resid))
    gram = pl.pallas_call(
        gram_kernel,
        out_shape=jax.ShapeDtypeStruct((rank, rank), F32),
        in_specs=[VMEM],
        out_specs=VMEM,
        compiler_params=params(),
        name="gram",
    )(old)
    gram_mine, gram_other = across(gram)
    y_part = pl.pallas_call(
        y_kernel,
        out_shape=jax.ShapeDtypeStruct((rank, users_dev), F32),
        in_specs=[VMEM] * 2,
        out_specs=VMEM,
        compiler_params=params(),
        cost_estimate=pl.CostEstimate(
            flops=2 * rank * users_dev * items_dev, bytes_accessed=8 << 20, transcendentals=0
        ),
        name="y_pass",
    )(old, resid)
    inverse, y_part = pl.pallas_call(
        scale_kernel,
        out_shape=(
            jax.ShapeDtypeStruct((rank, rank), F32),
            jax.ShapeDtypeStruct((rank, users_dev), BF16),
        ),
        in_specs=[VMEM] * 3,
        out_specs=(VMEM, VMEM),
        compiler_params=params(),
        name="scale_y",
    )(gram_mine, gram_other, y_part)
    y_mine, y_other = across(y_part)
    z, z_share = reduced(z_call(y_mine, y_other, resid))
    grams = pl.pallas_call(
        grams_kernel,
        out_shape=jax.ShapeDtypeStruct((2 * rank, rank), F32),
        in_specs=[VMEM] * 2,
        out_specs=VMEM,
        compiler_params=params(),
        name="grams",
    )(old, z)
    user_dir, item_dir, losses = pl.pallas_call(
        functools.partial(last_kernel, radius, math.sqrt(users), math.sqrt(items)),
        out_shape=(
            jax.ShapeDtypeStruct((rank, users_dev), F32),
            jax.ShapeDtypeStruct((rank, share), F32),
            jax.ShapeDtypeStruct((cap, tile), F32),
        ),
        in_specs=[SMEM] * 3 + [VMEM] * 10,
        out_specs=(VMEM, VMEM, VMEM),
        scratch_shapes=[
            pltpu.VMEM((users_dev, 3 * rank), BF16),
            pltpu.VMEM((item_tiles, 3 * rank, tile), BF16),
        ],
        compiler_params=params(),
        name="loss",
    )(count, rows, places, *across(grams), inverse, z, z_share, y_mine, y_other, ratings, a_t, bq)
    return (user_dir, item_dir, losses[None, None])


def solution(mesh):
    return jax.shard_map(
        shards,
        mesh=mesh,
        in_specs=(
            P("user", "item", None, None, None),
            P("user", "item", None),
            P("user", "item", None),
            P("user", "item"),
            P(None, "user"),
            P(None, ("item", "user")),
            P(None, ("item", "user")),
        ),
        out_specs=(P(None, "user"), P(None, ("item", "user")), P("user", "item", None, None)),
        check_vma=False,
    )
```

time: 683 us -> 113 us (0.17)
  blocking collectives: 268 us -> 0 us
  matrix products: 116 us -> 0 us
  waiting for transfers between devices: 156 us -> 43.6 us
  local copies, waits for them, and re-layouts: 69.1 us -> 4.29 us
  other arithmetic: 53.8 us -> 2.44 us
  Pallas kernels: 0 us -> 34.1 us
  starting transfers between devices: 0.16 us -> 26.3 us
  between operations: 14.8 us -> 1.52 us
    psum x4 -> x0, blocking collectives: 196 us -> none  [the longest x2 114 us: shards(): gram = lax.psum(gram_of(y_sum), 'user')]
    dot_general x96 -> x0, matrix products: 115 us -> none  [the longest x32 25.2 us: spread_add(): jnp.einsum('wu,wkr->ukr', onehot, part, precision=lax.Precision.HIGHEST,...]
    reduce_scatter x2 -> x0, waiting for transfers between devices: 97.3 us -> none  [shards(): z_share = lax.psum_scatter(z_part, 'user', scatter_dimension=1, tiled=True)]
    all_gather x4 -> x0, blocking collectives: 71.7 us -> none  [the longest x2 38.4 us: shards(): q_full = lax.all_gather(q_share, 'user', axis=1, tiled=True)]
    psum x2 -> x0, waiting for transfers between devices: 58.6 us -> none  [shards(): y_sum = lax.psum(y_part, 'item')]
    another operation x20 -> x0, other arithmetic: 48.3 us -> none  [the longest x12 26.1 us: orthonormal(): chol = jnp.linalg.cholesky(gram)]
    gather x80 -> x0, local copies, waits for them, and re-layouts: 47.7 us -> none  [the longest x16 9.57 us: predict(): a_tiles[rows_now]]
    ppermute x0 -> x23, waiting for transfers between devices: none -> 43.6 us  [the longest x4 16.1 us: across(): other = lax.ppermute(mine, 'item', xor_pairs(n_item, bit))]
  transfers between devices with their start and end apart: 4 -> 23, of which waited for: 4 -> 19; matrix products, arithmetic and copies ran while one was open for 1% -> 2% of each run, Pallas kernels for 0% -> 3%
where the time goes in v1:
time: 113 us; the launch traced here: 112 us
  waiting for transfers between devices  43.6 us (39%)
  Pallas kernels  34.1 us (30%)
  starting transfers between devices  26.3 us (23%)
  local copies, waits for them, and re-layouts  4.29 us (4%)
  other arithmetic  2.44 us (2%)
  between operations  1.52 us (1%)
    ppermute x9, starting transfers between devices, gather_blocks(): got.append(lax.ppermute(held, axis, xor_pairs(size, k << at)))  16.1 us
    ppermute x4, waiting for transfers between devices, across(): other = lax.ppermute(mine, 'item', xor_pairs(n_item, bit))  16.1 us
    pallas_call x1, Pallas kernels, shards(): pl.pallas_call(functools.partial(last_kernel, radius, math.sqrt(users), m...  12.8 us
    ppermute x9, waiting for transfers between devices, gather_blocks(): got.append(lax.ppermute(held, axis, xor_pairs(size, k << at)))  11.4 us
    pallas_call x1, Pallas kernels, shards(): pl.pallas_call(first_kernel, out_shape=(jax.ShapeDtypeStruct((users_dev,...  10.4 us
    ppermute x4, waiting for transfers between devices, reduce_blocks(): lax.ppermute(pieces[k].astype(BF16), axis, xor_pairs(size, k << at))  8.77 us
    ppermute x6, waiting for transfers between devices, reduce_blocks(): lax.ppermute(mine, axis, xor_pairs(size, k << at))  7.38 us
    ppermute x6, starting transfers between devices, reduce_blocks(): lax.ppermute(mine, axis, xor_pairs(size, k << at))  5.44 us
  transfers between devices with their start and end apart: 23, of which 19 were waited for; matrix products, arithmetic and copies ran while one was open for 2% of the time, Pallas kernels for 3%

profile of v1, /device:TPU:29, one launch (start us, length us, event | category | flops | bytes accessed | tf_op | source)
XLA Modules:
  0.0 112.3 jit_solution(18263803504414995540)
XLA Ops:
  1.4 1.3 %collective-permute-start.1 = (bf16[1,128,128]{2,1,0:T(8,128)(2,1)S(1)}, bf16[1,128,128]{2,1,0:T(8,128)(2,1)S(1)}, u32[]{:S(2)}, u32[]{:S(2)}) collective-permute-start(bf16[1,128,128]{2,1,0:T(8,128)(2,1)S(1)} %maximum_bitcast_fusion), channel_id=1, source_target_pairs={{0,16},{2,18},{4,20},{6,22},{8,24},{10,26},{12,28},{14,30},{16,0},... | collective-permute-start | bytes 98312 | tf_op jit(solution)/shard_map/ppermute | solution.py:49
  2.7 2.2 %collective-permute-start = (bf16[1,128,128]{2,1,0:T(8,128)(2,1)S(1)}, bf16[1,128,128]{2,1,0:T(8,128)(2,1)S(1)}, u32[]{:S(2)}, u32[]{:S(2)}) collective-permute-start(bf16[1,128,128]{2,1,0:T(8,128)(2,1)S(1)} %maximum_bitcast_fusion), channel_id=1, source_target_pairs={{0,8},{2,10},{4,12},{6,14},{8,0},{10,2},{12,4},{14,6},{16,24},{18,... | collective-permute-start | bytes 98312 | tf_op jit(solution)/shard_map/ppermute | solution.py:49
  7.0 3.5 %collective-permute-done.3 = bf16[4,128,128]{2,1,0:T(8,128)(2,1)S(1)} collective-permute-done((bf16[4,128,128]{2,1,0:T(8,128)(2,1)S(1)}, bf16[4,128,128]{2,1,0:T(8,128)(2,1)S(1)}, u32[]{:S(2)}, u32[]{:S(2)}) %collective-permute-start.3) | collective-permute-done | bytes 131104 | tf_op jit(solution)/shard_map/ppermute | solution.py:49
  10.6 2.9 %collective-permute-start.4 = (bf16[8,128,128]{2,1,0:T(8,128)(2,1)S(1)}, bf16[8,128,128]{2,1,0:T(8,128)(2,1)S(1)}, u32[]{:S(2)}, u32[]{:S(2)}) collective-permute-start(bf16[8,128,128]{2,1,0:T(8,128)(2,1)S(1)} %get-tuple-element.19), channel_id=1, source_target_pairs={{0,2},{2,0},{4,6},{6,4},{8,10},{10,8},{12,14},{14,12},{16,18},{18,... | collective-permute-start | bytes 786440 | tf_op jit(solution)/shard_map/ppermute | solution.py:49
  14.2 1.2 %copy.10 = bf16[64,2048]{0,1:T(8,128)(2,1)S(1)} copy(bf16[64,2048]{1,0:T(8,128)(2,1)} %param.11) | data formatting | bytes 524288 | tf_op args[4]
  16.1 2.2 %copy-done = bf16[1,1,128,128,128]{4,3,2,1,0:T(8,128)(2,1)S(1)} copy-done((bf16[1,1,128,128,128]{4,3,2,1,0:T(8,128)(2,1)S(1)}, bf16[1,1,128,128,128]{4,3,2,1,0:T(8,128)(2,1)}, u32[]{:S(2)}) %copy-start) | copy-done | bytes 4194328
  18.9 10.4 %resid_y.1 = (bf16[2048,2048]{1,0:T(8,128)(2,1)S(1)}, bf16[64,2048]{1,0:T(8,128)(2,1)S(1)}) custom-call(s32[1]{0:T(128)} %bitcast.15.count_ref, s32[128]{0:T(128)S(1)} %bitcast.21, s32[128]{0:T(128)S(1)} %add_bitcast_fusion.pos_ref, bf16[128,128,128]{2,1,0:T(8,128)(2,1)S(1)} %bitcast.17, bf16[2048,64]{1,0:T(8,128)(2,1)S(1)} %bitcast.19, ...), custom_call_target="tpu_custom_call" | custom-call | tf_op jit(solution)/shard_map/resid_y/pallas_call | solution.py:385
  30.1 6.6 %collective-permute-done.5.yb_ref = bf16[64,2048]{1,0:T(8,128)(2,1)S(1)} collective-permute-done((bf16[64,2048]{1,0:T(8,128)(2,1)S(1)}, bf16[64,2048]{1,0:T(8,128)(2,1)S(1)}, u32[]{:S(2)}, u32[]{:S(2)}) %collective-permute-start.5) | collective-permute-done | bytes 262176 | tf_op jit(solution)/shard_map/ppermute | solution.py:362
  36.7 2.5 %z_pass.2 = bf16[16,64,128]{2,1,0:T(8,128)(2,1)S(1)} custom-call(bf16[64,2048]{1,0:T(8,128)(2,1)S(1)} %get-tuple-element.10.ya_ref, bf16[64,2048]{1,0:T(8,128)(2,1)S(1)} %collective-permute-done.5.yb_ref, bf16[2048,2048]{1,0:T(8,128)(2,1)S(1)} %get-tuple-element.11.r_ref), custom_call_target="tpu_custom_call" | custom-call | tf_op jit(solution)/shard_map/z_pass/pallas_call | solution.py:396
  39.3 1.3 %collective-permute-done.6 = bf16[8,64,128]{2,1,0:T(8,128)(2,1)S(1)} collective-permute-done((bf16[8,64,128]{2,1,0:T(8,128)(2,1)S(1)}, bf16[8,64,128]{2,1,0:T(8,128)(2,1)S(1)}, u32[]{:S(2)}, u32[]{:S(2)}) %collective-permute-start.6) | collective-permute-done | bytes 131104 | tf_op jit(solution)/shard_map/ppermute | solution.py:61
  40.7 3.5 %collective-permute-done.7 = bf16[4,64,128]{2,1,0:T(8,128)(2,1)S(1)} collective-permute-done((bf16[4,64,128]{2,1,0:T(8,128)(2,1)S(1)}, bf16[4,64,128]{2,1,0:T(8,128)(2,1)S(1)}, u32[]{:S(2)}, u32[]{:S(2)}) %collective-permute-start.7) | collective-permute-done | bytes 65568 | tf_op jit(solution)/shard_map/ppermute | solution.py:61
  44.4 1.9 %collective-permute-start.10 = (bf16[4,64,128]{2,1,0:T(8,128)(2,1)S(1)}, bf16[4,64,128]{2,1,0:T(8,128)(2,1)S(1)}, u32[]{:S(2)}, u32[]{:S(2)}) collective-permute-start(bf16[4,64,128]{2,1,0:T(8,128)(2,1)S(1)} %fusion.1), channel_id=1, source_target_pairs={{0,24},{2,26},{4,28},{6,30},{8,16},{10,18},{12,20},{14,22},{16,8},... | collective-permute-start | bytes 196616 | tf_op jit(solution)/shard_map/ppermute | solution.py:70
  47.0 1.6 %collective-permute-done.9 = bf16[4,64,128]{2,1,0:T(8,128)(2,1)S(1)} collective-permute-done((bf16[4,64,128]{2,1,0:T(8,128)(2,1)S(1)}, bf16[4,64,128]{2,1,0:T(8,128)(2,1)S(1)}, u32[]{:S(2)}, u32[]{:S(2)}) %collective-permute-start.9) | collective-permute-done | bytes 65568 | tf_op jit(solution)/shard_map/ppermute | solution.py:70
  48.6 1.1 collective-permute-done.10
  50.5 1.0 collective-permute-start.11
  51.5 2.2 %collective-permute-done.11 = bf16[4,64,128]{2,1,0:T(8,128)(2,1)S(1)} collective-permute-done((bf16[4,64,128]{2,1,0:T(8,128)(2,1)S(1)}, bf16[4,64,128]{2,1,0:T(8,128)(2,1)S(1)}, u32[]{:S(2)}, u32[]{:S(2)}) %collective-permute-start.11) | collective-permute-done | bytes 65568 | tf_op jit(solution)/shard_map/ppermute | solution.py:49
  53.7 4.1 %collective-permute-start.12 = (bf16[8,64,128]{2,1,0:T(8,128)(2,1)S(1)}, bf16[8,64,128]{2,1,0:T(8,128)(2,1)S(1)}, u32[]{:S(2)}, u32[]{:S(2)}) collective-permute-start(bf16[8,64,128]{2,1,0:T(8,128)(2,1)S(1)} %pad_maximum_fusion.3), channel_id=1, source_target_pairs={{0,2},{2,0},{4,6},{6,4},{8,10},{10,8},{12,14},{14,12},{16,18},{18,... | collective-permute-start | bytes 393224 | tf_op jit(solution)/shard_map/ppermute | solution.py:49
  57.8 1.0 collective-permute-done.12
  59.0 1.1 collective-permute-start.13
  60.1 3.6 %y_pass.1.y_ref = f32[64,2048]{1,0:T(8,128)S(1)} custom-call(bf16[16,64,128]{2,1,0:T(8,128)(2,1)S(1)} %pad_maximum_fusion.z_ref.old_ref, bf16[2048,2048]{1,0:T(8,128)(2,1)S(1)} %get-tuple-element.11.r_ref), custom_call_target="tpu_custom_call" | custom-call | flops 536870912 | bytes 8388608 | tf_op jit(solution)/shard_map/y_pass/pallas_call | solution.py:406
  63.7 1.8 %scale_y.1 = (f32[64,64]{1,0:T(8,128)S(1)}, bf16[64,2048]{1,0:T(8,128)(2,1)S(1)}) custom-call(f32[64,64]{1,0:T(8,128)S(1)} %gram.1.ga_ref, f32[64,64]{1,0:T(8,128)S(1)} %collective-permute-done.13.gb_ref, f32[64,2048]{1,0:T(8,128)S(1)} %y_pass.1.y_ref), custom_call_target="tpu_custom_call" | custom-call | tf_op jit(solution)/shard_map/scale_y/pallas_call | solution.py:417
  66.1 6.8 %collective-permute-done.14.yb_ref = bf16[64,2048]{1,0:T(8,128)(2,1)S(1)} collective-permute-done((bf16[64,2048]{1,0:T(8,128)(2,1)S(1)}, bf16[64,2048]{1,0:T(8,128)(2,1)S(1)}, u32[]{:S(2)}, u32[]{:S(2)}) %collective-permute-start.14) | collective-permute-done | bytes 262176 | tf_op jit(solution)/shard_map/ppermute | solution.py:362
  72.9 2.5 %z_pass.3 = bf16[16,64,128]{2,1,0:T(8,128)(2,1)S(1)} custom-call(bf16[64,2048]{1,0:T(8,128)(2,1)S(1)} %get-tuple-element.12.ya_ref, bf16[64,2048]{1,0:T(8,128)(2,1)S(1)} %collective-permute-done.14.yb_ref, bf16[2048,2048]{1,0:T(8,128)(2,1)S(1)} %get-tuple-element.11.r_ref), custom_call_target="tpu_custom_call" | custom-call | tf_op jit(solution)/shard_map/z_pass/pallas_call | solution.py:429
  75.4 1.6 %collective-permute-start.15 = (bf16[8,64,128]{2,1,0:T(8,128)(2,1)S(1)}, bf16[8,64,128]{2,1,0:T(8,128)(2,1)S(1)}, u32[]{:S(2)}, u32[]{:S(2)}) collective-permute-start(bf16[8,64,128]{2,1,0:T(8,128)(2,1)S(1)} %slice.149), channel_id=1, source_target_pairs={{0,2},{2,0},{4,6},{6,4},{8,10},{10,8},{12,14},{14,12},{16,18},{18,... | collective-permute-start | bytes 393224 | tf_op jit(solution)/shard_map/ppermute | solution.py:61
  77.0 1.0 collective-permute-done.15
  78.3 2.9 %collective-permute-done.16 = bf16[4,64,128]{2,1,0:T(8,128)(2,1)S(1)} collective-permute-done((bf16[4,64,128]{2,1,0:T(8,128)(2,1)S(1)}, bf16[4,64,128]{2,1,0:T(8,128)(2,1)S(1)}, u32[]{:S(2)}, u32[]{:S(2)}) %collective-permute-start.16) | collective-permute-done | bytes 65568 | tf_op jit(solution)/shard_map/ppermute | solution.py:61
  81.4 2.5 %collective-permute-start.19 = (bf16[4,64,128]{2,1,0:T(8,128)(2,1)S(1)}, bf16[4,64,128]{2,1,0:T(8,128)(2,1)S(1)}, u32[]{:S(2)}, u32[]{:S(2)}) collective-permute-start(bf16[4,64,128]{2,1,0:T(8,128)(2,1)S(1)} %fusion), channel_id=1, source_target_pairs={{0,24},{2,26},{4,28},{6,30},{8,16},{10,18},{12,20},{14,22},{16,8},... | collective-permute-start | bytes 196616 | tf_op jit(solution)/shard_map/ppermute | solution.py:70
  83.9 3.1 %collective-permute-done.18 = bf16[4,64,128]{2,1,0:T(8,128)(2,1)S(1)} collective-permute-done((bf16[4,64,128]{2,1,0:T(8,128)(2,1)S(1)}, bf16[4,64,128]{2,1,0:T(8,128)(2,1)S(1)}, u32[]{:S(2)}, u32[]{:S(2)}) %collective-permute-start.18) | collective-permute-done | bytes 65568 | tf_op jit(solution)/shard_map/ppermute | solution.py:70
  88.4 2.8 %collective-permute-done.20 = bf16[4,64,128]{2,1,0:T(8,128)(2,1)S(1)} collective-permute-done((bf16[4,64,128]{2,1,0:T(8,128)(2,1)S(1)}, bf16[4,64,128]{2,1,0:T(8,128)(2,1)S(1)}, u32[]{:S(2)}, u32[]{:S(2)}) %collective-permute-start.20) | collective-permute-done | bytes 65568 | tf_op jit(solution)/shard_map/ppermute | solution.py:49
  91.2 3.8 %collective-permute-start.21 = (bf16[8,64,128]{2,1,0:T(8,128)(2,1)S(1)}, bf16[8,64,128]{2,1,0:T(8,128)(2,1)S(1)}, u32[]{:S(2)}, u32[]{:S(2)}) collective-permute-start(bf16[8,64,128]{2,1,0:T(8,128)(2,1)S(1)} %pad_maximum_fusion.4), channel_id=1, source_target_pairs={{0,2},{2,0},{4,6},{6,4},{8,10},{10,8},{12,14},{14,12},{16,18},{18,... | collective-permute-start | bytes 393224 | tf_op jit(solution)/shard_map/ppermute | solution.py:49
  96.8 2.7 %collective-permute-done.22.gb_ref = f32[128,64]{1,0:T(8,128)S(1)} collective-permute-done((f32[128,64]{1,0:T(8,128)S(1)}, f32[128,64]{1,0:T(8,128)S(1)}, u32[]{:S(2)}, u32[]{:S(2)}) %collective-permute-start.22) | collective-permute-done | bytes 32800 | tf_op jit(solution)/shard_map/ppermute | solution.py:362
  99.5 12.8 %loss.1 = (f32[64,2048]{1,0:T(8,128)}, f32[64,128]{1,0:T(8,128)}, f32[128,128]{1,0:T(8,128)}) custom-call(s32[1]{0:T(128)} %bitcast.16.count_ref, s32[128]{0:T(128)S(1)} %bitcast.22, s32[128]{0:T(128)S(1)} %add_bitcast_fusion.pos_ref, f32[128,64]{1,0:T(8,128)S(1)} %grams.1.ga_ref, f32[128,64]{1,0:T(8,128)S(1)} %collective-permute-done.22.gb_ref, ...), custom_call_target="tpu_custom_call" | custom-call | tf_op jit(solution)/shard_map/loss/pallas_call | solution.py:438
  (61 shorter events, 11.2 us)
Async XLA Ops:
  1.4 4.6 %collective-permute-start.2 = (bf16[1,128,128]{2,1,0:T(8,128)(2,1)S(1)}, bf16[1,128,128]{2,1,0:T(8,128)(2,1)S(1)}, u32[]{:S(2)}, u32[]{:S(2)}) collective-permute-start(bf16[1,128,128]{2,1,0:T(8,128)(2,1)S(1)} %maximum_bitcast_fusion), channel_id=1, source_target_pairs={{0,24},{2,26},{4,28},{6,30},{8,16},{10,18},{12,20},{14,22},{16,8},... | collective-permute-start | bytes 98312 | tf_op jit(solution)/shard_map/ppermute | solution.py:49
  1.4 4.6 %collective-permute-start.1 = (bf16[1,128,128]{2,1,0:T(8,128)(2,1)S(1)}, bf16[1,128,128]{2,1,0:T(8,128)(2,1)S(1)}, u32[]{:S(2)}, u32[]{:S(2)}) collective-permute-start(bf16[1,128,128]{2,1,0:T(8,128)(2,1)S(1)} %maximum_bitcast_fusion), channel_id=1, source_target_pairs={{0,16},{2,18},{4,20},{6,22},{8,24},{10,26},{12,28},{14,30},{16,0},... | collective-permute-start | bytes 98312 | tf_op jit(solution)/shard_map/ppermute | solution.py:49
  2.7 3.9 %collective-permute-start = (bf16[1,128,128]{2,1,0:T(8,128)(2,1)S(1)}, bf16[1,128,128]{2,1,0:T(8,128)(2,1)S(1)}, u32[]{:S(2)}, u32[]{:S(2)}) collective-permute-start(bf16[1,128,128]{2,1,0:T(8,128)(2,1)S(1)} %maximum_bitcast_fusion), channel_id=1, source_target_pairs={{0,8},{2,10},{4,12},{6,14},{8,0},{10,2},{12,4},{14,6},{16,24},{18,... | collective-permute-start | bytes 98312 | tf_op jit(solution)/shard_map/ppermute | solution.py:49
  6.6 3.9 %collective-permute-start.3 = (bf16[4,128,128]{2,1,0:T(8,128)(2,1)S(1)}, bf16[4,128,128]{2,1,0:T(8,128)(2,1)S(1)}, u32[]{:S(2)}, u32[]{:S(2)}) collective-permute-start(bf16[4,128,128]{2,1,0:T(8,128)(2,1)S(1)} %pad_maximum_fusion.2), channel_id=1, source_target_pairs={{0,4},{2,6},{4,0},{6,2},{8,12},{10,14},{12,8},{14,10},{16,20},{18,... | collective-permute-start | bytes 393224 | tf_op jit(solution)/shard_map/ppermute | solution.py:49
  10.6 5.5 %collective-permute-start.4 = (bf16[8,128,128]{2,1,0:T(8,128)(2,1)S(1)}, bf16[8,128,128]{2,1,0:T(8,128)(2,1)S(1)}, u32[]{:S(2)}, u32[]{:S(2)}) collective-permute-start(bf16[8,128,128]{2,1,0:T(8,128)(2,1)S(1)} %get-tuple-element.19), channel_id=1, source_target_pairs={{0,2},{2,0},{4,6},{6,4},{8,10},{10,8},{12,14},{14,12},{16,18},{18,... | collective-permute-start | bytes 786440 | tf_op jit(solution)/shard_map/ppermute | solution.py:49
  16.1 2.2 %copy-start = (bf16[1,1,128,128,128]{4,3,2,1,0:T(8,128)(2,1)S(1)}, bf16[1,1,128,128,128]{4,3,2,1,0:T(8,128)(2,1)}, u32[]{:S(2)}) copy-start(bf16[1,1,128,128,128]{4,3,2,1,0:T(8,128)(2,1)} %param.7) | copy-start | bytes 12582916
  18.3 0.7 copy-start.2
  29.3 7.3 %collective-permute-start.5 = (bf16[64,2048]{1,0:T(8,128)(2,1)S(1)}, bf16[64,2048]{1,0:T(8,128)(2,1)S(1)}, u32[]{:S(2)}, u32[]{:S(2)}) collective-permute-start(bf16[64,2048]{1,0:T(8,128)(2,1)S(1)} %get-tuple-element.10.ya_ref), channel_id=1, source_target_pairs={{0,1},{1,0},{2,3},{3,2},{4,5},{5,4},{6,7},{7,6},{8,9},{9,8},{10,11... | collective-permute-start | bytes 786440 | tf_op jit(solution)/shard_map/ppermute | solution.py:362
  39.2 1.4 %collective-permute-start.6 = (bf16[8,64,128]{2,1,0:T(8,128)(2,1)S(1)}, bf16[8,64,128]{2,1,0:T(8,128)(2,1)S(1)}, u32[]{:S(2)}, u32[]{:S(2)}) collective-permute-start(bf16[8,64,128]{2,1,0:T(8,128)(2,1)S(1)} %slice.135), channel_id=1, source_target_pairs={{0,2},{2,0},{4,6},{6,4},{8,10},{10,8},{12,14},{14,12},{16,18},{18,... | collective-permute-start | bytes 393224 | tf_op jit(solution)/shard_map/ppermute | solution.py:61
  40.7 3.6 %collective-permute-start.7 = (bf16[4,64,128]{2,1,0:T(8,128)(2,1)S(1)}, bf16[4,64,128]{2,1,0:T(8,128)(2,1)S(1)}, u32[]{:S(2)}, u32[]{:S(2)}) collective-permute-start(bf16[4,64,128]{2,1,0:T(8,128)(2,1)S(1)} %slice.175), channel_id=1, source_target_pairs={{0,4},{2,6},{4,0},{6,2},{8,12},{10,14},{12,8},{14,10},{16,20},{18,... | collective-permute-start | bytes 196616 | tf_op jit(solution)/shard_map/ppermute | solution.py:61
  44.3 4.3 %collective-permute-start.9 = (bf16[4,64,128]{2,1,0:T(8,128)(2,1)S(1)}, bf16[4,64,128]{2,1,0:T(8,128)(2,1)S(1)}, u32[]{:S(2)}, u32[]{:S(2)}) collective-permute-start(bf16[4,64,128]{2,1,0:T(8,128)(2,1)S(1)} %fusion.1), channel_id=1, source_target_pairs={{0,16},{2,18},{4,20},{6,22},{8,24},{10,26},{12,28},{14,30},{16,0},... | collective-permute-start | bytes 196616 | tf_op jit(solution)/shard_map/ppermute | solution.py:70
  44.4 5.3 %collective-permute-start.10 = (bf16[4,64,128]{2,1,0:T(8,128)(2,1)S(1)}, bf16[4,64,128]{2,1,0:T(8,128)(2,1)S(1)}, u32[]{:S(2)}, u32[]{:S(2)}) collective-permute-start(bf16[4,64,128]{2,1,0:T(8,128)(2,1)S(1)} %fusion.1), channel_id=1, source_target_pairs={{0,24},{2,26},{4,28},{6,30},{8,16},{10,18},{12,20},{14,22},{16,8},... | collective-permute-start | bytes 196616 | tf_op jit(solution)/shard_map/ppermute | solution.py:70
  46.2 4.2 %collective-permute-start.8 = (bf16[4,64,128]{2,1,0:T(8,128)(2,1)S(1)}, bf16[4,64,128]{2,1,0:T(8,128)(2,1)S(1)}, u32[]{:S(2)}, u32[]{:S(2)}) collective-permute-start(bf16[4,64,128]{2,1,0:T(8,128)(2,1)S(1)} %fusion.1), channel_id=1, source_target_pairs={{0,8},{2,10},{4,12},{6,14},{8,0},{10,2},{12,4},{14,6},{16,24},{18,... | collective-permute-start | bytes 196616 | tf_op jit(solution)/shard_map/ppermute | solution.py:70
  50.5 3.2 %collective-permute-start.11 = (bf16[4,64,128]{2,1,0:T(8,128)(2,1)S(1)}, bf16[4,64,128]{2,1,0:T(8,128)(2,1)S(1)}, u32[]{:S(2)}, u32[]{:S(2)}) collective-permute-start(bf16[4,64,128]{2,1,0:T(8,128)(2,1)S(1)} %add_convert_fusion), channel_id=1, source_target_pairs={{0,4},{2,6},{4,0},{6,2},{8,12},{10,14},{12,8},{14,10},{16,20},{18,... | collective-permute-start | bytes 196616 | tf_op jit(solution)/shard_map/ppermute | solution.py:49
  53.7 5.1 %collective-permute-start.12 = (bf16[8,64,128]{2,1,0:T(8,128)(2,1)S(1)}, bf16[8,64,128]{2,1,0:T(8,128)(2,1)S(1)}, u32[]{:S(2)}, u32[]{:S(2)}) collective-permute-start(bf16[8,64,128]{2,1,0:T(8,128)(2,1)S(1)} %pad_maximum_fusion.3), channel_id=1, source_target_pairs={{0,2},{2,0},{4,6},{6,4},{8,10},{10,8},{12,14},{14,12},{16,18},{18,... | collective-permute-start | bytes 393224 | tf_op jit(solution)/shard_map/ppermute | solution.py:49
  59.0 4.7 %collective-permute-start.13 = (f32[64,64]{1,0:T(8,128)S(1)}, f32[64,64]{1,0:T(8,128)S(1)}, u32[]{:S(2)}, u32[]{:S(2)}) collective-permute-start(f32[64,64]{1,0:T(8,128)S(1)} %gram.1.ga_ref), channel_id=1, source_target_pairs={{0,1},{1,0},{2,3},{3,2},{4,5},{5,4},{6,7},{7,6},{8,9},{9,8},{10,11... | collective-permute-start | bytes 49160 | tf_op jit(solution)/shard_map/ppermute | solution.py:362
  63.7 35.8 %copy-start.1 = (bf16[1,1,128,128,128]{4,3,2,1,0:T(8,128)(2,1)S(1)}, bf16[1,1,128,128,128]{4,3,2,1,0:T(8,128)(2,1)}, u32[]{:S(2)}) copy-start(bf16[1,1,128,128,128]{4,3,2,1,0:T(8,128)(2,1)} %param.7) | copy-start | bytes 12582916
  63.7 35.8 %copy-start.3 = (s32[1,1,128]{2,1,0:T(1,128)S(1)}, s32[1,1,128]{2,1,0:T(1,128)}, u32[]{:S(2)}) copy-start(s32[1,1,128]{2,1,0:T(1,128)} %param.8) | copy-start | bytes 1540
  65.6 7.3 %collective-permute-start.14 = (bf16[64,2048]{1,0:T(8,128)(2,1)S(1)}, bf16[64,2048]{1,0:T(8,128)(2,1)S(1)}, u32[]{:S(2)}, u32[]{:S(2)}) collective-permute-start(bf16[64,2048]{1,0:T(8,128)(2,1)S(1)} %get-tuple-element.12.ya_ref), channel_id=1, source_target_pairs={{0,1},{1,0},{2,3},{3,2},{4,5},{5,4},{6,7},{7,6},{8,9},{9,8},{10,11... | collective-permute-start | bytes 786440 | tf_op jit(solution)/shard_map/ppermute | solution.py:362
  75.4 2.6 %collective-permute-start.15 = (bf16[8,64,128]{2,1,0:T(8,128)(2,1)S(1)}, bf16[8,64,128]{2,1,0:T(8,128)(2,1)S(1)}, u32[]{:S(2)}, u32[]{:S(2)}) collective-permute-start(bf16[8,64,128]{2,1,0:T(8,128)(2,1)S(1)} %slice.149), channel_id=1, source_target_pairs={{0,2},{2,0},{4,6},{6,4},{8,10},{10,8},{12,14},{14,12},{16,18},{18,... | collective-permute-start | bytes 393224 | tf_op jit(solution)/shard_map/ppermute | solution.py:61
  78.0 3.2 %collective-permute-start.16 = (bf16[4,64,128]{2,1,0:T(8,128)(2,1)S(1)}, bf16[4,64,128]{2,1,0:T(8,128)(2,1)S(1)}, u32[]{:S(2)}, u32[]{:S(2)}) collective-permute-start(bf16[4,64,128]{2,1,0:T(8,128)(2,1)S(1)} %slice.174), channel_id=1, source_target_pairs={{0,4},{2,6},{4,0},{6,2},{8,12},{10,14},{12,8},{14,10},{16,20},{18,... | collective-permute-start | bytes 196616 | tf_op jit(solution)/shard_map/ppermute | solution.py:61
  81.2 5.8 %collective-permute-start.18 = (bf16[4,64,128]{2,1,0:T(8,128)(2,1)S(1)}, bf16[4,64,128]{2,1,0:T(8,128)(2,1)S(1)}, u32[]{:S(2)}, u32[]{:S(2)}) collective-permute-start(bf16[4,64,128]{2,1,0:T(8,128)(2,1)S(1)} %fusion), channel_id=1, source_target_pairs={{0,16},{2,18},{4,20},{6,22},{8,24},{10,26},{12,28},{14,30},{16,0},... | collective-permute-start | bytes 196616 | tf_op jit(solution)/shard_map/ppermute | solution.py:70
  81.4 5.6 %collective-permute-start.19 = (bf16[4,64,128]{2,1,0:T(8,128)(2,1)S(1)}, bf16[4,64,128]{2,1,0:T(8,128)(2,1)S(1)}, u32[]{:S(2)}, u32[]{:S(2)}) collective-permute-start(bf16[4,64,128]{2,1,0:T(8,128)(2,1)S(1)} %fusion), channel_id=1, source_target_pairs={{0,24},{2,26},{4,28},{6,30},{8,16},{10,18},{12,20},{14,22},{16,8},... | collective-permute-start | bytes 196616 | tf_op jit(solution)/shard_map/ppermute | solution.py:70
  83.9 4.0 %collective-permute-start.17 = (bf16[4,64,128]{2,1,0:T(8,128)(2,1)S(1)}, bf16[4,64,128]{2,1,0:T(8,128)(2,1)S(1)}, u32[]{:S(2)}, u32[]{:S(2)}) collective-permute-start(bf16[4,64,128]{2,1,0:T(8,128)(2,1)S(1)} %fusion), channel_id=1, source_target_pairs={{0,8},{2,10},{4,12},{6,14},{8,0},{10,2},{12,4},{14,6},{16,24},{18,... | collective-permute-start | bytes 196616 | tf_op jit(solution)/shard_map/ppermute | solution.py:70
  88.0 3.2 %collective-permute-start.20 = (bf16[4,64,128]{2,1,0:T(8,128)(2,1)S(1)}, bf16[4,64,128]{2,1,0:T(8,128)(2,1)S(1)}, u32[]{:S(2)}, u32[]{:S(2)}) collective-permute-start(bf16[4,64,128]{2,1,0:T(8,128)(2,1)S(1)} %get-tuple-element.17), channel_id=1, source_target_pairs={{0,4},{2,6},{4,0},{6,2},{8,12},{10,14},{12,8},{14,10},{16,20},{18,... | collective-permute-start | bytes 196616 | tf_op jit(solution)/shard_map/ppermute | solution.py:49
  91.2 4.8 %collective-permute-start.21 = (bf16[8,64,128]{2,1,0:T(8,128)(2,1)S(1)}, bf16[8,64,128]{2,1,0:T(8,128)(2,1)S(1)}, u32[]{:S(2)}, u32[]{:S(2)}) collective-permute-start(bf16[8,64,128]{2,1,0:T(8,128)(2,1)S(1)} %pad_maximum_fusion.4), channel_id=1, source_target_pairs={{0,2},{2,0},{4,6},{6,4},{8,10},{10,8},{12,14},{14,12},{16,18},{18,... | collective-permute-start | bytes 393224 | tf_op jit(solution)/shard_map/ppermute | solution.py:49
  96.3 3.2 %collective-permute-start.22 = (f32[128,64]{1,0:T(8,128)S(1)}, f32[128,64]{1,0:T(8,128)S(1)}, u32[]{:S(2)}, u32[]{:S(2)}) collective-permute-start(f32[128,64]{1,0:T(8,128)S(1)} %grams.1.ga_ref), channel_id=1, source_target_pairs={{0,1},{1,0},{2,3},{3,2},{4,5},{5,4},{6,7},{7,6},{8,9},{9,8},{10,11... | collective-permute-start | bytes 98312 | tf_op jit(solution)/shard_map/ppermute | solution.py:362

commit v2 on v1

v2 whole, which is shorter than its diff:
```python
import functools
import math

import jax
import jax.numpy as jnp
from jax import lax
from jax.experimental import pallas as pl
from jax.experimental.pallas import tpu as pltpu
from jax.sharding import PartitionSpec as P

ITERS = 2
F32 = jnp.float32
BF16 = jnp.bfloat16
VMEM = pl.BlockSpec(memory_space=pltpu.VMEM)
SMEM = pl.BlockSpec(memory_space=pltpu.SMEM)
NT = (((1,), (1,)), ((), ()))
NN = (((1,), (0,)), ((), ()))


def xor_pairs(size, mask):
    return [(i, i ^ mask) for i in range(size)]


def bit_groups(size):
    bits = size.bit_length() - 1
    groups, at = [], 0
    while at < bits:
        width = 1 if at < 2 else min(2, bits - at)
        groups.append((at, width))
        at += width
    return groups


def position_of(index, size):
    place = index * 0
    for at, width in bit_groups(size):
        place = place * (1 << width) + ((index >> at) & ((1 << width) - 1))
    return place


def gather_blocks(held, axis, size, groups, before=None):
    for number, (at, width) in enumerate(reversed(groups)):
        if before is not None:
            held = before(number - len(groups), held)
        got = [held]
        for k in range(1, 1 << width):
            got.append(lax.ppermute(held, axis, xor_pairs(size, k << at)))
        held = jnp.concatenate(got, axis=0)
    return held


def reduce_blocks(near, far, axis, size):
    groups = bit_groups(size)
    other = lax.ppermute(far.astype(BF16), axis, xor_pairs(size, 1))
    parts = near.astype(F32) + other.astype(F32)
    for at, width in groups[1:-1]:
        ways = 1 << width
        pieces = parts.reshape((ways, parts.shape[0] // ways) + parts.shape[1:])
        total = pieces[0].astype(F32)
        got = [
            lax.ppermute(pieces[k].astype(BF16), axis, xor_pairs(size, k << at))
            for k in range(1, ways)
        ]
        for piece in got:
            total = total + piece.astype(F32)
        parts = total
    at, width = groups[-1]
    mine = parts.astype(BF16)
    total = mine.astype(F32)
    got = [lax.ppermute(mine, axis, xor_pairs(size, k << at)) for k in range(1, 1 << width)]
    for k, piece in enumerate(got, 1):
        total = total + jnp.stack([piece[j ^ k] for j in range(1 << width)]).astype(F32)
    return total


def y_of(q_cat, r_ref, at, users):
    return lax.dot_general(
        q_cat, r_ref[at : at + users, :], NT, preferred_element_type=F32
    )


def cat_tiles(ref, rows):
    return jnp.concatenate([ref[t, rows, :] for t in range(ref.shape[0])], axis=1)


def prepare_kernel(a_ref, at_ref, r_ref):
    tile = 128

    def clear(i, carry):
        r_ref[pl.ds(pl.multiple_of(i * tile, tile), tile), :] = jnp.zeros(
            (tile, r_ref.shape[1]), BF16
        )
        return carry

    lax.fori_loop(0, r_ref.shape[0] // tile, clear, 0)
    for t in range(at_ref.shape[0] // tile):
        cols = slice(t * tile, (t + 1) * tile)
        at_ref[cols, :] = a_ref[:, cols].astype(F32).T.astype(BF16)


def first_kernel(slot_ref, vals_ref, at_ref, bq_ref, _, r_ref, y_ref):
    tile = vals_ref.shape[1]
    rank = bq_ref.shape[1] // 2
    count = slot_ref[2, 0]
    group = math.gcd(vals_ref.shape[0], 32)

    def body(i, carry):
        for j in range(group):
            slot = i * group + j
            row = pl.multiple_of(slot_ref[0, slot] * tile, tile)
            pos = slot_ref[1, slot]
            pred = lax.dot_general(
                at_ref[pl.ds(row, tile), :],
                bq_ref[pos, :rank, :],
                NN,
                preferred_element_type=F32,
            )
            kept = jnp.where(slot < count, 1.0, 0.0)
            resid = (pred - vals_ref[slot].astype(F32)) * kept
            r_ref[pl.ds(row, tile), pl.ds(pl.multiple_of(pos * tile, tile), tile)] = resid.astype(
                BF16
            )
        return carry

    lax.fori_loop(0, (count + group - 1) // group, body, 0)
    y_ref[...] = y_of(cat_tiles(bq_ref, slice(rank, 2 * rank)), r_ref, 0, y_ref.shape[1]).astype(
        BF16
    )


def omega_kernel(at, bq_ref, r_ref, y_ref):
    rank = bq_ref.shape[1] // 2
    y_ref[...] = y_of(cat_tiles(bq_ref, slice(rank, 2 * rank)), r_ref, at, y_ref.shape[1]).astype(
        BF16
    )


def z_of(ya_ref, yb_ref, r_ref, at, z_ref, first, old_ref):
    tile = z_ref.shape[2]
    users = ya_ref.shape[1]
    y = (ya_ref[...].astype(F32) + yb_ref[...].astype(F32)).astype(BF16)
    wide = math.gcd(z_ref.shape[0], 8)
    for i in range(0, z_ref.shape[0], wide):
        z = lax.dot_general(
            y,
            r_ref[at : at + users, (first + i) * tile : (first + i + wide) * tile],
            NN,
            preferred_element_type=F32,
        )
        for j in range(wide):
            part = z[:, j * tile : (j + 1) * tile]
            if old_ref is not None:
                part = part + old_ref[first + i + j]
            z_ref[i + j] = part.astype(z_ref.dtype)


def z_first_kernel(ya_ref, yb_ref, r_ref, z_ref):
    z_of(ya_ref, yb_ref, r_ref, 0, z_ref, 0, None)


def z_second_kernel(first, ya_ref, yb_ref, r_ref, old_ref, z_ref):
    z_of(ya_ref, yb_ref, r_ref, ya_ref.shape[1], z_ref, first, old_ref)


def gram_kernel(z_ref, g_ref):
    z = cat_tiles(z_ref, slice(None))
    g_ref[...] = lax.dot_general(z, z, NT, preferred_element_type=F32)


def grams_kernel(old_ref, z_ref, g_ref):
    z = cat_tiles(z_ref, slice(None))
    old = cat_tiles(old_ref, slice(None))
    both = jnp.concatenate([z, old], axis=0)
    g_ref[...] = lax.dot_general(both, z, NT, preferred_element_type=F32)


def chol_inverse(grams):
    rank = grams[0].shape[0]
    wide = 8
    blocks = rank // wide
    rows = lax.broadcasted_iota(jnp.int32, (wide, 2 * rank), 0)
    lanes = lax.broadcasted_iota(jnp.int32, (wide, 2 * rank), 1)
    mats = []
    for g in grams:
        padded = jnp.concatenate([g, jnp.zeros_like(g)], axis=1)
        mats.append(
            [
                jnp.where(lanes == rows + (rank + i * wide), 1.0, padded[i * wide : (i + 1) * wide])
                for i in range(blocks)
            ]
        )
    for p in range(blocks):
        below = range(p, blocks)
        cols = [
            [
                {
                    i: jnp.broadcast_to(
                        mat[i][:, p * wide + k : p * wide + k + 1], (wide, 2 * rank)
                    )
                    for i in below
                }
                for k in range(wide)
            ]
            for mat in mats
        ]
        for k in range(0, wide, 2):
            for mat, col in zip(mats, cols):
                d = col[k][p][k : k + 1, :]
                e = col[k][p][k + 1 : k + 2, :]
                f = col[k + 1][p][k + 1 : k + 2, :]
                first = 1.0 / d
                second = d / (d * f - e * e)
                ratio = e * first
                row = mat[p][k : k + 1, :] * first
                next_row = mat[p][k + 1 : k + 2, :] - mat[p][k : k + 1, :] * ratio
                next_scaled = next_row * second
                one, two = {}, {}
                for i in below:
                    one[i] = col[k][i]
                    two[i] = col[k + 1][i] - col[k][i] * ratio
                    if i == p:
                        one[i] = jnp.where(rows > k, one[i], 0.0)
                        two[i] = jnp.where(rows > k + 1, two[i], 0.0)
                heads = {}
                for q in range(k + 2, wide):
                    top = col[q][p][k : k + 1, :]
                    heads[q] = (
                        top * first,
                        (col[q][p][k + 1 : k + 2, :] - top * ratio) * second,
                    )
                for i in below:
                    mat[i] = mat[i] - one[i] * row - two[i] * next_scaled
                    for q in range(k + 2, wide):
                        col[q][i] = col[q][i] - one[i] * heads[q][0] - two[i] * heads[q][1]
    result = []
    for mat in mats:
        out = []
        for i in range(blocks):
            diagonal = jnp.sum(
                jnp.where(lanes == rows + i * wide, mat[i], 0.0), axis=1, keepdims=True
            )
            out.append(mat[i][:, rank:] * lax.rsqrt(diagonal))
        result.append(jnp.concatenate(out, axis=0))
    return result


def two_parts(mat):
    high = mat.astype(BF16)
    return high, (mat - high.astype(F32)).astype(BF16)


def apply_inverse(inverse, mat):
    high, low = two_parts(inverse)
    return lax.dot_general(
        jnp.concatenate([high, low], axis=1),
        jnp.concatenate([mat, mat], axis=0),
        NN,
        preferred_element_type=F32,
    )


def apply_wide(inverse, mat):
    high, low = two_parts(inverse)
    part, rest = two_parts(mat)
    return lax.dot_general(
        jnp.concatenate([high, low, high], axis=1),
        jnp.concatenate([part, part, rest], axis=0),
        NN,
        preferred_element_type=F32,
    )


def y_kernel(z_ref, r_ref, y_ref):
    y_ref[...] = y_of(cat_tiles(z_ref, slice(None)), r_ref, 0, y_ref.shape[1])


def scale_kernel(ga_ref, gb_ref, y_ref, inv_ref, out_ref):
    (inverse,) = chol_inverse([ga_ref[...] + gb_ref[...]])
    inv_ref[...] = inverse
    out_ref[...] = apply_wide(inverse, y_ref[...]).astype(BF16)


def y_scaled_kernel(at, inv_ref, z_ref, r_ref, out_ref):
    y = y_of(cat_tiles(z_ref, slice(None)), r_ref, at, out_ref.shape[1])
    out_ref[...] = apply_wide(inv_ref[...], y).astype(BF16)


def last_kernel(
    radius,
    user_scale,
    item_scale,
    slot_any,
    ga_ref,
    gb_ref,
    inv_ref,
    z_ref,
    share_ref,
    ya_0,
    ya_1,
    yb_0,
    yb_1,
    vals_ref,
    at_ref,
    bq_ref,
    user_ref,
    item_ref,
    loss_ref,
    left,
    right,
    slot_ref,
    slot_sem,
):
    slot_copy = pltpu.make_async_copy(slot_any, slot_ref, slot_sem)
    slot_copy.start()
    ya_refs, yb_refs = (ya_0, ya_1), (yb_0, yb_1)
    tile = vals_ref.shape[1]
    rank = z_ref.shape[1]
    gram = ga_ref[...] + gb_ref[...]
    y_gram = lax.dot_general(
        inv_ref[...], gram[rank:], NN, precision=lax.Precision.HIGHEST, preferred_element_type=F32
    )
    z_inv, y_inv = chol_inverse([gram[:rank], y_gram])
    for t in range(z_ref.shape[0]):
        q = apply_inverse(z_inv, z_ref[t]).astype(BF16)
        right[t, :rank] = bq_ref[t, :rank, :]
        right[t, rank : 2 * rank] = q
        right[t, 2 * rank : 3 * rank] = q
    tiles = ya_refs[0].shape[1] // tile
    for t in range(user_ref.shape[1] // tile):
        cols = slice(t * tile, (t + 1) * tile)
        here = slice(t % tiles * tile, (t % tiles + 1) * tile)
        y = ya_refs[t // tiles][:, here].astype(F32) + yb_refs[t // tiles][:, here].astype(F32)
        y_hat = apply_wide(y_inv, y)
        user_ref[:, cols] = y_hat * user_scale
        y_hat = y_hat.astype(BF16).astype(F32)
        turned = (y_hat * (-0.5 * radius)).T
        high, low = two_parts(turned)
        half = at_ref[cols, :].astype(F32) * 0.5
        left[cols, :] = jnp.concatenate([half.astype(BF16), high, low], axis=1)
    item_ref[...] = apply_wide(z_inv, share_ref[...]) * item_scale
    loss_ref[...] = jnp.zeros_like(loss_ref)
    slot_copy.wait()
    count = slot_ref[2, 0]
    many = math.gcd(vals_ref.shape[0], 64)
    few = math.gcd(many, 8)
    place = lax.broadcasted_iota(jnp.int32, (few, tile), 0)

    def losses(start, slots):
        for g in range(0, slots, few):
            at = pl.multiple_of(start + g, few)
            sums = []
            for j in range(few):
                slot = at + j
                row = pl.multiple_of(slot_ref[0, slot] * tile, tile)
                fresh = lax.dot_general(
                    left[pl.ds(row, tile), :],
                    right[slot_ref[1, slot]],
                    NN,
                    preferred_element_type=F32,
                )
                fresh = fresh - vals_ref[slot].astype(F32)
                sums.append(jnp.sum(fresh * fresh, axis=-1))
            total = jnp.where(place + at < count, jnp.stack(sums, axis=0), 0.0)
            loss_ref[pl.ds(at, few), :] = total * (1.0 / tile)

    def loop(start, stop, slots):
        def body(i, carry):
            losses(start + i * slots, slots)
            return carry

        return lax.fori_loop(0, (stop - start) // slots, body, 0)

    whole = count // many * many
    some = math.gcd(many, 16)
    loop(0, whole, many)
    loop(whole, (count + some - 1) // some * some, some)


def shards(tile_vals, tile_row, tile_col, tile_count, fac_a, fac_b, omega):
    ratings = tile_vals[0, 0]
    cap, tile, _ = ratings.shape
    rank, users_dev = fac_a.shape
    share = fac_b.shape[1]
    n_user = lax.axis_size("user")
    n_item = lax.axis_size("item")
    items_dev = share * n_user
    item_tiles = items_dev // tile
    users, items = users_dev * n_user, items_dev * n_item
    radius = math.sqrt(users * items / rank)
    me = lax.axis_index("user").astype(jnp.int32)

    by_tile = share == tile
    if not by_tile:
        order = position_of(jnp.arange(n_user, dtype=jnp.int32) ^ me, n_user)

    def to_tiles(blocks):
        if by_tile:
            return blocks
        blocks = blocks[order]
        wide = blocks.transpose(1, 0, 2).reshape(blocks.shape[1], item_tiles, tile)
        return wide.transpose(1, 0, 2)

    def to_blocks(tiles):
        if by_tile:
            return tiles
        wide = tiles.transpose(1, 0, 2).reshape(tiles.shape[1], n_user, share)
        return jnp.zeros((n_user, tiles.shape[1], share), tiles.dtype).at[order].set(
            wide.transpose(1, 0, 2)
        )

    def across(mine):
        bit = 1
        while True:
            other = lax.ppermute(mine, "item", xor_pairs(n_item, bit))
            bit *= 2
            if bit >= n_item:
                return mine, other
            mine = (mine.astype(F32) + other.astype(F32)).astype(mine.dtype)

    def reduced(near, far):
        if not by_tile:
            near, far = jnp.split(to_blocks(jnp.concatenate([near, far.astype(F32)])), 2)
        total = reduce_blocks(near, far, "user", n_user)
        groups = bit_groups(n_user)[:-1]
        return to_tiles(gather_blocks(total.astype(BF16), "user", n_user, groups)), total[0]

    def call(kernel, outs, name, *args, smem=0, hbm=0, flops=0, vmem=16, **more):
        outs = [jax.ShapeDtypeStruct(shape, dtype) for shape, dtype in outs]
        got = pl.pallas_call(
            kernel,
            out_shape=outs,
            in_specs=[SMEM] * smem
            + [pl.BlockSpec(memory_space=pl.ANY)] * hbm
            + [VMEM] * (len(args) - smem - hbm),
            out_specs=[VMEM] * len(outs),
            compiler_params=pltpu.CompilerParams(vmem_limit_bytes=vmem << 20),
            cost_estimate=pl.CostEstimate(flops=flops, bytes_accessed=1 << 16, transcendentals=0),
            name=name,
            **more,
        )(*args)
        return got[0] if len(outs) == 1 else got

    half = users_dev // 2
    r_shape = ((users_dev, items_dev), BF16)
    y_bf16, y_f32 = ((rank, half), BF16), ((rank, half), F32)
    z_bf16, z_f32 = ((item_tiles, rank, tile), BF16), ((item_tiles, rank, tile), F32)
    half_flops = 2 * rank * half * items_dev

    work = [fac_a, tile_row, tile_col, tile_count]

    def before(number, held):
        if number == 1 - len(bit_groups(n_user)):
            held, work[:] = lax.optimization_barrier((held, list(work)))
            user_factor, rows, cols, count = work
            cols = cols[0, 0]
            if by_tile:
                cols = position_of(cols ^ me, n_user)
            slots = jnp.stack([rows[0, 0], cols, jnp.broadcast_to(count[0, 0], (cap,))])
            a_t, cleared = call(
                prepare_kernel,
                [((users_dev, rank), BF16), r_shape],
                "prepare",
                user_factor,
                flops=1 << 31,
            )
            work[:] = [a_t, slots, cleared]
        elif number == -1:
            held, work[:2] = lax.optimization_barrier((held, list(work[:2])))
        return held

    both = lax.optimization_barrier(jnp.concatenate([fac_b, omega], axis=0))
    bq = to_tiles(gather_blocks(both[None], "user", n_user, bit_groups(n_user), before))
    a_t, slots, cleared = work

    def z_both(firsts, seconds):
        z = call(z_first_kernel, [z_f32], "z_first", *firsts, resid, flops=half_flops)
        near, far = item_tiles // 2, item_tiles - item_tiles // 2
        parts = (*seconds, resid, z)
        far = call(
            functools.partial(z_second_kernel, near),
            [((far, rank, tile), BF16)],
            "z_far",
            *parts,
            flops=half_flops // 2,
        )
        near = call(
            functools.partial(z_second_kernel, 0),
            [((near, rank, tile), F32)],
            "z_near",
            *parts,
            flops=half_flops // 2,
        )
        return reduced(near, far)

    resid, y_0 = call(
        first_kernel,
        [r_shape, y_bf16],
        "resid_y",
        slots,
        ratings,
        a_t,
        bq,
        cleared,
        smem=1,
        input_output_aliases={4: 0},
    )
    firsts = across(y_0)
    y_1 = call(functools.partial(omega_kernel, half), [y_bf16], "y_omega", bq, resid, flops=half_flops)
    old, _ = z_both(firsts, across(y_1))

    gram = across(call(gram_kernel, [((rank, rank), F32)], "gram", old))
    y_0 = call(y_kernel, [y_f32], "y_first", old, resid, flops=half_flops)
    inverse, y_0 = call(scale_kernel, [((rank, rank), F32), y_bf16], "scale_y", *gram, y_0)
    firsts = across(y_0)
    y_1 = call(
        functools.partial(y_scaled_kernel, half),
        [y_bf16],
        "y_second",
        inverse,
        old,
        resid,
        flops=half_flops,
    )
    seconds = across(y_1)
    z, z_share = z_both(firsts, seconds)

    grams = across(call(grams_kernel, [((2 * rank, rank), F32)], "grams", old, z))
    user_dir, item_dir, losses = call(
        functools.partial(last_kernel, radius, math.sqrt(users), math.sqrt(items)),
        [((rank, users_dev), F32), ((rank, share), F32), ((cap, tile), F32)],
        "loss",
        slots,
        *grams,
        inverse,
        z,
        z_share,
        firsts[0],
        seconds[0],
        firsts[1],
        seconds[1],
        ratings,
        a_t,
        bq,
        hbm=1,
        scratch_shapes=[
            pltpu.VMEM((users_dev, 3 * rank), BF16),
            pltpu.VMEM((item_tiles, 3 * rank, tile), BF16),
            pltpu.SMEM((3, cap), jnp.int32),
            pltpu.SemaphoreType.DMA,
        ],
    )
    return (user_dir, item_dir, losses[None, None])


def solution(mesh):
    return jax.shard_map(
        shards,
        mesh=mesh,
        in_specs=(
            P("user", "item", None, None, None),
            P("user", "item", None),
            P("user", "item", None),
            P("user", "item"),
            P(None, "user"),
            P(None, ("item", "user")),
            P(None, ("item", "user")),
        ),
        out_specs=(P(None, "user"), P(None, ("item", "user")), P("user", "item", None, None)),
        check_vma=False,
    )
```

time: 113 us -> 93.2 us (0.82)
  Pallas kernels: 34.1 us -> 21.8 us
  waiting for transfers between devices: 43.6 us -> 34.1 us
  starting transfers between devices: 26.3 us -> 30.5 us
  local copies, waits for them, and re-layouts: 4.29 us -> 1.14 us
    pallas_call x8 -> x15, Pallas kernels: 34.1 us -> 21.8 us  [call(): pl.pallas_call(kernel, out_shape=outs, in_specs=[SMEM] * smem + [pl.Block...]
    ppermute x4 -> x6, waiting for transfers between devices: 16.1 us -> 9.5 us  [across(): other = lax.ppermute(mine, 'item', xor_pairs(n_item, bit))]
    ppermute x0 -> x2, starting transfers between devices: none -> 3.61 us  [reduce_blocks(): other = lax.ppermute(far.astype(BF16), axis, xor_pairs(size, 1))]
    unnamed x12 -> x5, local copies, waits for them, and re-layouts: 4.12 us -> 0.97 us
    ppermute x4 -> x2, waiting for transfers between devices: 8.77 us -> 5.82 us  [reduce_blocks(): lax.ppermute(pieces[k].astype(BF16), axis, xor_pairs(size, k << at))]
    ppermute x4 -> x6, starting transfers between devices: 2.78 us -> 5.16 us  [across(): other = lax.ppermute(mine, 'item', xor_pairs(n_item, bit))]
    ppermute x4 -> x2, starting transfers between devices: 1.97 us -> 0.53 us  [reduce_blocks(): lax.ppermute(pieces[k].astype(BF16), axis, xor_pairs(size, k << at))]
    ppermute x9, waiting for transfers between devices: 11.4 us -> 9.96 us  [gather_blocks(): got.append(lax.ppermute(held, axis, xor_pairs(size, k << at)))]
  transfers between devices with their start and end apart: 23 -> 25, of which waited for: 19 -> 23; matrix products, arithmetic and copies ran while one was open for 2% -> 2% of each run, Pallas kernels for 3% -> 8%
where the time goes in v2:
time: 93.2 us; the launch traced here: 91.7 us
  waiting for transfers between devices  34.1 us (37%)
  starting transfers between devices  30.5 us (33%)
  Pallas kernels  21.8 us (23%)
  other arithmetic  2.43 us (3%)
  between operations  1.66 us (2%)
  local copies, waits for them, and re-layouts  1.14 us (1%)
    pallas_call x15, Pallas kernels, call(): pl.pallas_call(kernel, out_shape=outs, in_specs=[SMEM] * smem + [pl.Block...  21.8 us
    ppermute x9, starting transfers between devices, gather_blocks(): got.append(lax.ppermute(held, axis, xor_pairs(size, k << at)))  15.1 us
    ppermute x9, waiting for transfers between devices, gather_blocks(): got.append(lax.ppermute(held, axis, xor_pairs(size, k << at)))  9.96 us
    ppermute x6, waiting for transfers between devices, across(): other = lax.ppermute(mine, 'item', xor_pairs(n_item, bit))  9.5 us
    ppermute x6, waiting for transfers between devices, reduce_blocks(): lax.ppermute(mine, axis, xor_pairs(size, k << at))  7.86 us
    ppermute x6, starting transfers between devices, reduce_blocks(): lax.ppermute(mine, axis, xor_pairs(size, k << at))  6.12 us
    ppermute x2, waiting for transfers between devices, reduce_blocks(): lax.ppermute(pieces[k].astype(BF16), axis, xor_pairs(size, k << at))  5.82 us
    ppermute x6, starting transfers between devices, across(): other = lax.ppermute(mine, 'item', xor_pairs(n_item, bit))  5.16 us
  transfers between devices with their start and end apart: 25, of which 23 were waited for; matrix products, arithmetic and copies ran while one was open for 2% of the time, Pallas kernels for 8%

profile of v2, /device:TPU:29, one launch (start us, length us, event | category | flops | bytes accessed | tf_op | source)
XLA Modules:
  0.0 91.7 jit_solution(9509110103578103626)
XLA Ops:
  1.4 1.3 %collective-permute-start.1 = (bf16[1,128,128]{2,1,0:T(8,128)(2,1)S(1)}, bf16[1,128,128]{2,1,0:T(8,128)(2,1)S(1)}, u32[]{:S(2)}, u32[]{:S(2)}) collective-permute-start(bf16[1,128,128]{2,1,0:T(8,128)(2,1)S(1)} %bitcast.15), channel_id=1, source_target_pairs={{0,16},{2,18},{4,20},{6,22},{8,24},{10,26},{12,28},{14,30},{16,0},... | collective-permute-start | bytes 98312 | tf_op jit(solution)/shard_map/ppermute | solution.py:47
  2.7 2.2 %collective-permute-start = (bf16[1,128,128]{2,1,0:T(8,128)(2,1)S(1)}, bf16[1,128,128]{2,1,0:T(8,128)(2,1)S(1)}, u32[]{:S(2)}, u32[]{:S(2)}) collective-permute-start(bf16[1,128,128]{2,1,0:T(8,128)(2,1)S(1)} %bitcast.16), channel_id=1, source_target_pairs={{0,8},{2,10},{4,12},{6,14},{8,0},{10,2},{12,4},{14,6},{16,24},{18,... | collective-permute-start | bytes 98312 | tf_op jit(solution)/shard_map/ppermute | solution.py:47
  10.5 2.9 %collective-permute-start.4 = (bf16[8,128,128]{2,1,0:T(8,128)(2,1)S(1)}, bf16[8,128,128]{2,1,0:T(8,128)(2,1)S(1)}, u32[]{:S(2)}, u32[]{:S(2)}) collective-permute-start(bf16[8,128,128]{2,1,0:T(8,128)(2,1)S(1)} %pad_maximum_fusion), channel_id=1, source_target_pairs={{0,2},{2,0},{4,6},{6,4},{8,10},{10,8},{12,14},{14,12},{16,18},{18,... | collective-permute-start | bytes 786440 | tf_op jit(solution)/shard_map/ppermute | solution.py:47
  13.5 1.1 %collective-permute-done.4 = bf16[8,128,128]{2,1,0:T(8,128)(2,1)S(1)} collective-permute-done((bf16[8,128,128]{2,1,0:T(8,128)(2,1)S(1)}, bf16[8,128,128]{2,1,0:T(8,128)(2,1)S(1)}, u32[]{:S(2)}, u32[]{:S(2)}) %collective-permute-start.4) | collective-permute-done | bytes 262176 | tf_op jit(solution)/shard_map/ppermute | solution.py:47
  14.7 3.9 %resid_y.1 = (bf16[2048,2048]{1,0:T(8,128)(2,1)S(1)}, bf16[64,1024]{1,0:T(8,128)(2,1)S(1)}) custom-call(s32[3,128]{1,0:T(4,128)S(1)} %add_add_fusion.slot_ref.slot_any, bf16[128,128,128]{2,1,0:T(8,128)(2,1)S(1)} %bitcast.12, bf16[2048,64]{1,0:T(8,128)(2,1)S(1)} %get-tuple-element.28.at_ref, ...), custom_call_target="tpu_custom_call", output_to_operand_aliasing={{0}: (4, {})} | custom-call | bytes 65536 | tf_op jit(solution)/shard_map/resid_y/pallas_call | solution.py:429
  18.6 1.3 %collective-permute-start.6 = (bf16[64,1024]{1,0:T(8,128)(2,1)S(1)}, bf16[64,1024]{1,0:T(8,128)(2,1)S(1)}, u32[]{:S(2)}, u32[]{:S(2)}) collective-permute-start(bf16[64,1024]{1,0:T(8,128)(2,1)S(1)} %get-tuple-element.31.ya_ref), channel_id=1, source_target_pairs={{0,1},{1,0},{2,3},{3,2},{4,5},{5,4},{6,7},{7,6},{8,9},{9,8},{10,11... | collective-permute-start | bytes 393224 | tf_op jit(solution)/shard_map/ppermute | solution.py:414
  19.8 1.4 %y_omega.1.ya_ref = bf16[64,1024]{1,0:T(8,128)(2,1)S(1)} custom-call(bf16[16,128,128]{2,1,0:T(8,128)(2,1)S(1)} %constant_dynamic-update-slice_fusion.bq_ref, bf16[2048,2048]{1,0:T(8,128)(2,1)S(1)} %get-tuple-element.30.r_ref), custom_call_target="tpu_custom_call" | custom-call | flops 268435456 | bytes 65536 | tf_op jit(solution)/shard_map/y_omega/pallas_call | solution.py:429
  21.5 1.8 %collective-permute-done.6.yb_ref = bf16[64,1024]{1,0:T(8,128)(2,1)S(1)} collective-permute-done((bf16[64,1024]{1,0:T(8,128)(2,1)S(1)}, bf16[64,1024]{1,0:T(8,128)(2,1)S(1)}, u32[]{:S(2)}, u32[]{:S(2)}) %collective-permute-start.6) | collective-permute-done | bytes 131104 | tf_op jit(solution)/shard_map/ppermute | solution.py:414
  24.2 1.8 %collective-permute-done.5.yb_ref = bf16[64,1024]{1,0:T(8,128)(2,1)S(1)} collective-permute-done((bf16[64,1024]{1,0:T(8,128)(2,1)S(1)}, bf16[64,1024]{1,0:T(8,128)(2,1)S(1)}, u32[]{:S(2)}, u32[]{:S(2)}) %collective-permute-start.5) | collective-permute-done | bytes 131104 | tf_op jit(solution)/shard_map/ppermute | solution.py:414
  26.5 1.4 %collective-permute-start.7 = (bf16[8,64,128]{2,1,0:T(8,128)(2,1)S(1)}, bf16[8,64,128]{2,1,0:T(8,128)(2,1)S(1)}, u32[]{:S(2)}, u32[]{:S(2)}) collective-permute-start(bf16[8,64,128]{2,1,0:T(8,128)(2,1)S(1)} %z_far.2), channel_id=1, source_target_pairs={{0,2},{2,0},{4,6},{6,4},{8,10},{10,8},{12,14},{14,12},{16,18},{18,... | collective-permute-start | bytes 393224 | tf_op jit(solution)/shard_map/ppermute | solution.py:54
  29.0 3.1 %collective-permute-done.8 = bf16[4,64,128]{2,1,0:T(8,128)(2,1)S(1)} collective-permute-done((bf16[4,64,128]{2,1,0:T(8,128)(2,1)S(1)}, bf16[4,64,128]{2,1,0:T(8,128)(2,1)S(1)}, u32[]{:S(2)}, u32[]{:S(2)}) %collective-permute-start.8) | collective-permute-done | bytes 65568 | tf_op jit(solution)/shard_map/ppermute | solution.py:61
  32.2 3.3 %collective-permute-start.11 = (bf16[4,64,128]{2,1,0:T(8,128)(2,1)S(1)}, bf16[4,64,128]{2,1,0:T(8,128)(2,1)S(1)}, u32[]{:S(2)}, u32[]{:S(2)}) collective-permute-start(bf16[4,64,128]{2,1,0:T(8,128)(2,1)S(1)} %fusion.1), channel_id=1, source_target_pairs={{0,24},{2,26},{4,28},{6,30},{8,16},{10,18},{12,20},{14,22},{16,8},... | collective-permute-start | bytes 196616 | tf_op jit(solution)/shard_map/ppermute | solution.py:70
  36.2 1.8 %collective-permute-done.11 = bf16[4,64,128]{2,1,0:T(8,128)(2,1)S(1)} collective-permute-done((bf16[4,64,128]{2,1,0:T(8,128)(2,1)S(1)}, bf16[4,64,128]{2,1,0:T(8,128)(2,1)S(1)}, u32[]{:S(2)}, u32[]{:S(2)}) %collective-permute-start.11) | collective-permute-done | bytes 65568 | tf_op jit(solution)/shard_map/ppermute | solution.py:70
  38.0 1.4 %collective-permute-done.9 = bf16[4,64,128]{2,1,0:T(8,128)(2,1)S(1)} collective-permute-done((bf16[4,64,128]{2,1,0:T(8,128)(2,1)S(1)}, bf16[4,64,128]{2,1,0:T(8,128)(2,1)S(1)}, u32[]{:S(2)}, u32[]{:S(2)}) %collective-permute-start.9) | collective-permute-done | bytes 65568 | tf_op jit(solution)/shard_map/ppermute | solution.py:70
  39.8 2.9 %collective-permute-done.12 = bf16[4,64,128]{2,1,0:T(8,128)(2,1)S(1)} collective-permute-done((bf16[4,64,128]{2,1,0:T(8,128)(2,1)S(1)}, bf16[4,64,128]{2,1,0:T(8,128)(2,1)S(1)}, u32[]{:S(2)}, u32[]{:S(2)}) %collective-permute-start.12) | collective-permute-done | bytes 65568 | tf_op jit(solution)/shard_map/ppermute | solution.py:47
  42.7 3.7 %collective-permute-start.13 = (bf16[8,64,128]{2,1,0:T(8,128)(2,1)S(1)}, bf16[8,64,128]{2,1,0:T(8,128)(2,1)S(1)}, u32[]{:S(2)}, u32[]{:S(2)}) collective-permute-start(bf16[8,64,128]{2,1,0:T(8,128)(2,1)S(1)} %pad_maximum_fusion.4), channel_id=1, source_target_pairs={{0,2},{2,0},{4,6},{6,4},{8,10},{10,8},{12,14},{14,12},{16,18},{18,... | collective-permute-start | bytes 393224 | tf_op jit(solution)/shard_map/ppermute | solution.py:47
  46.4 1.0 %collective-permute-done.13 = bf16[8,64,128]{2,1,0:T(8,128)(2,1)S(1)} collective-permute-done((bf16[8,64,128]{2,1,0:T(8,128)(2,1)S(1)}, bf16[8,64,128]{2,1,0:T(8,128)(2,1)S(1)}, u32[]{:S(2)}, u32[]{:S(2)}) %collective-permute-start.13) | collective-permute-done | bytes 131104 | tf_op jit(solution)/shard_map/ppermute | solution.py:47
  47.6 1.0 %collective-permute-start.14 = (f32[64,64]{1,0:T(8,128)S(1)}, f32[64,64]{1,0:T(8,128)S(1)}, u32[]{:S(2)}, u32[]{:S(2)}) collective-permute-start(f32[64,64]{1,0:T(8,128)S(1)} %gram.1.ga_ref), channel_id=1, source_target_pairs={{0,1},{1,0},{2,3},{3,2},{4,5},{5,4},{6,7},{7,6},{8,9},{9,8},{10,11... | collective-permute-start | bytes 49160 | tf_op jit(solution)/shard_map/ppermute | solution.py:414
  48.6 1.4 %y_first.1.y_ref = f32[64,1024]{1,0:T(8,128)S(1)} custom-call(bf16[16,64,128]{2,1,0:T(8,128)(2,1)S(1)} %pad_maximum_fusion.1.z_ref.old_ref, bf16[2048,2048]{1,0:T(8,128)(2,1)S(1)} %get-tuple-element.30.r_ref), custom_call_target="tpu_custom_call" | custom-call | flops 268435456 | bytes 65536 | tf_op jit(solution)/shard_map/y_first/pallas_call | solution.py:429
  50.4 1.6 %scale_y.1 = (f32[64,64]{1,0:T(8,128)S(1)}, bf16[64,1024]{1,0:T(8,128)(2,1)S(1)}) custom-call(f32[64,64]{1,0:T(8,128)S(1)} %gram.1.ga_ref, f32[64,64]{1,0:T(8,128)S(1)} %collective-permute-done.14.gb_ref, f32[64,1024]{1,0:T(8,128)S(1)} %y_first.1.y_ref), custom_call_target="tpu_custom_call" | custom-call | bytes 65536 | tf_op jit(solution)/shard_map/scale_y/pallas_call | solution.py:429
  53.0 1.5 %y_second.1.ya_ref.ya_1 = bf16[64,1024]{1,0:T(8,128)(2,1)S(1)} custom-call(f32[64,64]{1,0:T(8,128)S(1)} %get-tuple-element.32.inv_ref, bf16[16,64,128]{2,1,0:T(8,128)(2,1)S(1)} %pad_maximum_fusion.1.z_ref.old_ref, bf16[2048,2048]{1,0:T(8,128)(2,1)S(1)} %get-tuple-element.30.r_ref), custom_call_target="tpu_custom_call" | custom-call | flops 268435456 | bytes 65536 | tf_op jit(solution)/shard_map/y_second/pallas_call | solution.py:429
  56.8 2.5 %collective-permute-done.15.yb_ref.yb_1 = bf16[64,1024]{1,0:T(8,128)(2,1)S(1)} collective-permute-done((bf16[64,1024]{1,0:T(8,128)(2,1)S(1)}, bf16[64,1024]{1,0:T(8,128)(2,1)S(1)}, u32[]{:S(2)}, u32[]{:S(2)}) %collective-permute-start.15) | collective-permute-done | bytes 131104 | tf_op jit(solution)/shard_map/ppermute | solution.py:414
  59.8 2.2 %collective-permute-start.17 = (bf16[8,64,128]{2,1,0:T(8,128)(2,1)S(1)}, bf16[8,64,128]{2,1,0:T(8,128)(2,1)S(1)}, u32[]{:S(2)}, u32[]{:S(2)}) collective-permute-start(bf16[8,64,128]{2,1,0:T(8,128)(2,1)S(1)} %z_far.3), channel_id=1, source_target_pairs={{0,2},{2,0},{4,6},{6,4},{8,10},{10,8},{12,14},{14,12},{16,18},{18,... | collective-permute-start | bytes 393224 | tf_op jit(solution)/shard_map/ppermute | solution.py:54
  63.4 2.7 %collective-permute-done.18 = bf16[4,64,128]{2,1,0:T(8,128)(2,1)S(1)} collective-permute-done((bf16[4,64,128]{2,1,0:T(8,128)(2,1)S(1)}, bf16[4,64,128]{2,1,0:T(8,128)(2,1)S(1)}, u32[]{:S(2)}, u32[]{:S(2)}) %collective-permute-start.18) | collective-permute-done | bytes 65568 | tf_op jit(solution)/shard_map/ppermute | solution.py:61
  66.3 2.6 %collective-permute-start.21 = (bf16[4,64,128]{2,1,0:T(8,128)(2,1)S(1)}, bf16[4,64,128]{2,1,0:T(8,128)(2,1)S(1)}, u32[]{:S(2)}, u32[]{:S(2)}) collective-permute-start(bf16[4,64,128]{2,1,0:T(8,128)(2,1)S(1)} %fusion), channel_id=1, source_target_pairs={{0,24},{2,26},{4,28},{6,30},{8,16},{10,18},{12,20},{14,22},{16,8},... | collective-permute-start | bytes 196616 | tf_op jit(solution)/shard_map/ppermute | solution.py:70
  68.9 3.1 %collective-permute-done.20 = bf16[4,64,128]{2,1,0:T(8,128)(2,1)S(1)} collective-permute-done((bf16[4,64,128]{2,1,0:T(8,128)(2,1)S(1)}, bf16[4,64,128]{2,1,0:T(8,128)(2,1)S(1)}, u32[]{:S(2)}, u32[]{:S(2)}) %collective-permute-start.20) | collective-permute-done | bytes 65568 | tf_op jit(solution)/shard_map/ppermute | solution.py:70
  73.5 2.7 %collective-permute-done.22 = bf16[4,64,128]{2,1,0:T(8,128)(2,1)S(1)} collective-permute-done((bf16[4,64,128]{2,1,0:T(8,128)(2,1)S(1)}, bf16[4,64,128]{2,1,0:T(8,128)(2,1)S(1)}, u32[]{:S(2)}, u32[]{:S(2)}) %collective-permute-start.22) | collective-permute-done | bytes 65568 | tf_op jit(solution)/shard_map/ppermute | solution.py:47
  76.2 3.8 %collective-permute-start.23 = (bf16[8,64,128]{2,1,0:T(8,128)(2,1)S(1)}, bf16[8,64,128]{2,1,0:T(8,128)(2,1)S(1)}, u32[]{:S(2)}, u32[]{:S(2)}) collective-permute-start(bf16[8,64,128]{2,1,0:T(8,128)(2,1)S(1)} %pad_maximum_fusion.5), channel_id=1, source_target_pairs={{0,2},{2,0},{4,6},{6,4},{8,10},{10,8},{12,14},{14,12},{16,18},{18,... | collective-permute-start | bytes 393224 | tf_op jit(solution)/shard_map/ppermute | solution.py:47
  80.0 1.0 %collective-permute-done.23 = bf16[8,64,128]{2,1,0:T(8,128)(2,1)S(1)} collective-permute-done((bf16[8,64,128]{2,1,0:T(8,128)(2,1)S(1)}, bf16[8,64,128]{2,1,0:T(8,128)(2,1)S(1)}, u32[]{:S(2)}, u32[]{:S(2)}) %collective-permute-start.23) | collective-permute-done | bytes 131104 | tf_op jit(solution)/shard_map/ppermute | solution.py:47
  81.3 1.0 %collective-permute-start.24 = (f32[128,64]{1,0:T(8,128)S(1)}, f32[128,64]{1,0:T(8,128)S(1)}, u32[]{:S(2)}, u32[]{:S(2)}) collective-permute-start(f32[128,64]{1,0:T(8,128)S(1)} %grams.1.ga_ref), channel_id=1, source_target_pairs={{0,1},{1,0},{2,3},{3,2},{4,5},{5,4},{6,7},{7,6},{8,9},{9,8},{10,11... | collective-permute-start | bytes 98312 | tf_op jit(solution)/shard_map/ppermute | solution.py:414
  82.3 2.2 %collective-permute-done.24.gb_ref = f32[128,64]{1,0:T(8,128)S(1)} collective-permute-done((f32[128,64]{1,0:T(8,128)S(1)}, f32[128,64]{1,0:T(8,128)S(1)}, u32[]{:S(2)}, u32[]{:S(2)}) %collective-permute-start.24) | collective-permute-done | bytes 32800 | tf_op jit(solution)/shard_map/ppermute | solution.py:414
  84.4 7.2 %loss.1 = (f32[64,2048]{1,0:T(8,128)}, f32[64,128]{1,0:T(8,128)}, f32[128,128]{1,0:T(8,128)}) custom-call(s32[3,128]{1,0:T(4,128)S(1)} %add_add_fusion.slot_ref.slot_any, f32[128,64]{1,0:T(8,128)S(1)} %grams.1.ga_ref, f32[128,64]{1,0:T(8,128)S(1)} %collective-permute-done.24.gb_ref, f32[64,64]{1,0:T(8,128)S(1)} %get-tuple-element.32.inv_ref, ...), custom_call_target="tpu_custom_call" | custom-call | bytes 65536 | tf_op jit(solution)/shard_map/loss/pallas_call | solution.py:429
  (64 shorter events, 17.1 us)
Async XLA Ops:
  1.4 4.6 %collective-permute-start.2 = (bf16[1,128,128]{2,1,0:T(8,128)(2,1)S(1)}, bf16[1,128,128]{2,1,0:T(8,128)(2,1)S(1)}, u32[]{:S(2)}, u32[]{:S(2)}) collective-permute-start(bf16[1,128,128]{2,1,0:T(8,128)(2,1)S(1)} %bitcast.14), channel_id=1, source_target_pairs={{0,24},{2,26},{4,28},{6,30},{8,16},{10,18},{12,20},{14,22},{16,8},... | collective-permute-start | bytes 98312 | tf_op jit(solution)/shard_map/ppermute | solution.py:47
  1.4 4.6 %collective-permute-start.1 = (bf16[1,128,128]{2,1,0:T(8,128)(2,1)S(1)}, bf16[1,128,128]{2,1,0:T(8,128)(2,1)S(1)}, u32[]{:S(2)}, u32[]{:S(2)}) collective-permute-start(bf16[1,128,128]{2,1,0:T(8,128)(2,1)S(1)} %bitcast.15), channel_id=1, source_target_pairs={{0,16},{2,18},{4,20},{6,22},{8,24},{10,26},{12,28},{14,30},{16,0},... | collective-permute-start | bytes 98312 | tf_op jit(solution)/shard_map/ppermute | solution.py:47
  2.7 3.9 %collective-permute-start = (bf16[1,128,128]{2,1,0:T(8,128)(2,1)S(1)}, bf16[1,128,128]{2,1,0:T(8,128)(2,1)S(1)}, u32[]{:S(2)}, u32[]{:S(2)}) collective-permute-start(bf16[1,128,128]{2,1,0:T(8,128)(2,1)S(1)} %bitcast.16), channel_id=1, source_target_pairs={{0,8},{2,10},{4,12},{6,14},{8,0},{10,2},{12,4},{14,6},{16,24},{18,... | collective-permute-start | bytes 98312 | tf_op jit(solution)/shard_map/ppermute | solution.py:47
  4.9 9.8 %copy-start = (bf16[1,1,128,128,128]{4,3,2,1,0:T(8,128)(2,1)S(1)}, bf16[1,1,128,128,128]{4,3,2,1,0:T(8,128)(2,1)}, u32[]{:S(2)}) copy-start(bf16[1,1,128,128,128]{4,3,2,1,0:T(8,128)(2,1)} %param.7) | copy-start | bytes 12582916
  6.6 3.9 %collective-permute-start.3 = (bf16[4,128,128]{2,1,0:T(8,128)(2,1)S(1)}, bf16[4,128,128]{2,1,0:T(8,128)(2,1)S(1)}, u32[]{:S(2)}, u32[]{:S(2)}) collective-permute-start(bf16[4,128,128]{2,1,0:T(8,128)(2,1)S(1)} %pad_maximum_fusion.3), channel_id=1, source_target_pairs={{0,4},{2,6},{4,0},{6,2},{8,12},{10,14},{12,8},{14,10},{16,20},{18,... | collective-permute-start | bytes 393224 | tf_op jit(solution)/shard_map/ppermute | solution.py:47
  8.3 0.9 %copy-start.1 = (bf16[64,2048]{1,0:T(8,128)(2,1)S(1)}, bf16[64,2048]{1,0:T(8,128)(2,1)}, u32[]{:S(2)}) copy-start(bf16[64,2048]{1,0:T(8,128)(2,1)} %a_ref) | copy-start | bytes 786436
  10.5 4.1 %collective-permute-start.4 = (bf16[8,128,128]{2,1,0:T(8,128)(2,1)S(1)}, bf16[8,128,128]{2,1,0:T(8,128)(2,1)S(1)}, u32[]{:S(2)}, u32[]{:S(2)}) collective-permute-start(bf16[8,128,128]{2,1,0:T(8,128)(2,1)S(1)} %pad_maximum_fusion), channel_id=1, source_target_pairs={{0,2},{2,0},{4,6},{6,4},{8,10},{10,8},{12,14},{14,12},{16,18},{18,... | collective-permute-start | bytes 786440 | tf_op jit(solution)/shard_map/ppermute | solution.py:47
  18.6 4.8 %collective-permute-start.6 = (bf16[64,1024]{1,0:T(8,128)(2,1)S(1)}, bf16[64,1024]{1,0:T(8,128)(2,1)S(1)}, u32[]{:S(2)}, u32[]{:S(2)}) collective-permute-start(bf16[64,1024]{1,0:T(8,128)(2,1)S(1)} %get-tuple-element.31.ya_ref), channel_id=1, source_target_pairs={{0,1},{1,0},{2,3},{3,2},{4,5},{5,4},{6,7},{7,6},{8,9},{9,8},{10,11... | collective-permute-start | bytes 393224 | tf_op jit(solution)/shard_map/ppermute | solution.py:414
  21.2 4.8 %collective-permute-start.5 = (bf16[64,1024]{1,0:T(8,128)(2,1)S(1)}, bf16[64,1024]{1,0:T(8,128)(2,1)S(1)}, u32[]{:S(2)}, u32[]{:S(2)}) collective-permute-start(bf16[64,1024]{1,0:T(8,128)(2,1)S(1)} %y_omega.1.ya_ref), channel_id=1, source_target_pairs={{0,1},{1,0},{2,3},{3,2},{4,5},{5,4},{6,7},{7,6},{8,9},{9,8},{10,11... | collective-permute-start | bytes 393224 | tf_op jit(solution)/shard_map/ppermute | solution.py:414
  26.5 2.4 %collective-permute-start.7 = (bf16[8,64,128]{2,1,0:T(8,128)(2,1)S(1)}, bf16[8,64,128]{2,1,0:T(8,128)(2,1)S(1)}, u32[]{:S(2)}, u32[]{:S(2)}) collective-permute-start(bf16[8,64,128]{2,1,0:T(8,128)(2,1)S(1)} %z_far.2), channel_id=1, source_target_pairs={{0,2},{2,0},{4,6},{6,4},{8,10},{10,8},{12,14},{14,12},{16,18},{18,... | collective-permute-start | bytes 393224 | tf_op jit(solution)/shard_map/ppermute | solution.py:54
  28.9 3.2 %collective-permute-start.8 = (bf16[4,64,128]{2,1,0:T(8,128)(2,1)S(1)}, bf16[4,64,128]{2,1,0:T(8,128)(2,1)S(1)}, u32[]{:S(2)}, u32[]{:S(2)}) collective-permute-start(bf16[4,64,128]{2,1,0:T(8,128)(2,1)S(1)} %slice.149), channel_id=1, source_target_pairs={{0,4},{2,6},{4,0},{6,2},{8,12},{10,14},{12,8},{14,10},{16,20},{18,... | collective-permute-start | bytes 196616 | tf_op jit(solution)/shard_map/ppermute | solution.py:61
  32.1 4.1 %collective-permute-start.10 = (bf16[4,64,128]{2,1,0:T(8,128)(2,1)S(1)}, bf16[4,64,128]{2,1,0:T(8,128)(2,1)S(1)}, u32[]{:S(2)}, u32[]{:S(2)}) collective-permute-start(bf16[4,64,128]{2,1,0:T(8,128)(2,1)S(1)} %fusion.1), channel_id=1, source_target_pairs={{0,16},{2,18},{4,20},{6,22},{8,24},{10,26},{12,28},{14,30},{16,0},... | collective-permute-start | bytes 196616 | tf_op jit(solution)/shard_map/ppermute | solution.py:70
  32.2 5.8 %collective-permute-start.11 = (bf16[4,64,128]{2,1,0:T(8,128)(2,1)S(1)}, bf16[4,64,128]{2,1,0:T(8,128)(2,1)S(1)}, u32[]{:S(2)}, u32[]{:S(2)}) collective-permute-start(bf16[4,64,128]{2,1,0:T(8,128)(2,1)S(1)} %fusion.1), channel_id=1, source_target_pairs={{0,24},{2,26},{4,28},{6,30},{8,16},{10,18},{12,20},{14,22},{16,8},... | collective-permute-start | bytes 196616 | tf_op jit(solution)/shard_map/ppermute | solution.py:70
  35.6 3.9 %collective-permute-start.9 = (bf16[4,64,128]{2,1,0:T(8,128)(2,1)S(1)}, bf16[4,64,128]{2,1,0:T(8,128)(2,1)S(1)}, u32[]{:S(2)}, u32[]{:S(2)}) collective-permute-start(bf16[4,64,128]{2,1,0:T(8,128)(2,1)S(1)} %fusion.1), channel_id=1, source_target_pairs={{0,8},{2,10},{4,12},{6,14},{8,0},{10,2},{12,4},{14,6},{16,24},{18,... | collective-permute-start | bytes 196616 | tf_op jit(solution)/shard_map/ppermute | solution.py:70
  39.5 3.2 %collective-permute-start.12 = (bf16[4,64,128]{2,1,0:T(8,128)(2,1)S(1)}, bf16[4,64,128]{2,1,0:T(8,128)(2,1)S(1)}, u32[]{:S(2)}, u32[]{:S(2)}) collective-permute-start(bf16[4,64,128]{2,1,0:T(8,128)(2,1)S(1)} %add_convert_fusion), channel_id=1, source_target_pairs={{0,4},{2,6},{4,0},{6,2},{8,12},{10,14},{12,8},{14,10},{16,20},{18,... | collective-permute-start | bytes 196616 | tf_op jit(solution)/shard_map/ppermute | solution.py:47
  42.7 4.7 %collective-permute-start.13 = (bf16[8,64,128]{2,1,0:T(8,128)(2,1)S(1)}, bf16[8,64,128]{2,1,0:T(8,128)(2,1)S(1)}, u32[]{:S(2)}, u32[]{:S(2)}) collective-permute-start(bf16[8,64,128]{2,1,0:T(8,128)(2,1)S(1)} %pad_maximum_fusion.4), channel_id=1, source_target_pairs={{0,2},{2,0},{4,6},{6,4},{8,10},{10,8},{12,14},{14,12},{16,18},{18,... | collective-permute-start | bytes 393224 | tf_op jit(solution)/shard_map/ppermute | solution.py:47
  47.6 2.8 %collective-permute-start.14 = (f32[64,64]{1,0:T(8,128)S(1)}, f32[64,64]{1,0:T(8,128)S(1)}, u32[]{:S(2)}, u32[]{:S(2)}) collective-permute-start(f32[64,64]{1,0:T(8,128)S(1)} %gram.1.ga_ref), channel_id=1, source_target_pairs={{0,1},{1,0},{2,3},{3,2},{4,5},{5,4},{6,7},{7,6},{8,9},{9,8},{10,11... | collective-permute-start | bytes 49160 | tf_op jit(solution)/shard_map/ppermute | solution.py:414
  52.0 3.9 %collective-permute-start.16 = (bf16[64,1024]{1,0:T(8,128)(2,1)S(1)}, bf16[64,1024]{1,0:T(8,128)(2,1)S(1)}, u32[]{:S(2)}, u32[]{:S(2)}) collective-permute-start(bf16[64,1024]{1,0:T(8,128)(2,1)S(1)} %get-tuple-element.33.ya_ref.ya_0), channel_id=1, source_target_pairs={{0,1},{1,0},{2,3},{3,2},{4,5},{5,4},{6,7},{7,6},{8,9},{9,8},{10,11... | collective-permute-start | bytes 393224 | tf_op jit(solution)/shard_map/ppermute | solution.py:414
  54.6 4.7 %collective-permute-start.15 = (bf16[64,1024]{1,0:T(8,128)(2,1)S(1)}, bf16[64,1024]{1,0:T(8,128)(2,1)S(1)}, u32[]{:S(2)}, u32[]{:S(2)}) collective-permute-start(bf16[64,1024]{1,0:T(8,128)(2,1)S(1)} %y_second.1.ya_ref.ya_1), channel_id=1, source_target_pairs={{0,1},{1,0},{2,3},{3,2},{4,5},{5,4},{6,7},{7,6},{8,9},{9,8},{10,11... | collective-permute-start | bytes 393224 | tf_op jit(solution)/shard_map/ppermute | solution.py:414
  59.8 3.2 %collective-permute-start.17 = (bf16[8,64,128]{2,1,0:T(8,128)(2,1)S(1)}, bf16[8,64,128]{2,1,0:T(8,128)(2,1)S(1)}, u32[]{:S(2)}, u32[]{:S(2)}) collective-permute-start(bf16[8,64,128]{2,1,0:T(8,128)(2,1)S(1)} %z_far.3), channel_id=1, source_target_pairs={{0,2},{2,0},{4,6},{6,4},{8,10},{10,8},{12,14},{14,12},{16,18},{18,... | collective-permute-start | bytes 393224 | tf_op jit(solution)/shard_map/ppermute | solution.py:54
  63.0 3.2 %collective-permute-start.18 = (bf16[4,64,128]{2,1,0:T(8,128)(2,1)S(1)}, bf16[4,64,128]{2,1,0:T(8,128)(2,1)S(1)}, u32[]{:S(2)}, u32[]{:S(2)}) collective-permute-start(bf16[4,64,128]{2,1,0:T(8,128)(2,1)S(1)} %slice.148), channel_id=1, source_target_pairs={{0,4},{2,6},{4,0},{6,2},{8,12},{10,14},{12,8},{14,10},{16,20},{18,... | collective-permute-start | bytes 196616 | tf_op jit(solution)/shard_map/ppermute | solution.py:61
  66.2 5.8 %collective-permute-start.20 = (bf16[4,64,128]{2,1,0:T(8,128)(2,1)S(1)}, bf16[4,64,128]{2,1,0:T(8,128)(2,1)S(1)}, u32[]{:S(2)}, u32[]{:S(2)}) collective-permute-start(bf16[4,64,128]{2,1,0:T(8,128)(2,1)S(1)} %fusion), channel_id=1, source_target_pairs={{0,16},{2,18},{4,20},{6,22},{8,24},{10,26},{12,28},{14,30},{16,0},... | collective-permute-start | bytes 196616 | tf_op jit(solution)/shard_map/ppermute | solution.py:70
  66.3 5.8 %collective-permute-start.21 = (bf16[4,64,128]{2,1,0:T(8,128)(2,1)S(1)}, bf16[4,64,128]{2,1,0:T(8,128)(2,1)S(1)}, u32[]{:S(2)}, u32[]{:S(2)}) collective-permute-start(bf16[4,64,128]{2,1,0:T(8,128)(2,1)S(1)} %fusion), channel_id=1, source_target_pairs={{0,24},{2,26},{4,28},{6,30},{8,16},{10,18},{12,20},{14,22},{16,8},... | collective-permute-start | bytes 196616 | tf_op jit(solution)/shard_map/ppermute | solution.py:70
  68.9 4.1 %collective-permute-start.19 = (bf16[4,64,128]{2,1,0:T(8,128)(2,1)S(1)}, bf16[4,64,128]{2,1,0:T(8,128)(2,1)S(1)}, u32[]{:S(2)}, u32[]{:S(2)}) collective-permute-start(bf16[4,64,128]{2,1,0:T(8,128)(2,1)S(1)} %fusion), channel_id=1, source_target_pairs={{0,8},{2,10},{4,12},{6,14},{8,0},{10,2},{12,4},{14,6},{16,24},{18,... | collective-permute-start | bytes 196616 | tf_op jit(solution)/shard_map/ppermute | solution.py:70
  73.0 3.2 %collective-permute-start.22 = (bf16[4,64,128]{2,1,0:T(8,128)(2,1)S(1)}, bf16[4,64,128]{2,1,0:T(8,128)(2,1)S(1)}, u32[]{:S(2)}, u32[]{:S(2)}) collective-permute-start(bf16[4,64,128]{2,1,0:T(8,128)(2,1)S(1)} %get-tuple-element.37), channel_id=1, source_target_pairs={{0,4},{2,6},{4,0},{6,2},{8,12},{10,14},{12,8},{14,10},{16,20},{18,... | collective-permute-start | bytes 196616 | tf_op jit(solution)/shard_map/ppermute | solution.py:47
  76.2 4.8 %collective-permute-start.23 = (bf16[8,64,128]{2,1,0:T(8,128)(2,1)S(1)}, bf16[8,64,128]{2,1,0:T(8,128)(2,1)S(1)}, u32[]{:S(2)}, u32[]{:S(2)}) collective-permute-start(bf16[8,64,128]{2,1,0:T(8,128)(2,1)S(1)} %pad_maximum_fusion.5), channel_id=1, source_target_pairs={{0,2},{2,0},{4,6},{6,4},{8,10},{10,8},{12,14},{14,12},{16,18},{18,... | collective-permute-start | bytes 393224 | tf_op jit(solution)/shard_map/ppermute | solution.py:47
  81.3 3.2 %collective-permute-start.24 = (f32[128,64]{1,0:T(8,128)S(1)}, f32[128,64]{1,0:T(8,128)S(1)}, u32[]{:S(2)}, u32[]{:S(2)}) collective-permute-start(f32[128,64]{1,0:T(8,128)S(1)} %grams.1.ga_ref), channel_id=1, source_target_pairs={{0,1},{1,0},{2,3},{3,2},{4,5},{5,4},{6,7},{7,6},{8,9},{9,8},{10,11... | collective-permute-start | bytes 98312 | tf_op jit(solution)/shard_map/ppermute | solution.py:414

commit v3 on v2

--- a/solution.py
+++ b/solution.py
@@ -49,23 +49,23 @@
     return held
 
 
-def reduce_blocks(near, far, axis, size):
+def reduce_blocks(near, far, axis, size, kind):
     groups = bit_groups(size)
-    other = lax.ppermute(far.astype(BF16), axis, xor_pairs(size, 1))
+    other = lax.ppermute(far.astype(kind), axis, xor_pairs(size, 1))
     parts = near.astype(F32) + other.astype(F32)
     for at, width in groups[1:-1]:
         ways = 1 << width
         pieces = parts.reshape((ways, parts.shape[0] // ways) + parts.shape[1:])
         total = pieces[0].astype(F32)
         got = [
-            lax.ppermute(pieces[k].astype(BF16), axis, xor_pairs(size, k << at))
+            lax.ppermute(pieces[k].astype(kind), axis, xor_pairs(size, k << at))
             for k in range(1, ways)
         ]
         for piece in got:
             total = total + piece.astype(F32)
         parts = total
     at, width = groups[-1]
-    mine = parts.astype(BF16)
+    mine = parts.astype(kind)
     total = mine.astype(F32)
     got = [lax.ppermute(mine, axis, xor_pairs(size, k << at)) for k in range(1, 1 << width)]
     for k, piece in enumerate(got, 1):
@@ -123,22 +123,17 @@
         return carry
 
     lax.fori_loop(0, (count + group - 1) // group, body, 0)
-    y_ref[...] = y_of(cat_tiles(bq_ref, slice(rank, 2 * rank)), r_ref, 0, y_ref.shape[1]).astype(
-        BF16
-    )
+    y_ref[...] = y_of(cat_tiles(bq_ref, slice(rank, 2 * rank)), r_ref, 0, y_ref.shape[1])
 
 
 def omega_kernel(at, bq_ref, r_ref, y_ref):
     rank = bq_ref.shape[1] // 2
-    y_ref[...] = y_of(cat_tiles(bq_ref, slice(rank, 2 * rank)), r_ref, at, y_ref.shape[1]).astype(
-        BF16
-    )
-
-
-def z_of(ya_ref, yb_ref, r_ref, at, z_ref, first, old_ref):
+    y_ref[...] = y_of(cat_tiles(bq_ref, slice(rank, 2 * rank)), r_ref, at, y_ref.shape[1])
+
+
+def z_of(y, r_ref, at, z_ref, first, old_ref):
     tile = z_ref.shape[2]
-    users = ya_ref.shape[1]
-    y = (ya_ref[...].astype(F32) + yb_ref[...].astype(F32)).astype(BF16)
+    users = y.shape[1]
     wide = math.gcd(z_ref.shape[0], 8)
     for i in range(0, z_ref.shape[0], wide):
         z = lax.dot_general(
@@ -154,24 +149,51 @@
             z_ref[i + j] = part.astype(z_ref.dtype)
 
 
-def z_first_kernel(ya_ref, yb_ref, r_ref, z_ref):
-    z_of(ya_ref, yb_ref, r_ref, 0, z_ref, 0, None)
-
-
-def z_second_kernel(first, ya_ref, yb_ref, r_ref, old_ref, z_ref):
-    z_of(ya_ref, yb_ref, r_ref, ya_ref.shape[1], z_ref, first, old_ref)
+def exact_dot(left, right, dims):
+    return lax.dot_general(
+        left, right, dims, precision=lax.Precision.HIGHEST, preferred_element_type=F32
+    )
+
+
+def y_gram_kernel(ya_ref, yb_ref, y_ref, g_ref):
+    y = ya_ref[...] + yb_ref[...]
+    y_ref[...] = y
+    g_ref[...] = exact_dot(y, y, NT)
+
+
+def y_gram_more_kernel(ya_ref, yb_ref, old_ref, y_ref, g_ref):
+    y = ya_ref[...] + yb_ref[...]
+    y_ref[...] = y
+    g_ref[...] = old_ref[...] + exact_dot(y, y, NT)
+
+
+def y_hat_kernel(g_ref, y_0, y_1, out_ref):
+    (inverse,) = chol_inverse([g_ref[...]])
+    half = y_0.shape[1]
+    out_ref[:, :half] = apply_wide(inverse, y_0[...])
+    out_ref[:, half:] = apply_wide(inverse, y_1[...])
+
+
+def y_near_hat_kernel(g_ref, y_0, ya_ref, yb_ref, out_ref):
+    gram = g_ref[...]
+    rows = lax.broadcasted_iota(jnp.int32, gram.shape, 0)
+    diagonal = rows == lax.broadcasted_iota(jnp.int32, gram.shape, 1)
+    (inverse,) = chol_inverse([gram + jnp.where(diagonal, gram * 1e-6 + 1e-30, 0.0)])
+    half = y_0.shape[1]
+    out_ref[:, :half] = apply_wide(inverse, y_0[...])
+    out_ref[:, half:] = apply_wide(inverse, ya_ref[...] + yb_ref[...])
+
+
+def z_kernel(first, y_ref, r_ref, z_ref):
+    z_of(y_ref[...].astype(BF16), r_ref, 0, z_ref, first, None)
 
 
 def gram_kernel(z_ref, g_ref):
     z = cat_tiles(z_ref, slice(None))
-    g_ref[...] = lax.dot_general(z, z, NT, preferred_element_type=F32)
-
-
-def grams_kernel(old_ref, z_ref, g_ref):
-    z = cat_tiles(z_ref, slice(None))
-    old = cat_tiles(old_ref, slice(None))
-    both = jnp.concatenate([z, old], axis=0)
-    g_ref[...] = lax.dot_general(both, z, NT, preferred_element_type=F32)
+    if z.dtype == F32:
+        g_ref[...] = exact_dot(z, z, NT)
+    else:
+        g_ref[...] = lax.dot_general(z, z, NT, preferred_element_type=F32)
 
 
 def chol_inverse(grams):
@@ -270,73 +292,53 @@
     )
 
 
-def y_kernel(z_ref, r_ref, y_ref):
-    y_ref[...] = y_of(cat_tiles(z_ref, slice(None)), r_ref, 0, y_ref.shape[1])
-
-
-def scale_kernel(ga_ref, gb_ref, y_ref, inv_ref, out_ref):
+def q_kernel(ga_ref, gb_ref, z_ref, q_ref):
     (inverse,) = chol_inverse([ga_ref[...] + gb_ref[...]])
-    inv_ref[...] = inverse
-    out_ref[...] = apply_wide(inverse, y_ref[...]).astype(BF16)
-
-
-def y_scaled_kernel(at, inv_ref, z_ref, r_ref, out_ref):
-    y = y_of(cat_tiles(z_ref, slice(None)), r_ref, at, out_ref.shape[1])
-    out_ref[...] = apply_wide(inv_ref[...], y).astype(BF16)
+    for t in range(z_ref.shape[0]):
+        q_ref[t] = apply_wide(inverse, z_ref[t]).astype(BF16)
+
+
+def y_kernel(at, q_ref, r_ref, y_ref):
+    y_ref[...] = y_of(cat_tiles(q_ref, slice(None)), r_ref, at, y_ref.shape[1])
+
+
+def left_kernel(radius, user_scale, y_ref, at_ref, left_ref, user_ref):
+    tile = 128
+    user_ref[...] = y_ref[...] * user_scale
+    for t in range(0, y_ref.shape[1], tile):
+        rows = slice(t, t + tile)
+        turned = (y_ref[:, rows].astype(BF16).astype(F32) * (-0.5 * radius)).T
+        high, low = two_parts(turned)
+        half = at_ref[rows, :].astype(F32) * 0.5
+        left_ref[rows, :] = jnp.concatenate([half.astype(BF16), high, low], axis=1)
 
 
 def last_kernel(
-    radius,
-    user_scale,
     item_scale,
     slot_any,
     ga_ref,
     gb_ref,
-    inv_ref,
     z_ref,
     share_ref,
-    ya_0,
-    ya_1,
-    yb_0,
-    yb_1,
     vals_ref,
-    at_ref,
+    left,
     bq_ref,
-    user_ref,
     item_ref,
     loss_ref,
-    left,
     right,
     slot_ref,
     slot_sem,
 ):
     slot_copy = pltpu.make_async_copy(slot_any, slot_ref, slot_sem)
     slot_copy.start()
-    ya_refs, yb_refs = (ya_0, ya_1), (yb_0, yb_1)
     tile = vals_ref.shape[1]
     rank = z_ref.shape[1]
-    gram = ga_ref[...] + gb_ref[...]
-    y_gram = lax.dot_general(
-        inv_ref[...], gram[rank:], NN, precision=lax.Precision.HIGHEST, preferred_element_type=F32
-    )
-    z_inv, y_inv = chol_inverse([gram[:rank], y_gram])
+    (z_inv,) = chol_inverse([ga_ref[...] + gb_ref[...]])
     for t in range(z_ref.shape[0]):
         q = apply_inverse(z_inv, z_ref[t]).astype(BF16)
         right[t, :rank] = bq_ref[t, :rank, :]
         right[t, rank : 2 * rank] = q
         right[t, 2 * rank : 3 * rank] = q
-    tiles = ya_refs[0].shape[1] // tile
-    for t in range(user_ref.shape[1] // tile):
-        cols = slice(t * tile, (t + 1) * tile)
-        here = slice(t % tiles * tile, (t % tiles + 1) * tile)
-        y = ya_refs[t // tiles][:, here].astype(F32) + yb_refs[t // tiles][:, here].astype(F32)
-        y_hat = apply_wide(y_inv, y)
-        user_ref[:, cols] = y_hat * user_scale
-        y_hat = y_hat.astype(BF16).astype(F32)
-        turned = (y_hat * (-0.5 * radius)).T
-        high, low = two_parts(turned)
-        half = at_ref[cols, :].astype(F32) * 0.5
-        left[cols, :] = jnp.concatenate([half.astype(BF16), high, low], axis=1)
     item_ref[...] = apply_wide(z_inv, share_ref[...]) * item_scale
     loss_ref[...] = jnp.zeros_like(loss_ref)
     slot_copy.wait()
@@ -417,12 +419,20 @@
                 return mine, other
             mine = (mine.astype(F32) + other.astype(F32)).astype(mine.dtype)
 
-    def reduced(near, far):
+    def reduced(near, far, kind, work=()):
         if not by_tile:
             near, far = jnp.split(to_blocks(jnp.concatenate([near, far.astype(F32)])), 2)
-        total = reduce_blocks(near, far, "user", n_user)
+        total = reduce_blocks(near, far, "user", n_user, kind)
+        work = list(work)
+
+        def before(number, held):
+            if number == -1 and work:
+                held, work[:] = lax.optimization_barrier((held, list(work)))
+            return held
+
         groups = bit_groups(n_user)[:-1]
-        return to_tiles(gather_blocks(total.astype(BF16), "user", n_user, groups)), total[0]
+        z = gather_blocks(total.astype(kind), "user", n_user, groups, before)
+        return to_tiles(z), total[0], work
 
     def call(kernel, outs, name, *args, smem=0, hbm=0, flops=0, vmem=16, **more):
         outs = [jax.ShapeDtypeStruct(shape, dtype) for shape, dtype in outs]
@@ -442,8 +452,7 @@
 
     half = users_dev // 2
     r_shape = ((users_dev, items_dev), BF16)
-    y_bf16, y_f32 = ((rank, half), BF16), ((rank, half), F32)
-    z_bf16, z_f32 = ((item_tiles, rank, tile), BF16), ((item_tiles, rank, tile), F32)
+    y_f32 = ((rank, half), F32)
     half_flops = 2 * rank * half * items_dev
 
     work = [fac_a, tile_row, tile_col, tile_count]
@@ -472,29 +481,41 @@
     bq = to_tiles(gather_blocks(both[None], "user", n_user, bit_groups(n_user), before))
     a_t, slots, cleared = work
 
-    def z_both(firsts, seconds):
-        z = call(z_first_kernel, [z_f32], "z_first", *firsts, resid, flops=half_flops)
+    def over_users(part):
+        for at, width in bit_groups(n_user):
+            terms = [part]
+            for k in range(1, 1 << width):
+                terms.append(lax.ppermute(part, "user", xor_pairs(n_user, k << at)))
+            while len(terms) > 1:
+                terms = [a + b for a, b in zip(terms[::2], terms[1::2])]
+            part = terms[0]
+        return part
+
+    square = ((rank, rank), F32)
+
+    def user_step(firsts, seconds, exact):
+        y_0, gram = call(y_gram_kernel, [y_f32, square], "y_gram", *firsts, flops=half_flops)
+        whole = [((rank, users_dev), F32)]
+        if not exact:
+            return call(y_near_hat_kernel, whole, "y_hat", over_users(gram), y_0, *seconds)
+        y_1, gram = call(y_gram_more_kernel, [y_f32, square], "y_gram_more", *seconds, gram)
+        return call(y_hat_kernel, whole, "y_hat", over_users(gram), y_0, y_1)
+
+    def item_step(y_hat, kind, work=()):
         near, far = item_tiles // 2, item_tiles - item_tiles // 2
-        parts = (*seconds, resid, z)
-        far = call(
-            functools.partial(z_second_kernel, near),
-            [((far, rank, tile), BF16)],
-            "z_far",
-            *parts,
-            flops=half_flops // 2,
+        kernel = functools.partial(z_kernel, near)
+        later = call(
+            kernel, [((far, rank, tile), kind)], "z_far", y_hat, resid, flops=half_flops
         )
-        near = call(
-            functools.partial(z_second_kernel, 0),
-            [((near, rank, tile), F32)],
-            "z_near",
-            *parts,
-            flops=half_flops // 2,
+        kernel = functools.partial(z_kernel, 0)
+        sooner = call(
+            kernel, [((near, rank, tile), F32)], "z_near", y_hat, resid, flops=half_flops
         )
-        return reduced(near, far)
+        return reduced(sooner, later, kind, work)
 
     resid, y_0 = call(
         first_kernel,
-        [r_shape, y_bf16],
+        [r_shape, y_f32],
         "resid_y",
         slots,
         ratings,
@@ -505,45 +526,41 @@
         input_output_aliases={4: 0},
     )
     firsts = across(y_0)
-    y_1 = call(functools.partial(omega_kernel, half), [y_bf16], "y_omega", bq, resid, flops=half_flops)
-    old, _ = z_both(firsts, across(y_1))
-
-    gram = across(call(gram_kernel, [((rank, rank), F32)], "gram", old))
-    y_0 = call(y_kernel, [y_f32], "y_first", old, resid, flops=half_flops)
-    inverse, y_0 = call(scale_kernel, [((rank, rank), F32), y_bf16], "scale_y", *gram, y_0)
-    firsts = across(y_0)
-    y_1 = call(
-        functools.partial(y_scaled_kernel, half),
-        [y_bf16],
-        "y_second",
-        inverse,
-        old,
-        resid,
-        flops=half_flops,
-    )
+    y_1 = call(functools.partial(omega_kernel, half), [y_f32], "y_omega", bq, resid, flops=half_flops)
     seconds = across(y_1)
-    z, z_share = z_both(firsts, seconds)
-
-    grams = across(call(grams_kernel, [((2 * rank, rank), F32)], "grams", old, z))
-    user_dir, item_dir, losses = call(
-        functools.partial(last_kernel, radius, math.sqrt(users), math.sqrt(items)),
-        [((rank, users_dev), F32), ((rank, share), F32), ((cap, tile), F32)],
+    old, _, _ = item_step(user_step(firsts, seconds, False), F32)
+
+    gram = across(call(gram_kernel, [square], "gram", old))
+    q = call(q_kernel, [((item_tiles, rank, tile), BF16)], "q", *gram, old)
+    kernel = functools.partial(y_kernel, 0)
+    firsts = across(call(kernel, [y_f32], "y_first", q, resid, flops=half_flops))
+    kernel = functools.partial(y_kernel, half)
+    seconds = across(call(kernel, [y_f32], "y_second", q, resid, flops=half_flops))
+    y_hat = user_step(firsts, seconds, True)
+    left, user_dir = call(
+        functools.partial(left_kernel, radius, math.sqrt(users)),
+        [((users_dev, 3 * rank), BF16), ((rank, users_dev), F32)],
+        "left",
+        y_hat,
+        a_t,
+        flops=1 << 30,
+    )
+    z, z_share, (left, user_dir) = item_step(y_hat, BF16, (left, user_dir))
+
+    grams = across(call(gram_kernel, [square], "gram", z))
+    item_dir, losses = call(
+        functools.partial(last_kernel, math.sqrt(items)),
+        [((rank, share), F32), ((cap, tile), F32)],
         "loss",
         slots,
         *grams,
-        inverse,
         z,
         z_share,
-        firsts[0],
-        seconds[0],
-        firsts[1],
-        seconds[1],
         ratings,
-        a_t,
+        left,
         bq,
         hbm=1,
         scratch_shapes=[
-            pltpu.VMEM((users_dev, 3 * rank), BF16),
             pltpu.VMEM((item_tiles, 3 * rank, tile), BF16),
             pltpu.SMEM((3, cap), jnp.int32),
             pltpu.SemaphoreType.DMA,

time: 93.2 us -> 137 us (1.47)
  waiting for transfers between devices: 34.1 us -> 61.3 us
  starting transfers between devices: 30.5 us -> 42.6 us
  Pallas kernels: 21.8 us -> 26.4 us
    ppermute x4 -> x14, starting transfers between devices: 4.15 us -> 17.6 us  [the longest x10 11.2 us: over_users(): terms.append(lax.ppermute(part, 'user', xor_pairs(n_user, k << at)))]
    ppermute x4 -> x14, waiting for transfers between devices: 6.82 us -> 18.4 us  [the longest x10 10.2 us: over_users(): terms.append(lax.ppermute(part, 'user', xor_pairs(n_user, k << at)))]
    ppermute x6, waiting for transfers between devices: 9.5 us -> 20.2 us  [across(): other = lax.ppermute(mine, 'item', xor_pairs(n_item, bit))]
    ppermute x6, waiting for transfers between devices: 7.86 us -> 12.5 us  [reduce_blocks(): lax.ppermute(mine, axis, xor_pairs(size, k << at))]
    pallas_call x15 -> x19, Pallas kernels: 21.8 us -> 26.4 us  [call(): pl.pallas_call(kernel, out_shape=outs, in_specs=[SMEM] * smem + [pl.Block...]
  transfers between devices with their start and end apart: 25 -> 35, of which waited for: 23 -> 30; matrix products, arithmetic and copies ran while one was open for 2% -> 1% of each run, Pallas kernels for 8% -> 5%
where the time goes in v3:
time: 137 us; the launch traced here: 136 us
  waiting for transfers between devices  61.3 us (45%)
  starting transfers between devices  42.6 us (31%)
  Pallas kernels  26.4 us (19%)
  other arithmetic  2.46 us (2%)
  between operations  1.86 us (1%)
    pallas_call x19, Pallas kernels, call(): pl.pallas_call(kernel, out_shape=outs, in_specs=[SMEM] * smem + [pl.Block...  26.4 us
    ppermute x6, waiting for transfers between devices, across(): other = lax.ppermute(mine, 'item', xor_pairs(n_item, bit))  20.2 us
    ppermute x9, starting transfers between devices, gather_blocks(): got.append(lax.ppermute(held, axis, xor_pairs(size, k << at)))  14.4 us
    ppermute x6, waiting for transfers between devices, reduce_blocks(): lax.ppermute(mine, axis, xor_pairs(size, k << at))  12.5 us
    ppermute x10, starting transfers between devices, over_users(): terms.append(lax.ppermute(part, 'user', xor_pairs(n_user, k << at)))  11.2 us
    ppermute x10, waiting for transfers between devices, over_users(): terms.append(lax.ppermute(part, 'user', xor_pairs(n_user, k << at)))  10.2 us
    ppermute x9, waiting for transfers between devices, gather_blocks(): got.append(lax.ppermute(held, axis, xor_pairs(size, k << at)))  10.1 us
    ppermute x2, waiting for transfers between devices, reduce_blocks(): lax.ppermute(pieces[k].astype(kind), axis, xor_pairs(size, k << at))  7.76 us
  transfers between devices with their start and end apart: 35, of which 30 were waited for; matrix products, arithmetic and copies ran while one was open for 1% of the time, Pallas kernels for 5%

profile of v3, /device:TPU:29, one launch (start us, length us, event | category | flops | bytes accessed | tf_op | source)
XLA Modules:
  0.0 135.8 jit_solution(1033671191342990808)
XLA Ops:
  2.7 2.2 %collective-permute-start = (bf16[1,128,128]{2,1,0:T(8,128)(2,1)S(1)}, bf16[1,128,128]{2,1,0:T(8,128)(2,1)S(1)}, u32[]{:S(2)}, u32[]{:S(2)}) collective-permute-start(bf16[1,128,128]{2,1,0:T(8,128)(2,1)S(1)} %bitcast.16), channel_id=1, source_target_pairs={{0,8},{2,10},{4,12},{6,14},{8,0},{10,2},{12,4},{14,6},{16,24},{18,... | collective-permute-start | bytes 98312 | tf_op jit(solution)/shard_map/ppermute | solution.py:47
  10.5 2.9 %collective-permute-start.4 = (bf16[8,128,128]{2,1,0:T(8,128)(2,1)S(1)}, bf16[8,128,128]{2,1,0:T(8,128)(2,1)S(1)}, u32[]{:S(2)}, u32[]{:S(2)}) collective-permute-start(bf16[8,128,128]{2,1,0:T(8,128)(2,1)S(1)} %pad_maximum_fusion.1), channel_id=1, source_target_pairs={{0,2},{2,0},{4,6},{6,4},{8,10},{10,8},{12,14},{14,12},{16,18},{18,... | collective-permute-start | bytes 786440 | tf_op jit(solution)/shard_map/ppermute | solution.py:47
  14.7 3.9 %resid_y.1 = (bf16[2048,2048]{1,0:T(8,128)(2,1)S(1)}, f32[64,1024]{1,0:T(8,128)S(1)}) custom-call(s32[3,128]{1,0:T(4,128)S(1)} %add_add_fusion.2.slot_ref.slot_any, bf16[128,128,128]{2,1,0:T(8,128)(2,1)S(1)} %bitcast.12, bf16[2048,64]{1,0:T(8,128)(2,1)S(1)} %get-tuple-element.35.at_ref, ...), custom_call_target="tpu_custom_call", output_to_operand_aliasing={{0}: (4, {})} | custom-call | bytes 65536 | tf_op jit(solution)/shard_map/resid_y/pallas_call | solution.py:439
  19.9 6.3 %collective-permute-done.5.yb_ref = f32[64,1024]{1,0:T(8,128)S(1)} collective-permute-done((f32[64,1024]{1,0:T(8,128)S(1)}, f32[64,1024]{1,0:T(8,128)S(1)}, u32[]{:S(2)}, u32[]{:S(2)}) %collective-permute-start.5) | collective-permute-done | bytes 262176 | tf_op jit(solution)/shard_map/ppermute | solution.py:416
  30.8 2.8 %collective-permute-done.7 = f32[64,64]{1,0:T(8,128)S(1)} collective-permute-done((f32[64,64]{1,0:T(8,128)S(1)}, f32[64,64]{1,0:T(8,128)S(1)}, u32[]{:S(2)}, u32[]{:S(2)}) %collective-permute-start.7) | collective-permute-done | bytes 16416 | tf_op jit(solution)/shard_map/ppermute | solution.py:488
  34.3 1.8 %collective-permute-start.9 = (f32[64,64]{1,0:T(8,128)S(1)}, f32[64,64]{1,0:T(8,128)S(1)}, u32[]{:S(2)}, u32[]{:S(2)}) collective-permute-start(f32[64,64]{1,0:T(8,128)S(1)} %add.83), channel_id=1, source_target_pairs={{0,16},{2,18},{4,20},{6,22},{8,24},{10,26},{12,28},{14,30},{16,0},... | collective-permute-start | bytes 49160 | tf_op jit(solution)/shard_map/ppermute | solution.py:488
  38.8 1.7 %y_hat.2.y_ref = f32[64,2048]{1,0:T(8,128)S(1)} custom-call(f32[64,64]{1,0:T(8,128)S(1)} %add_add_fusion.1.g_ref, f32[64,1024]{1,0:T(8,128)S(1)} %get-tuple-element.40.y_0, f32[64,1024]{1,0:T(8,128)S(1)} %y_omega.1.ya_ref, f32[64,1024]{1,0:T(8,128)S(1)} %collective-permute-done.11.yb_ref), custom_call_target="tpu_custom_call" | custom-call | bytes 65536 | tf_op jit(solution)/shard_map/y_hat/pallas_call | solution.py:439
  41.4 2.9 %collective-permute-start.12 = (f32[8,64,128]{2,1,0:T(8,128)S(1)}, f32[8,64,128]{2,1,0:T(8,128)S(1)}, u32[]{:S(2)}, u32[]{:S(2)}) collective-permute-start(f32[8,64,128]{2,1,0:T(8,128)S(1)} %z_far.2), channel_id=1, source_target_pairs={{0,2},{2,0},{4,6},{6,4},{8,10},{10,8},{12,14},{14,12},{16,18},{18,... | collective-permute-start | bytes 786440 | tf_op jit(solution)/shard_map/ppermute | solution.py:54
  45.6 4.7 %collective-permute-done.13 = f32[4,64,128]{2,1,0:T(8,128)S(1)} collective-permute-done((f32[4,64,128]{2,1,0:T(8,128)S(1)}, f32[4,64,128]{2,1,0:T(8,128)S(1)}, u32[]{:S(2)}, u32[]{:S(2)}) %collective-permute-start.13) | collective-permute-done | bytes 131104 | tf_op jit(solution)/shard_map/ppermute | solution.py:61
  51.1 2.5 %collective-permute-start.16 = (f32[4,64,128]{2,1,0:T(8,128)S(1)}, f32[4,64,128]{2,1,0:T(8,128)S(1)}, u32[]{:S(2)}, u32[]{:S(2)}) collective-permute-start(f32[4,64,128]{2,1,0:T(8,128)S(1)} %slice_add_fusion.1), channel_id=1, source_target_pairs={{0,24},{2,26},{4,28},{6,30},{8,16},{10,18},{12,20},{14,22},{16,8},... | collective-permute-start | bytes 393224 | tf_op jit(solution)/shard_map/ppermute | solution.py:70
  53.6 7.1 %collective-permute-done.15 = f32[4,64,128]{2,1,0:T(8,128)S(1)} collective-permute-done((f32[4,64,128]{2,1,0:T(8,128)S(1)}, f32[4,64,128]{2,1,0:T(8,128)S(1)}, u32[]{:S(2)}, u32[]{:S(2)}) %collective-permute-start.15) | collective-permute-done | bytes 131104 | tf_op jit(solution)/shard_map/ppermute | solution.py:70
  62.2 3.8 %collective-permute-done.17 = f32[4,64,128]{2,1,0:T(8,128)S(1)} collective-permute-done((f32[4,64,128]{2,1,0:T(8,128)S(1)}, f32[4,64,128]{2,1,0:T(8,128)S(1)}, u32[]{:S(2)}, u32[]{:S(2)}) %collective-permute-start.17) | collective-permute-done | bytes 131104 | tf_op jit(solution)/shard_map/ppermute | solution.py:47
  66.0 3.4 %collective-permute-start.18 = (f32[8,64,128]{2,1,0:T(8,128)S(1)}, f32[8,64,128]{2,1,0:T(8,128)S(1)}, u32[]{:S(2)}, u32[]{:S(2)}) collective-permute-start(f32[8,64,128]{2,1,0:T(8,128)S(1)} %pad_maximum_fusion.2), channel_id=1, source_target_pairs={{0,2},{2,0},{4,6},{6,4},{8,10},{10,8},{12,14},{14,12},{16,18},{18,... | collective-permute-start | bytes 786440 | tf_op jit(solution)/shard_map/ppermute | solution.py:47
  71.3 2.7 %collective-permute-done.19.gb_ref = f32[64,64]{1,0:T(8,128)S(1)} collective-permute-done((f32[64,64]{1,0:T(8,128)S(1)}, f32[64,64]{1,0:T(8,128)S(1)}, u32[]{:S(2)}, u32[]{:S(2)}) %collective-permute-start.19) | collective-permute-done | bytes 16416 | tf_op jit(solution)/shard_map/ppermute | solution.py:416
  74.0 1.8 %q.1.q_ref = bf16[16,64,128]{2,1,0:T(8,128)(2,1)S(1)} custom-call(f32[64,64]{1,0:T(8,128)S(1)} %gram.2.ga_ref, f32[64,64]{1,0:T(8,128)S(1)} %collective-permute-done.19.gb_ref, f32[16,64,128]{2,1,0:T(8,128)S(1)} %pad_maximum_fusion.z_ref), custom_call_target="tpu_custom_call" | custom-call | bytes 65536 | tf_op jit(solution)/shard_map/q/pallas_call | solution.py:439
  75.8 1.4 %y_first.1.ya_ref = f32[64,1024]{1,0:T(8,128)S(1)} custom-call(bf16[16,64,128]{2,1,0:T(8,128)(2,1)S(1)} %q.1.q_ref, bf16[2048,2048]{1,0:T(8,128)(2,1)S(1)} %get-tuple-element.41.r_ref), custom_call_target="tpu_custom_call" | custom-call | flops 268435456 | bytes 65536 | tf_op jit(solution)/shard_map/y_first/pallas_call | solution.py:439
  78.7 1.4 %collective-permute-start.20 = (f32[64,1024]{1,0:T(8,128)S(1)}, f32[64,1024]{1,0:T(8,128)S(1)}, u32[]{:S(2)}, u32[]{:S(2)}) collective-permute-start(f32[64,1024]{1,0:T(8,128)S(1)} %y_second.1.ya_ref), channel_id=1, source_target_pairs={{0,1},{1,0},{2,3},{3,2},{4,5},{5,4},{6,7},{7,6},{8,9},{9,8},{10,11... | collective-permute-start | bytes 786440 | tf_op jit(solution)/shard_map/ppermute | solution.py:416
  80.1 3.4 %collective-permute-done.21.yb_ref = f32[64,1024]{1,0:T(8,128)S(1)} collective-permute-done((f32[64,1024]{1,0:T(8,128)S(1)}, f32[64,1024]{1,0:T(8,128)S(1)}, u32[]{:S(2)}, u32[]{:S(2)}) %collective-permute-start.21) | collective-permute-done | bytes 262176 | tf_op jit(solution)/shard_map/ppermute | solution.py:416
  83.9 5.2 %collective-permute-done.20.yb_ref = f32[64,1024]{1,0:T(8,128)S(1)} collective-permute-done((f32[64,1024]{1,0:T(8,128)S(1)}, f32[64,1024]{1,0:T(8,128)S(1)}, u32[]{:S(2)}, u32[]{:S(2)}) %collective-permute-start.20) | collective-permute-done | bytes 262176 | tf_op jit(solution)/shard_map/ppermute | solution.py:416
  89.5 2.5 %collective-permute-start.22 = (f32[64,64]{1,0:T(8,128)S(1)}, f32[64,64]{1,0:T(8,128)S(1)}, u32[]{:S(2)}, u32[]{:S(2)}) collective-permute-start(f32[64,64]{1,0:T(8,128)S(1)} %get-tuple-element.43), channel_id=1, source_target_pairs={{0,2},{2,0},{4,6},{6,4},{8,10},{10,8},{12,14},{14,12},{16,18},{18,... | collective-permute-start | bytes 49160 | tf_op jit(solution)/shard_map/ppermute | solution.py:488
  92.9 2.7 %collective-permute-done.23 = f32[64,64]{1,0:T(8,128)S(1)} collective-permute-done((f32[64,64]{1,0:T(8,128)S(1)}, f32[64,64]{1,0:T(8,128)S(1)}, u32[]{:S(2)}, u32[]{:S(2)}) %collective-permute-start.23) | collective-permute-done | bytes 16416 | tf_op jit(solution)/shard_map/ppermute | solution.py:488
  95.6 1.7 %collective-permute-start.26 = (f32[64,64]{1,0:T(8,128)S(1)}, f32[64,64]{1,0:T(8,128)S(1)}, u32[]{:S(2)}, u32[]{:S(2)}) collective-permute-start(f32[64,64]{1,0:T(8,128)S(1)} %add.93), channel_id=1, source_target_pairs={{0,24},{2,26},{4,28},{6,30},{8,16},{10,18},{12,20},{14,22},{16,8},... | collective-permute-start | bytes 49160 | tf_op jit(solution)/shard_map/ppermute | solution.py:488
  101.4 1.7 %y_hat.3.y_ref = f32[64,2048]{1,0:T(8,128)S(1)} custom-call(f32[64,64]{1,0:T(8,128)S(1)} %add_add_fusion.g_ref, f32[64,1024]{1,0:T(8,128)S(1)} %get-tuple-element.44.y_0, f32[64,1024]{1,0:T(8,128)S(1)} %get-tuple-element.45.y_1), custom_call_target="tpu_custom_call" | custom-call | bytes 65536 | tf_op jit(solution)/shard_map/y_hat/pallas_call | solution.py:439
  103.9 3.3 %collective-permute-start.27 = (bf16[8,64,128]{2,1,0:T(8,128)(2,1)S(1)}, bf16[8,64,128]{2,1,0:T(8,128)(2,1)S(1)}, u32[]{:S(2)}, u32[]{:S(2)}) collective-permute-start(bf16[8,64,128]{2,1,0:T(8,128)(2,1)S(1)} %z_far.3), channel_id=1, source_target_pairs={{0,2},{2,0},{4,6},{6,4},{8,10},{10,8},{12,14},{14,12},{16,18},{18,... | collective-permute-start | bytes 393224 | tf_op jit(solution)/shard_map/ppermute | solution.py:54
  108.3 3.1 %collective-permute-done.28 = bf16[4,64,128]{2,1,0:T(8,128)(2,1)S(1)} collective-permute-done((bf16[4,64,128]{2,1,0:T(8,128)(2,1)S(1)}, bf16[4,64,128]{2,1,0:T(8,128)(2,1)S(1)}, u32[]{:S(2)}, u32[]{:S(2)}) %collective-permute-start.28) | collective-permute-done | bytes 65568 | tf_op jit(solution)/shard_map/ppermute | solution.py:61
  112.5 1.6 %collective-permute-start.31 = (bf16[4,64,128]{2,1,0:T(8,128)(2,1)S(1)}, bf16[4,64,128]{2,1,0:T(8,128)(2,1)S(1)}, u32[]{:S(2)}, u32[]{:S(2)}) collective-permute-start(bf16[4,64,128]{2,1,0:T(8,128)(2,1)S(1)} %fusion), channel_id=1, source_target_pairs={{0,24},{2,26},{4,28},{6,30},{8,16},{10,18},{12,20},{14,22},{16,8},... | collective-permute-start | bytes 196616 | tf_op jit(solution)/shard_map/ppermute | solution.py:70
  114.2 2.0 %collective-permute-done.30 = bf16[4,64,128]{2,1,0:T(8,128)(2,1)S(1)} collective-permute-done((bf16[4,64,128]{2,1,0:T(8,128)(2,1)S(1)}, bf16[4,64,128]{2,1,0:T(8,128)(2,1)S(1)}, u32[]{:S(2)}, u32[]{:S(2)}) %collective-permute-start.30) | collective-permute-done | bytes 65568 | tf_op jit(solution)/shard_map/ppermute | solution.py:70
  116.2 1.7 %collective-permute-done.31 = bf16[4,64,128]{2,1,0:T(8,128)(2,1)S(1)} collective-permute-done((bf16[4,64,128]{2,1,0:T(8,128)(2,1)S(1)}, bf16[4,64,128]{2,1,0:T(8,128)(2,1)S(1)}, u32[]{:S(2)}, u32[]{:S(2)}) %collective-permute-start.31) | collective-permute-done | bytes 65568 | tf_op jit(solution)/shard_map/ppermute | solution.py:70
  119.7 1.8 %collective-permute-done.32 = bf16[4,64,128]{2,1,0:T(8,128)(2,1)S(1)} collective-permute-done((bf16[4,64,128]{2,1,0:T(8,128)(2,1)S(1)}, bf16[4,64,128]{2,1,0:T(8,128)(2,1)S(1)}, u32[]{:S(2)}, u32[]{:S(2)}) %collective-permute-start.32) | collective-permute-done | bytes 65568 | tf_op jit(solution)/shard_map/ppermute | solution.py:47
  121.5 4.1 %collective-permute-start.33 = (bf16[8,64,128]{2,1,0:T(8,128)(2,1)S(1)}, bf16[8,64,128]{2,1,0:T(8,128)(2,1)S(1)}, u32[]{:S(2)}, u32[]{:S(2)}) collective-permute-start(bf16[8,64,128]{2,1,0:T(8,128)(2,1)S(1)} %pad_maximum_fusion.4), channel_id=1, source_target_pairs={{0,2},{2,0},{4,6},{6,4},{8,10},{10,8},{12,14},{14,12},{16,18},{18,... | collective-permute-start | bytes 393224 | tf_op jit(solution)/shard_map/ppermute | solution.py:47
  127.0 2.7 %collective-permute-done.34.gb_ref = f32[64,64]{1,0:T(8,128)S(1)} collective-permute-done((f32[64,64]{1,0:T(8,128)S(1)}, f32[64,64]{1,0:T(8,128)S(1)}, u32[]{:S(2)}, u32[]{:S(2)}) %collective-permute-start.34) | collective-permute-done | bytes 16416 | tf_op jit(solution)/shard_map/ppermute | solution.py:416
  129.7 5.9 %loss.1 = (f32[64,128]{1,0:T(8,128)}, f32[128,128]{1,0:T(8,128)}) custom-call(s32[3,128]{1,0:T(4,128)S(1)} %add_add_fusion.2.slot_ref.slot_any, f32[64,64]{1,0:T(8,128)S(1)} %gram.3.ga_ref, f32[64,64]{1,0:T(8,128)S(1)} %collective-permute-done.34.gb_ref, bf16[16,64,128]{2,1,0:T(8,128)(2,1)S(1)} %constant_dynamic-update-slice_fusion.2.z_ref, ...), custom_call_target="tpu_custom_call" | custom-call | bytes 65536 | tf_op jit(solution)/shard_map/loss/pallas_call | solution.py:439
  (95 shorter events, 37.4 us)
Async XLA Ops:
  1.4 4.6 %collective-permute-start.2 = (bf16[1,128,128]{2,1,0:T(8,128)(2,1)S(1)}, bf16[1,128,128]{2,1,0:T(8,128)(2,1)S(1)}, u32[]{:S(2)}, u32[]{:S(2)}) collective-permute-start(bf16[1,128,128]{2,1,0:T(8,128)(2,1)S(1)} %bitcast.14), channel_id=1, source_target_pairs={{0,24},{2,26},{4,28},{6,30},{8,16},{10,18},{12,20},{14,22},{16,8},... | collective-permute-start | bytes 98312 | tf_op jit(solution)/shard_map/ppermute | solution.py:47
  1.4 4.6 %collective-permute-start.1 = (bf16[1,128,128]{2,1,0:T(8,128)(2,1)S(1)}, bf16[1,128,128]{2,1,0:T(8,128)(2,1)S(1)}, u32[]{:S(2)}, u32[]{:S(2)}) collective-permute-start(bf16[1,128,128]{2,1,0:T(8,128)(2,1)S(1)} %bitcast.15), channel_id=1, source_target_pairs={{0,16},{2,18},{4,20},{6,22},{8,24},{10,26},{12,28},{14,30},{16,0},... | collective-permute-start | bytes 98312 | tf_op jit(solution)/shard_map/ppermute | solution.py:47
  2.7 3.9 %collective-permute-start = (bf16[1,128,128]{2,1,0:T(8,128)(2,1)S(1)}, bf16[1,128,128]{2,1,0:T(8,128)(2,1)S(1)}, u32[]{:S(2)}, u32[]{:S(2)}) collective-permute-start(bf16[1,128,128]{2,1,0:T(8,128)(2,1)S(1)} %bitcast.16), channel_id=1, source_target_pairs={{0,8},{2,10},{4,12},{6,14},{8,0},{10,2},{12,4},{14,6},{16,24},{18,... | collective-permute-start | bytes 98312 | tf_op jit(solution)/shard_map/ppermute | solution.py:47
  6.6 3.9 %collective-permute-start.3 = (bf16[4,128,128]{2,1,0:T(8,128)(2,1)S(1)}, bf16[4,128,128]{2,1,0:T(8,128)(2,1)S(1)}, u32[]{:S(2)}, u32[]{:S(2)}) collective-permute-start(bf16[4,128,128]{2,1,0:T(8,128)(2,1)S(1)} %pad_maximum_fusion.3), channel_id=1, source_target_pairs={{0,4},{2,6},{4,0},{6,2},{8,12},{10,14},{12,8},{14,10},{16,20},{18,... | collective-permute-start | bytes 393224 | tf_op jit(solution)/shard_map/ppermute | solution.py:47
  10.5 4.1 %collective-permute-start.4 = (bf16[8,128,128]{2,1,0:T(8,128)(2,1)S(1)}, bf16[8,128,128]{2,1,0:T(8,128)(2,1)S(1)}, u32[]{:S(2)}, u32[]{:S(2)}) collective-permute-start(bf16[8,128,128]{2,1,0:T(8,128)(2,1)S(1)} %pad_maximum_fusion.1), channel_id=1, source_target_pairs={{0,2},{2,0},{4,6},{6,4},{8,10},{10,8},{12,14},{14,12},{16,18},{18,... | collective-permute-start | bytes 786440 | tf_op jit(solution)/shard_map/ppermute | solution.py:47
  18.6 7.6 %collective-permute-start.5 = (f32[64,1024]{1,0:T(8,128)S(1)}, f32[64,1024]{1,0:T(8,128)S(1)}, u32[]{:S(2)}, u32[]{:S(2)}) collective-permute-start(f32[64,1024]{1,0:T(8,128)S(1)} %get-tuple-element.38.ya_ref), channel_id=1, source_target_pairs={{0,1},{1,0},{2,3},{3,2},{4,5},{5,4},{6,7},{7,6},{8,9},{9,8},{10,11... | collective-permute-start | bytes 786440 | tf_op jit(solution)/shard_map/ppermute | solution.py:416
  26.5 4.0 %collective-permute-start.6 = (f32[64,64]{1,0:T(8,128)S(1)}, f32[64,64]{1,0:T(8,128)S(1)}, u32[]{:S(2)}, u32[]{:S(2)}) collective-permute-start(f32[64,64]{1,0:T(8,128)S(1)} %get-tuple-element.39), channel_id=1, source_target_pairs={{0,2},{2,0},{4,6},{6,4},{8,10},{10,8},{12,14},{14,12},{16,18},{18,... | collective-permute-start | bytes 49160 | tf_op jit(solution)/shard_map/ppermute | solution.py:488
  29.2 9.6 %collective-permute-start.11 = (f32[64,1024]{1,0:T(8,128)S(1)}, f32[64,1024]{1,0:T(8,128)S(1)}, u32[]{:S(2)}, u32[]{:S(2)}) collective-permute-start(f32[64,1024]{1,0:T(8,128)S(1)} %y_omega.1.ya_ref), channel_id=1, source_target_pairs={{0,1},{1,0},{2,3},{3,2},{4,5},{5,4},{6,7},{7,6},{8,9},{9,8},{10,11... | collective-permute-start | bytes 786440 | tf_op jit(solution)/shard_map/ppermute | solution.py:416
  30.5 3.1 %collective-permute-start.7 = (f32[64,64]{1,0:T(8,128)S(1)}, f32[64,64]{1,0:T(8,128)S(1)}, u32[]{:S(2)}, u32[]{:S(2)}) collective-permute-start(f32[64,64]{1,0:T(8,128)S(1)} %add.82), channel_id=1, source_target_pairs={{0,4},{2,6},{4,0},{6,2},{8,12},{10,14},{12,8},{14,10},{16,20},{18,... | collective-permute-start | bytes 49160 | tf_op jit(solution)/shard_map/ppermute | solution.py:488
  33.6 4.6 %collective-permute-start.10 = (f32[64,64]{1,0:T(8,128)S(1)}, f32[64,64]{1,0:T(8,128)S(1)}, u32[]{:S(2)}, u32[]{:S(2)}) collective-permute-start(f32[64,64]{1,0:T(8,128)S(1)} %add.83), channel_id=1, source_target_pairs={{0,24},{2,26},{4,28},{6,30},{8,16},{10,18},{12,20},{14,22},{16,8},... | collective-permute-start | bytes 49160 | tf_op jit(solution)/shard_map/ppermute | solution.py:488
  34.3 4.0 %collective-permute-start.9 = (f32[64,64]{1,0:T(8,128)S(1)}, f32[64,64]{1,0:T(8,128)S(1)}, u32[]{:S(2)}, u32[]{:S(2)}) collective-permute-start(f32[64,64]{1,0:T(8,128)S(1)} %add.83), channel_id=1, source_target_pairs={{0,16},{2,18},{4,20},{6,22},{8,24},{10,26},{12,28},{14,30},{16,0},... | collective-permute-start | bytes 49160 | tf_op jit(solution)/shard_map/ppermute | solution.py:488
  41.4 4.1 %collective-permute-start.12 = (f32[8,64,128]{2,1,0:T(8,128)S(1)}, f32[8,64,128]{2,1,0:T(8,128)S(1)}, u32[]{:S(2)}, u32[]{:S(2)}) collective-permute-start(f32[8,64,128]{2,1,0:T(8,128)S(1)} %z_far.2), channel_id=1, source_target_pairs={{0,2},{2,0},{4,6},{6,4},{8,10},{10,8},{12,14},{14,12},{16,18},{18,... | collective-permute-start | bytes 786440 | tf_op jit(solution)/shard_map/ppermute | solution.py:54
  45.5 4.8 %collective-permute-start.13 = (f32[4,64,128]{2,1,0:T(8,128)S(1)}, f32[4,64,128]{2,1,0:T(8,128)S(1)}, u32[]{:S(2)}, u32[]{:S(2)}) collective-permute-start(f32[4,64,128]{2,1,0:T(8,128)S(1)} %slice.114), channel_id=1, source_target_pairs={{0,4},{2,6},{4,0},{6,2},{8,12},{10,14},{12,8},{14,10},{16,20},{18,... | collective-permute-start | bytes 393224 | tf_op jit(solution)/shard_map/ppermute | solution.py:61
  50.3 10.4 %collective-permute-start.15 = (f32[4,64,128]{2,1,0:T(8,128)S(1)}, f32[4,64,128]{2,1,0:T(8,128)S(1)}, u32[]{:S(2)}, u32[]{:S(2)}) collective-permute-start(f32[4,64,128]{2,1,0:T(8,128)S(1)} %slice_add_fusion.1), channel_id=1, source_target_pairs={{0,16},{2,18},{4,20},{6,22},{8,24},{10,26},{12,28},{14,30},{16,0},... | collective-permute-start | bytes 393224 | tf_op jit(solution)/shard_map/ppermute | solution.py:70
  51.1 9.6 %collective-permute-start.16 = (f32[4,64,128]{2,1,0:T(8,128)S(1)}, f32[4,64,128]{2,1,0:T(8,128)S(1)}, u32[]{:S(2)}, u32[]{:S(2)}) collective-permute-start(f32[4,64,128]{2,1,0:T(8,128)S(1)} %slice_add_fusion.1), channel_id=1, source_target_pairs={{0,24},{2,26},{4,28},{6,30},{8,16},{10,18},{12,20},{14,22},{16,8},... | collective-permute-start | bytes 393224 | tf_op jit(solution)/shard_map/ppermute | solution.py:70
  53.6 8.5 %collective-permute-start.14 = (f32[4,64,128]{2,1,0:T(8,128)S(1)}, f32[4,64,128]{2,1,0:T(8,128)S(1)}, u32[]{:S(2)}, u32[]{:S(2)}) collective-permute-start(f32[4,64,128]{2,1,0:T(8,128)S(1)} %slice_add_fusion.1), channel_id=1, source_target_pairs={{0,8},{2,10},{4,12},{6,14},{8,0},{10,2},{12,4},{14,6},{16,24},{18,... | collective-permute-start | bytes 393224 | tf_op jit(solution)/shard_map/ppermute | solution.py:70
  62.1 3.9 %collective-permute-start.17 = (f32[4,64,128]{2,1,0:T(8,128)S(1)}, f32[4,64,128]{2,1,0:T(8,128)S(1)}, u32[]{:S(2)}, u32[]{:S(2)}) collective-permute-start(f32[4,64,128]{2,1,0:T(8,128)S(1)} %fusion.2), channel_id=1, source_target_pairs={{0,4},{2,6},{4,0},{6,2},{8,12},{10,14},{12,8},{14,10},{16,20},{18,... | collective-permute-start | bytes 393224 | tf_op jit(solution)/shard_map/ppermute | solution.py:47
  66.0 4.5 %collective-permute-start.18 = (f32[8,64,128]{2,1,0:T(8,128)S(1)}, f32[8,64,128]{2,1,0:T(8,128)S(1)}, u32[]{:S(2)}, u32[]{:S(2)}) collective-permute-start(f32[8,64,128]{2,1,0:T(8,128)S(1)} %pad_maximum_fusion.2), channel_id=1, source_target_pairs={{0,2},{2,0},{4,6},{6,4},{8,10},{10,8},{12,14},{14,12},{16,18},{18,... | collective-permute-start | bytes 786440 | tf_op jit(solution)/shard_map/ppermute | solution.py:47
  71.1 2.8 %collective-permute-start.19 = (f32[64,64]{1,0:T(8,128)S(1)}, f32[64,64]{1,0:T(8,128)S(1)}, u32[]{:S(2)}, u32[]{:S(2)}) collective-permute-start(f32[64,64]{1,0:T(8,128)S(1)} %gram.2.ga_ref), channel_id=1, source_target_pairs={{0,1},{1,0},{2,3},{3,2},{4,5},{5,4},{6,7},{7,6},{8,9},{9,8},{10,11... | collective-permute-start | bytes 49160 | tf_op jit(solution)/shard_map/ppermute | solution.py:416
  77.2 6.3 %collective-permute-start.21 = (f32[64,1024]{1,0:T(8,128)S(1)}, f32[64,1024]{1,0:T(8,128)S(1)}, u32[]{:S(2)}, u32[]{:S(2)}) collective-permute-start(f32[64,1024]{1,0:T(8,128)S(1)} %y_first.1.ya_ref), channel_id=1, source_target_pairs={{0,1},{1,0},{2,3},{3,2},{4,5},{5,4},{6,7},{7,6},{8,9},{9,8},{10,11... | collective-permute-start | bytes 786440 | tf_op jit(solution)/shard_map/ppermute | solution.py:416
  78.7 10.4 %collective-permute-start.20 = (f32[64,1024]{1,0:T(8,128)S(1)}, f32[64,1024]{1,0:T(8,128)S(1)}, u32[]{:S(2)}, u32[]{:S(2)}) collective-permute-start(f32[64,1024]{1,0:T(8,128)S(1)} %y_second.1.ya_ref), channel_id=1, source_target_pairs={{0,1},{1,0},{2,3},{3,2},{4,5},{5,4},{6,7},{7,6},{8,9},{9,8},{10,11... | collective-permute-start | bytes 786440 | tf_op jit(solution)/shard_map/ppermute | solution.py:416
  89.5 3.4 %collective-permute-start.22 = (f32[64,64]{1,0:T(8,128)S(1)}, f32[64,64]{1,0:T(8,128)S(1)}, u32[]{:S(2)}, u32[]{:S(2)}) collective-permute-start(f32[64,64]{1,0:T(8,128)S(1)} %get-tuple-element.43), channel_id=1, source_target_pairs={{0,2},{2,0},{4,6},{6,4},{8,10},{10,8},{12,14},{14,12},{16,18},{18,... | collective-permute-start | bytes 49160 | tf_op jit(solution)/shard_map/ppermute | solution.py:488
  95.6 4.6 %collective-permute-start.26 = (f32[64,64]{1,0:T(8,128)S(1)}, f32[64,64]{1,0:T(8,128)S(1)}, u32[]{:S(2)}, u32[]{:S(2)}) collective-permute-start(f32[64,64]{1,0:T(8,128)S(1)} %add.93), channel_id=1, source_target_pairs={{0,24},{2,26},{4,28},{6,30},{8,16},{10,18},{12,20},{14,22},{16,8},... | collective-permute-start | bytes 49160 | tf_op jit(solution)/shard_map/ppermute | solution.py:488
  97.3 3.7 %collective-permute-start.25 = (f32[64,64]{1,0:T(8,128)S(1)}, f32[64,64]{1,0:T(8,128)S(1)}, u32[]{:S(2)}, u32[]{:S(2)}) collective-permute-start(f32[64,64]{1,0:T(8,128)S(1)} %add.93), channel_id=1, source_target_pairs={{0,16},{2,18},{4,20},{6,22},{8,24},{10,26},{12,28},{14,30},{16,0},... | collective-permute-start | bytes 49160 | tf_op jit(solution)/shard_map/ppermute | solution.py:488
  103.9 4.3 %collective-permute-start.27 = (bf16[8,64,128]{2,1,0:T(8,128)(2,1)S(1)}, bf16[8,64,128]{2,1,0:T(8,128)(2,1)S(1)}, u32[]{:S(2)}, u32[]{:S(2)}) collective-permute-start(bf16[8,64,128]{2,1,0:T(8,128)(2,1)S(1)} %z_far.3), channel_id=1, source_target_pairs={{0,2},{2,0},{4,6},{6,4},{8,10},{10,8},{12,14},{14,12},{16,18},{18,... | collective-permute-start | bytes 393224 | tf_op jit(solution)/shard_map/ppermute | solution.py:54
  108.2 3.2 %collective-permute-start.28 = (bf16[4,64,128]{2,1,0:T(8,128)(2,1)S(1)}, bf16[4,64,128]{2,1,0:T(8,128)(2,1)S(1)}, u32[]{:S(2)}, u32[]{:S(2)}) collective-permute-start(bf16[4,64,128]{2,1,0:T(8,128)(2,1)S(1)} %slice.144), channel_id=1, source_target_pairs={{0,4},{2,6},{4,0},{6,2},{8,12},{10,14},{12,8},{14,10},{16,20},{18,... | collective-permute-start | bytes 196616 | tf_op jit(solution)/shard_map/ppermute | solution.py:61
  111.4 4.8 %collective-permute-start.30 = (bf16[4,64,128]{2,1,0:T(8,128)(2,1)S(1)}, bf16[4,64,128]{2,1,0:T(8,128)(2,1)S(1)}, u32[]{:S(2)}, u32[]{:S(2)}) collective-permute-start(bf16[4,64,128]{2,1,0:T(8,128)(2,1)S(1)} %fusion), channel_id=1, source_target_pairs={{0,16},{2,18},{4,20},{6,22},{8,24},{10,26},{12,28},{14,30},{16,0},... | collective-permute-start | bytes 196616 | tf_op jit(solution)/shard_map/ppermute | solution.py:70
  112.5 5.4 %collective-permute-start.31 = (bf16[4,64,128]{2,1,0:T(8,128)(2,1)S(1)}, bf16[4,64,128]{2,1,0:T(8,128)(2,1)S(1)}, u32[]{:S(2)}, u32[]{:S(2)}) collective-permute-start(bf16[4,64,128]{2,1,0:T(8,128)(2,1)S(1)} %fusion), channel_id=1, source_target_pairs={{0,24},{2,26},{4,28},{6,30},{8,16},{10,18},{12,20},{14,22},{16,8},... | collective-permute-start | bytes 196616 | tf_op jit(solution)/shard_map/ppermute | solution.py:70
  114.2 4.1 %collective-permute-start.29 = (bf16[4,64,128]{2,1,0:T(8,128)(2,1)S(1)}, bf16[4,64,128]{2,1,0:T(8,128)(2,1)S(1)}, u32[]{:S(2)}, u32[]{:S(2)}) collective-permute-start(bf16[4,64,128]{2,1,0:T(8,128)(2,1)S(1)} %fusion), channel_id=1, source_target_pairs={{0,8},{2,10},{4,12},{6,14},{8,0},{10,2},{12,4},{14,6},{16,24},{18,... | collective-permute-start | bytes 196616 | tf_op jit(solution)/shard_map/ppermute | solution.py:70
  118.3 3.2 %collective-permute-start.32 = (bf16[4,64,128]{2,1,0:T(8,128)(2,1)S(1)}, bf16[4,64,128]{2,1,0:T(8,128)(2,1)S(1)}, u32[]{:S(2)}, u32[]{:S(2)}) collective-permute-start(bf16[4,64,128]{2,1,0:T(8,128)(2,1)S(1)} %get-tuple-element.53), channel_id=1, source_target_pairs={{0,4},{2,6},{4,0},{6,2},{8,12},{10,14},{12,8},{14,10},{16,20},{18,... | collective-permute-start | bytes 196616 | tf_op jit(solution)/shard_map/ppermute | solution.py:47
  121.5 5.1 %collective-permute-start.33 = (bf16[8,64,128]{2,1,0:T(8,128)(2,1)S(1)}, bf16[8,64,128]{2,1,0:T(8,128)(2,1)S(1)}, u32[]{:S(2)}, u32[]{:S(2)}) collective-permute-start(bf16[8,64,128]{2,1,0:T(8,128)(2,1)S(1)} %pad_maximum_fusion.4), channel_id=1, source_target_pairs={{0,2},{2,0},{4,6},{6,4},{8,10},{10,8},{12,14},{14,12},{16,18},{18,... | collective-permute-start | bytes 393224 | tf_op jit(solution)/shard_map/ppermute | solution.py:47
  126.9 2.8 %collective-permute-start.34 = (f32[64,64]{1,0:T(8,128)S(1)}, f32[64,64]{1,0:T(8,128)S(1)}, u32[]{:S(2)}, u32[]{:S(2)}) collective-permute-start(f32[64,64]{1,0:T(8,128)S(1)} %gram.3.ga_ref), channel_id=1, source_target_pairs={{0,1},{1,0},{2,3},{3,2},{4,5},{5,4},{6,7},{7,6},{8,9},{9,8},{10,11... | collective-permute-start | bytes 49160 | tf_op jit(solution)/shard_map/ppermute | solution.py:416
  (5 other events, 19.0 us)

commit v4 on v3

--- a/solution.py
+++ b/solution.py
@@ -156,13 +156,13 @@
 
 
 def y_gram_kernel(ya_ref, yb_ref, y_ref, g_ref):
-    y = ya_ref[...] + yb_ref[...]
+    y = ya_ref[...].astype(F32) + yb_ref[...].astype(F32)
     y_ref[...] = y
     g_ref[...] = exact_dot(y, y, NT)
 
 
 def y_gram_more_kernel(ya_ref, yb_ref, old_ref, y_ref, g_ref):
-    y = ya_ref[...] + yb_ref[...]
+    y = ya_ref[...].astype(F32) + yb_ref[...].astype(F32)
     y_ref[...] = y
     g_ref[...] = old_ref[...] + exact_dot(y, y, NT)
 
@@ -299,7 +299,8 @@
 
 
 def y_kernel(at, q_ref, r_ref, y_ref):
-    y_ref[...] = y_of(cat_tiles(q_ref, slice(None)), r_ref, at, y_ref.shape[1])
+    y = y_of(cat_tiles(q_ref, slice(None)), r_ref, at, y_ref.shape[1])
+    y_ref[...] = y.astype(y_ref.dtype)
 
 
 def left_kernel(radius, user_scale, y_ref, at_ref, left_ref, user_ref):
@@ -452,7 +453,9 @@
 
     half = users_dev // 2
     r_shape = ((users_dev, items_dev), BF16)
-    y_f32 = ((rank, half), F32)
+    y_f32, y_bf16 = ((rank, half), F32), ((rank, half), BF16)
+    some = users_dev // 4
+    y_some, y_rest = ((rank, some), F32), ((rank, users_dev - some), F32)
     half_flops = 2 * rank * half * items_dev
 
     work = [fac_a, tile_row, tile_col, tile_count]
@@ -494,7 +497,8 @@
     square = ((rank, rank), F32)
 
     def user_step(firsts, seconds, exact):
-        y_0, gram = call(y_gram_kernel, [y_f32, square], "y_gram", *firsts, flops=half_flops)
+        summed = [(firsts[0].shape, F32), square]
+        y_0, gram = call(y_gram_kernel, summed, "y_gram", *firsts, flops=half_flops)
         whole = [((rank, users_dev), F32)]
         if not exact:
             return call(y_near_hat_kernel, whole, "y_hat", over_users(gram), y_0, *seconds)
@@ -515,7 +519,7 @@
 
     resid, y_0 = call(
         first_kernel,
-        [r_shape, y_f32],
+        [r_shape, y_some],
         "resid_y",
         slots,
         ratings,
@@ -526,16 +530,18 @@
         input_output_aliases={4: 0},
     )
     firsts = across(y_0)
-    y_1 = call(functools.partial(omega_kernel, half), [y_f32], "y_omega", bq, resid, flops=half_flops)
+    kernel = functools.partial(omega_kernel, some)
+    y_1 = call(kernel, [y_rest], "y_omega", bq, resid, flops=half_flops)
+    firsts, y_1 = lax.optimization_barrier((firsts, y_1))
     seconds = across(y_1)
     old, _, _ = item_step(user_step(firsts, seconds, False), F32)
 
     gram = across(call(gram_kernel, [square], "gram", old))
     q = call(q_kernel, [((item_tiles, rank, tile), BF16)], "q", *gram, old)
     kernel = functools.partial(y_kernel, 0)
-    firsts = across(call(kernel, [y_f32], "y_first", q, resid, flops=half_flops))
+    firsts = across(call(kernel, [y_bf16], "y_first", q, resid, flops=half_flops))
     kernel = functools.partial(y_kernel, half)
-    seconds = across(call(kernel, [y_f32], "y_second", q, resid, flops=half_flops))
+    seconds = across(call(kernel, [y_bf16], "y_second", q, resid, flops=half_flops))
     y_hat = user_step(firsts, seconds, True)
     left, user_dir = call(
         functools.partial(left_kernel, radius, math.sqrt(users)),

time: 137 us -> 128 us (0.934)
  waiting for transfers between devices: 61.3 us -> 50.7 us
  starting transfers between devices: 42.6 us -> 44 us
    ppermute x6, waiting for transfers between devices: 20.2 us -> 9.75 us  [across(): other = lax.ppermute(mine, 'item', xor_pairs(n_item, bit))]
  transfers between devices with their start and end apart: 35 -> 35, of which waited for: 30 -> 31; matrix products, arithmetic and copies ran while one was open for 1% -> 1% of each run, Pallas kernels for 5% -> 6%
where the time goes in v4:
time: 128 us; the launch traced here: 126 us
  waiting for transfers between devices  50.7 us (40%)
  starting transfers between devices  44 us (34%)
  Pallas kernels  25.6 us (20%)
  other arithmetic  2.45 us (2%)
  between operations  1.86 us (1%)
    pallas_call x19, Pallas kernels, call(): pl.pallas_call(kernel, out_shape=outs, in_specs=[SMEM] * smem + [pl.Block...  25.6 us
    ppermute x9, starting transfers between devices, gather_blocks(): got.append(lax.ppermute(held, axis, xor_pairs(size, k << at)))  15 us
    ppermute x6, waiting for transfers between devices, reduce_blocks(): lax.ppermute(mine, axis, xor_pairs(size, k << at))  12.5 us
    ppermute x10, starting transfers between devices, over_users(): terms.append(lax.ppermute(part, 'user', xor_pairs(n_user, k << at)))  11.1 us
    ppermute x10, waiting for transfers between devices, over_users(): terms.append(lax.ppermute(part, 'user', xor_pairs(n_user, k << at)))  11 us
    ppermute x6, waiting for transfers between devices, across(): other = lax.ppermute(mine, 'item', xor_pairs(n_item, bit))  9.75 us
    ppermute x9, waiting for transfers between devices, gather_blocks(): got.append(lax.ppermute(held, axis, xor_pairs(size, k << at)))  9.53 us
    ppermute x2, waiting for transfers between devices, reduce_blocks(): lax.ppermute(pieces[k].astype(kind), axis, xor_pairs(size, k << at))  7.44 us
  transfers between devices with their start and end apart: 35, of which 31 were waited for; matrix products, arithmetic and copies ran while one was open for 1% of the time, Pallas kernels for 6%

profile of v4, /device:TPU:29, one launch (start us, length us, event | category | flops | bytes accessed | tf_op | source)
XLA Modules:
  0.0 125.9 jit_solution(6278319324301432828)
XLA Ops:
  2.7 2.2 %collective-permute-start = (bf16[1,128,128]{2,1,0:T(8,128)(2,1)S(1)}, bf16[1,128,128]{2,1,0:T(8,128)(2,1)S(1)}, u32[]{:S(2)}, u32[]{:S(2)}) collective-permute-start(bf16[1,128,128]{2,1,0:T(8,128)(2,1)S(1)} %bitcast.16), channel_id=1, source_target_pairs={{0,8},{2,10},{4,12},{6,14},{8,0},{10,2},{12,4},{14,6},{16,24},{18,... | collective-permute-start | bytes 98312 | tf_op jit(solution)/shard_map/ppermute | solution.py:47
  10.5 2.9 %collective-permute-start.4 = (bf16[8,128,128]{2,1,0:T(8,128)(2,1)S(1)}, bf16[8,128,128]{2,1,0:T(8,128)(2,1)S(1)}, u32[]{:S(2)}, u32[]{:S(2)}) collective-permute-start(bf16[8,128,128]{2,1,0:T(8,128)(2,1)S(1)} %pad_maximum_fusion.1), channel_id=1, source_target_pairs={{0,2},{2,0},{4,6},{6,4},{8,10},{10,8},{12,14},{14,12},{16,18},{18,... | collective-permute-start | bytes 786440 | tf_op jit(solution)/shard_map/ppermute | solution.py:47
  14.7 3.3 %resid_y.1 = (bf16[2048,2048]{1,0:T(8,128)(2,1)S(1)}, f32[64,512]{1,0:T(8,128)S(1)}) custom-call(s32[3,128]{1,0:T(4,128)S(1)} %add_add_fusion.2.slot_ref.slot_any, bf16[128,128,128]{2,1,0:T(8,128)(2,1)S(1)} %bitcast.12, bf16[2048,64]{1,0:T(8,128)(2,1)S(1)} %get-tuple-element.38.at_ref, ...), custom_call_target="tpu_custom_call", output_to_operand_aliasing={{0}: (4, {})} | custom-call | bytes 65536 | tf_op jit(solution)/shard_map/resid_y/pallas_call | solution.py:440
  19.2 2.0 %y_omega.1.ya_ref = f32[64,1536]{1,0:T(8,128)S(1)} custom-call(bf16[16,128,128]{2,1,0:T(8,128)(2,1)S(1)} %constant_dynamic-update-slice_fusion.bq_ref, bf16[2048,2048]{1,0:T(8,128)(2,1)S(1)} %get-tuple-element.42.r_ref), custom_call_target="tpu_custom_call" | custom-call | flops 268435456 | bytes 65536 | tf_op jit(solution)/shard_map/y_omega/pallas_call | solution.py:440
  21.3 1.5 %collective-permute-done.5.yb_ref = f32[64,512]{1,0:T(8,128)S(1)} collective-permute-done((f32[64,512]{1,0:T(8,128)S(1)}, f32[64,512]{1,0:T(8,128)S(1)}, u32[]{:S(2)}, u32[]{:S(2)}) %collective-permute-start.5) | collective-permute-done | bytes 131104 | tf_op jit(solution)/shard_map/ppermute | solution.py:417
  24.2 1.5 %collective-permute-start.6 = (f32[64,64]{1,0:T(8,128)S(1)}, f32[64,64]{1,0:T(8,128)S(1)}, u32[]{:S(2)}, u32[]{:S(2)}) collective-permute-start(f32[64,64]{1,0:T(8,128)S(1)} %get-tuple-element.45), channel_id=1, source_target_pairs={{0,2},{2,0},{4,6},{6,4},{8,10},{10,8},{12,14},{14,12},{16,18},{18,... | collective-permute-start | bytes 49160 | tf_op jit(solution)/shard_map/ppermute | solution.py:491
  26.6 3.1 %collective-permute-done.7 = f32[64,64]{1,0:T(8,128)S(1)} collective-permute-done((f32[64,64]{1,0:T(8,128)S(1)}, f32[64,64]{1,0:T(8,128)S(1)}, u32[]{:S(2)}, u32[]{:S(2)}) %collective-permute-start.7) | collective-permute-done | bytes 16416 | tf_op jit(solution)/shard_map/ppermute | solution.py:491
  30.3 1.8 %collective-permute-start.9 = (f32[64,64]{1,0:T(8,128)S(1)}, f32[64,64]{1,0:T(8,128)S(1)}, u32[]{:S(2)}, u32[]{:S(2)}) collective-permute-start(f32[64,64]{1,0:T(8,128)S(1)} %add.83), channel_id=1, source_target_pairs={{0,16},{2,18},{4,20},{6,22},{8,24},{10,26},{12,28},{14,30},{16,0},... | collective-permute-start | bytes 49160 | tf_op jit(solution)/shard_map/ppermute | solution.py:491
  34.9 1.7 %y_hat.2.y_ref = f32[64,2048]{1,0:T(8,128)S(1)} custom-call(f32[64,64]{1,0:T(8,128)S(1)} %add_add_fusion.1.g_ref, f32[64,512]{1,0:T(8,128)S(1)} %get-tuple-element.46.y_0, f32[64,1536]{1,0:T(8,128)S(1)} %y_omega.1.ya_ref, f32[64,1536]{1,0:T(8,128)S(1)} %collective-permute-done.11.yb_ref), custom_call_target="tpu_custom_call" | custom-call | bytes 65536 | tf_op jit(solution)/shard_map/y_hat/pallas_call | solution.py:440
  37.5 3.0 %collective-permute-start.12 = (f32[8,64,128]{2,1,0:T(8,128)S(1)}, f32[8,64,128]{2,1,0:T(8,128)S(1)}, u32[]{:S(2)}, u32[]{:S(2)}) collective-permute-start(f32[8,64,128]{2,1,0:T(8,128)S(1)} %z_far.2), channel_id=1, source_target_pairs={{0,2},{2,0},{4,6},{6,4},{8,10},{10,8},{12,14},{14,12},{16,18},{18,... | collective-permute-start | bytes 786440 | tf_op jit(solution)/shard_map/ppermute | solution.py:54
  41.7 4.7 %collective-permute-done.13 = f32[4,64,128]{2,1,0:T(8,128)S(1)} collective-permute-done((f32[4,64,128]{2,1,0:T(8,128)S(1)}, f32[4,64,128]{2,1,0:T(8,128)S(1)}, u32[]{:S(2)}, u32[]{:S(2)}) %collective-permute-start.13) | collective-permute-done | bytes 131104 | tf_op jit(solution)/shard_map/ppermute | solution.py:61
  47.2 2.5 %collective-permute-start.16 = (f32[4,64,128]{2,1,0:T(8,128)S(1)}, f32[4,64,128]{2,1,0:T(8,128)S(1)}, u32[]{:S(2)}, u32[]{:S(2)}) collective-permute-start(f32[4,64,128]{2,1,0:T(8,128)S(1)} %slice_add_fusion.1), channel_id=1, source_target_pairs={{0,24},{2,26},{4,28},{6,30},{8,16},{10,18},{12,20},{14,22},{16,8},... | collective-permute-start | bytes 393224 | tf_op jit(solution)/shard_map/ppermute | solution.py:70
  49.7 7.1 %collective-permute-done.15 = f32[4,64,128]{2,1,0:T(8,128)S(1)} collective-permute-done((f32[4,64,128]{2,1,0:T(8,128)S(1)}, f32[4,64,128]{2,1,0:T(8,128)S(1)}, u32[]{:S(2)}, u32[]{:S(2)}) %collective-permute-start.15) | collective-permute-done | bytes 131104 | tf_op jit(solution)/shard_map/ppermute | solution.py:70
  58.5 3.6 %collective-permute-done.17 = f32[4,64,128]{2,1,0:T(8,128)S(1)} collective-permute-done((f32[4,64,128]{2,1,0:T(8,128)S(1)}, f32[4,64,128]{2,1,0:T(8,128)S(1)}, u32[]{:S(2)}, u32[]{:S(2)}) %collective-permute-start.17) | collective-permute-done | bytes 131104 | tf_op jit(solution)/shard_map/ppermute | solution.py:47
  62.1 3.4 %collective-permute-start.18 = (f32[8,64,128]{2,1,0:T(8,128)S(1)}, f32[8,64,128]{2,1,0:T(8,128)S(1)}, u32[]{:S(2)}, u32[]{:S(2)}) collective-permute-start(f32[8,64,128]{2,1,0:T(8,128)S(1)} %pad_maximum_fusion.2), channel_id=1, source_target_pairs={{0,2},{2,0},{4,6},{6,4},{8,10},{10,8},{12,14},{14,12},{16,18},{18,... | collective-permute-start | bytes 786440 | tf_op jit(solution)/shard_map/ppermute | solution.py:47
  67.6 2.5 %collective-permute-done.19.gb_ref = f32[64,64]{1,0:T(8,128)S(1)} collective-permute-done((f32[64,64]{1,0:T(8,128)S(1)}, f32[64,64]{1,0:T(8,128)S(1)}, u32[]{:S(2)}, u32[]{:S(2)}) %collective-permute-start.19) | collective-permute-done | bytes 16416 | tf_op jit(solution)/shard_map/ppermute | solution.py:417
  70.1 1.8 %q.1.q_ref = bf16[16,64,128]{2,1,0:T(8,128)(2,1)S(1)} custom-call(f32[64,64]{1,0:T(8,128)S(1)} %gram.2.ga_ref, f32[64,64]{1,0:T(8,128)S(1)} %collective-permute-done.19.gb_ref, f32[16,64,128]{2,1,0:T(8,128)S(1)} %pad_maximum_fusion.z_ref), custom_call_target="tpu_custom_call" | custom-call | bytes 65536 | tf_op jit(solution)/shard_map/q/pallas_call | solution.py:440
  71.9 1.4 %y_first.1.ya_ref = bf16[64,1024]{1,0:T(8,128)(2,1)S(1)} custom-call(bf16[16,64,128]{2,1,0:T(8,128)(2,1)S(1)} %q.1.q_ref, bf16[2048,2048]{1,0:T(8,128)(2,1)S(1)} %get-tuple-element.42.r_ref), custom_call_target="tpu_custom_call" | custom-call | flops 268435456 | bytes 65536 | tf_op jit(solution)/shard_map/y_first/pallas_call | solution.py:440
  77.5 2.8 %collective-permute-done.20.yb_ref = bf16[64,1024]{1,0:T(8,128)(2,1)S(1)} collective-permute-done((bf16[64,1024]{1,0:T(8,128)(2,1)S(1)}, bf16[64,1024]{1,0:T(8,128)(2,1)S(1)}, u32[]{:S(2)}, u32[]{:S(2)}) %collective-permute-start.20) | collective-permute-done | bytes 131104 | tf_op jit(solution)/shard_map/ppermute | solution.py:417
  80.7 2.1 %collective-permute-start.22 = (f32[64,64]{1,0:T(8,128)S(1)}, f32[64,64]{1,0:T(8,128)S(1)}, u32[]{:S(2)}, u32[]{:S(2)}) collective-permute-start(f32[64,64]{1,0:T(8,128)S(1)} %get-tuple-element.49), channel_id=1, source_target_pairs={{0,2},{2,0},{4,6},{6,4},{8,10},{10,8},{12,14},{14,12},{16,18},{18,... | collective-permute-start | bytes 49160 | tf_op jit(solution)/shard_map/ppermute | solution.py:491
  84.0 2.4 %collective-permute-done.23 = f32[64,64]{1,0:T(8,128)S(1)} collective-permute-done((f32[64,64]{1,0:T(8,128)S(1)}, f32[64,64]{1,0:T(8,128)S(1)}, u32[]{:S(2)}, u32[]{:S(2)}) %collective-permute-start.23) | collective-permute-done | bytes 16416 | tf_op jit(solution)/shard_map/ppermute | solution.py:491
  86.5 1.6 %collective-permute-start.26 = (f32[64,64]{1,0:T(8,128)S(1)}, f32[64,64]{1,0:T(8,128)S(1)}, u32[]{:S(2)}, u32[]{:S(2)}) collective-permute-start(f32[64,64]{1,0:T(8,128)S(1)} %add.93), channel_id=1, source_target_pairs={{0,24},{2,26},{4,28},{6,30},{8,16},{10,18},{12,20},{14,22},{16,8},... | collective-permute-start | bytes 49160 | tf_op jit(solution)/shard_map/ppermute | solution.py:491
  92.2 1.7 %y_hat.3.y_ref = f32[64,2048]{1,0:T(8,128)S(1)} custom-call(f32[64,64]{1,0:T(8,128)S(1)} %add_add_fusion.g_ref, f32[64,1024]{1,0:T(8,128)S(1)} %get-tuple-element.50.y_0, f32[64,1024]{1,0:T(8,128)S(1)} %get-tuple-element.51.y_1), custom_call_target="tpu_custom_call" | custom-call | bytes 65536 | tf_op jit(solution)/shard_map/y_hat/pallas_call | solution.py:440
  94.7 3.3 %collective-permute-start.27 = (bf16[8,64,128]{2,1,0:T(8,128)(2,1)S(1)}, bf16[8,64,128]{2,1,0:T(8,128)(2,1)S(1)}, u32[]{:S(2)}, u32[]{:S(2)}) collective-permute-start(bf16[8,64,128]{2,1,0:T(8,128)(2,1)S(1)} %z_far.3), channel_id=1, source_target_pairs={{0,2},{2,0},{4,6},{6,4},{8,10},{10,8},{12,14},{14,12},{16,18},{18,... | collective-permute-start | bytes 393224 | tf_op jit(solution)/shard_map/ppermute | solution.py:54
  99.5 2.7 %collective-permute-done.28 = bf16[4,64,128]{2,1,0:T(8,128)(2,1)S(1)} collective-permute-done((bf16[4,64,128]{2,1,0:T(8,128)(2,1)S(1)}, bf16[4,64,128]{2,1,0:T(8,128)(2,1)S(1)}, u32[]{:S(2)}, u32[]{:S(2)}) %collective-permute-start.28) | collective-permute-done | bytes 65568 | tf_op jit(solution)/shard_map/ppermute | solution.py:61
  103.4 1.6 %collective-permute-start.31 = (bf16[4,64,128]{2,1,0:T(8,128)(2,1)S(1)}, bf16[4,64,128]{2,1,0:T(8,128)(2,1)S(1)}, u32[]{:S(2)}, u32[]{:S(2)}) collective-permute-start(bf16[4,64,128]{2,1,0:T(8,128)(2,1)S(1)} %fusion), channel_id=1, source_target_pairs={{0,24},{2,26},{4,28},{6,30},{8,16},{10,18},{12,20},{14,22},{16,8},... | collective-permute-start | bytes 196616 | tf_op jit(solution)/shard_map/ppermute | solution.py:70
  105.0 2.0 %collective-permute-done.30 = bf16[4,64,128]{2,1,0:T(8,128)(2,1)S(1)} collective-permute-done((bf16[4,64,128]{2,1,0:T(8,128)(2,1)S(1)}, bf16[4,64,128]{2,1,0:T(8,128)(2,1)S(1)}, u32[]{:S(2)}, u32[]{:S(2)}) %collective-permute-start.30) | collective-permute-done | bytes 65568 | tf_op jit(solution)/shard_map/ppermute | solution.py:70
  107.0 1.7 %collective-permute-done.31 = bf16[4,64,128]{2,1,0:T(8,128)(2,1)S(1)} collective-permute-done((bf16[4,64,128]{2,1,0:T(8,128)(2,1)S(1)}, bf16[4,64,128]{2,1,0:T(8,128)(2,1)S(1)}, u32[]{:S(2)}, u32[]{:S(2)}) %collective-permute-start.31) | collective-permute-done | bytes 65568 | tf_op jit(solution)/shard_map/ppermute | solution.py:70
  110.9 1.4 %collective-permute-done.32 = bf16[4,64,128]{2,1,0:T(8,128)(2,1)S(1)} collective-permute-done((bf16[4,64,128]{2,1,0:T(8,128)(2,1)S(1)}, bf16[4,64,128]{2,1,0:T(8,128)(2,1)S(1)}, u32[]{:S(2)}, u32[]{:S(2)}) %collective-permute-start.32) | collective-permute-done | bytes 65568 | tf_op jit(solution)/shard_map/ppermute | solution.py:47
  112.4 4.1 %collective-permute-start.33 = (bf16[8,64,128]{2,1,0:T(8,128)(2,1)S(1)}, bf16[8,64,128]{2,1,0:T(8,128)(2,1)S(1)}, u32[]{:S(2)}, u32[]{:S(2)}) collective-permute-start(bf16[8,64,128]{2,1,0:T(8,128)(2,1)S(1)} %pad_maximum_fusion.4), channel_id=1, source_target_pairs={{0,2},{2,0},{4,6},{6,4},{8,10},{10,8},{12,14},{14,12},{16,18},{18,... | collective-permute-start | bytes 393224 | tf_op jit(solution)/shard_map/ppermute | solution.py:47
  118.4 2.1 %collective-permute-done.34.gb_ref = f32[64,64]{1,0:T(8,128)S(1)} collective-permute-done((f32[64,64]{1,0:T(8,128)S(1)}, f32[64,64]{1,0:T(8,128)S(1)}, u32[]{:S(2)}, u32[]{:S(2)}) %collective-permute-start.34) | collective-permute-done | bytes 16416 | tf_op jit(solution)/shard_map/ppermute | solution.py:417
  120.5 5.2 %loss.1 = (f32[64,128]{1,0:T(8,128)}, f32[128,128]{1,0:T(8,128)}) custom-call(s32[3,128]{1,0:T(4,128)S(1)} %add_add_fusion.2.slot_ref.slot_any, f32[64,64]{1,0:T(8,128)S(1)} %gram.3.ga_ref, f32[64,64]{1,0:T(8,128)S(1)} %collective-permute-done.34.gb_ref, bf16[16,64,128]{2,1,0:T(8,128)(2,1)S(1)} %constant_dynamic-update-slice_fusion.2.z_ref, ...), custom_call_target="tpu_custom_call" | custom-call | bytes 65536 | tf_op jit(solution)/shard_map/loss/pallas_call | solution.py:440
  (95 shorter events, 39.3 us)
Async XLA Ops:
  1.4 4.6 %collective-permute-start.2 = (bf16[1,128,128]{2,1,0:T(8,128)(2,1)S(1)}, bf16[1,128,128]{2,1,0:T(8,128)(2,1)S(1)}, u32[]{:S(2)}, u32[]{:S(2)}) collective-permute-start(bf16[1,128,128]{2,1,0:T(8,128)(2,1)S(1)} %bitcast.14), channel_id=1, source_target_pairs={{0,24},{2,26},{4,28},{6,30},{8,16},{10,18},{12,20},{14,22},{16,8},... | collective-permute-start | bytes 98312 | tf_op jit(solution)/shard_map/ppermute | solution.py:47
  1.4 4.6 %collective-permute-start.1 = (bf16[1,128,128]{2,1,0:T(8,128)(2,1)S(1)}, bf16[1,128,128]{2,1,0:T(8,128)(2,1)S(1)}, u32[]{:S(2)}, u32[]{:S(2)}) collective-permute-start(bf16[1,128,128]{2,1,0:T(8,128)(2,1)S(1)} %bitcast.15), channel_id=1, source_target_pairs={{0,16},{2,18},{4,20},{6,22},{8,24},{10,26},{12,28},{14,30},{16,0},... | collective-permute-start | bytes 98312 | tf_op jit(solution)/shard_map/ppermute | solution.py:47
  2.7 3.9 %collective-permute-start = (bf16[1,128,128]{2,1,0:T(8,128)(2,1)S(1)}, bf16[1,128,128]{2,1,0:T(8,128)(2,1)S(1)}, u32[]{:S(2)}, u32[]{:S(2)}) collective-permute-start(bf16[1,128,128]{2,1,0:T(8,128)(2,1)S(1)} %bitcast.16), channel_id=1, source_target_pairs={{0,8},{2,10},{4,12},{6,14},{8,0},{10,2},{12,4},{14,6},{16,24},{18,... | collective-permute-start | bytes 98312 | tf_op jit(solution)/shard_map/ppermute | solution.py:47
  6.6 3.9 %collective-permute-start.3 = (bf16[4,128,128]{2,1,0:T(8,128)(2,1)S(1)}, bf16[4,128,128]{2,1,0:T(8,128)(2,1)S(1)}, u32[]{:S(2)}, u32[]{:S(2)}) collective-permute-start(bf16[4,128,128]{2,1,0:T(8,128)(2,1)S(1)} %pad_maximum_fusion.3), channel_id=1, source_target_pairs={{0,4},{2,6},{4,0},{6,2},{8,12},{10,14},{12,8},{14,10},{16,20},{18,... | collective-permute-start | bytes 393224 | tf_op jit(solution)/shard_map/ppermute | solution.py:47
  10.5 4.1 %collective-permute-start.4 = (bf16[8,128,128]{2,1,0:T(8,128)(2,1)S(1)}, bf16[8,128,128]{2,1,0:T(8,128)(2,1)S(1)}, u32[]{:S(2)}, u32[]{:S(2)}) collective-permute-start(bf16[8,128,128]{2,1,0:T(8,128)(2,1)S(1)} %pad_maximum_fusion.1), channel_id=1, source_target_pairs={{0,2},{2,0},{4,6},{6,4},{8,10},{10,8},{12,14},{14,12},{16,18},{18,... | collective-permute-start | bytes 786440 | tf_op jit(solution)/shard_map/ppermute | solution.py:47
  18.0 4.8 %collective-permute-start.5 = (f32[64,512]{1,0:T(8,128)S(1)}, f32[64,512]{1,0:T(8,128)S(1)}, u32[]{:S(2)}, u32[]{:S(2)}) collective-permute-start(f32[64,512]{1,0:T(8,128)S(1)} %get-tuple-element.43.ya_ref), channel_id=1, source_target_pairs={{0,1},{1,0},{2,3},{3,2},{4,5},{5,4},{6,7},{7,6},{8,9},{9,8},{10,11... | collective-permute-start | bytes 393224 | tf_op jit(solution)/shard_map/ppermute | solution.py:417
  22.7 12.2 %collective-permute-start.11 = (f32[64,1536]{1,0:T(8,128)S(1)}, f32[64,1536]{1,0:T(8,128)S(1)}, u32[]{:S(2)}, u32[]{:S(2)}) collective-permute-start(f32[64,1536]{1,0:T(8,128)S(1)} %y_omega.1.ya_ref), channel_id=1, source_target_pairs={{0,1},{1,0},{2,3},{3,2},{4,5},{5,4},{6,7},{7,6},{8,9},{9,8},{10,11... | collective-permute-start | bytes 1179656 | tf_op jit(solution)/shard_map/ppermute | solution.py:417
  26.6 3.1 %collective-permute-start.7 = (f32[64,64]{1,0:T(8,128)S(1)}, f32[64,64]{1,0:T(8,128)S(1)}, u32[]{:S(2)}, u32[]{:S(2)}) collective-permute-start(f32[64,64]{1,0:T(8,128)S(1)} %add.82), channel_id=1, source_target_pairs={{0,4},{2,6},{4,0},{6,2},{8,12},{10,14},{12,8},{14,10},{16,20},{18,... | collective-permute-start | bytes 49160 | tf_op jit(solution)/shard_map/ppermute | solution.py:491
  29.7 4.6 %collective-permute-start.10 = (f32[64,64]{1,0:T(8,128)S(1)}, f32[64,64]{1,0:T(8,128)S(1)}, u32[]{:S(2)}, u32[]{:S(2)}) collective-permute-start(f32[64,64]{1,0:T(8,128)S(1)} %add.83), channel_id=1, source_target_pairs={{0,24},{2,26},{4,28},{6,30},{8,16},{10,18},{12,20},{14,22},{16,8},... | collective-permute-start | bytes 49160 | tf_op jit(solution)/shard_map/ppermute | solution.py:491
  30.3 4.0 %collective-permute-start.9 = (f32[64,64]{1,0:T(8,128)S(1)}, f32[64,64]{1,0:T(8,128)S(1)}, u32[]{:S(2)}, u32[]{:S(2)}) collective-permute-start(f32[64,64]{1,0:T(8,128)S(1)} %add.83), channel_id=1, source_target_pairs={{0,16},{2,18},{4,20},{6,22},{8,24},{10,26},{12,28},{14,30},{16,0},... | collective-permute-start | bytes 49160 | tf_op jit(solution)/shard_map/ppermute | solution.py:491
  37.5 4.1 %collective-permute-start.12 = (f32[8,64,128]{2,1,0:T(8,128)S(1)}, f32[8,64,128]{2,1,0:T(8,128)S(1)}, u32[]{:S(2)}, u32[]{:S(2)}) collective-permute-start(f32[8,64,128]{2,1,0:T(8,128)S(1)} %z_far.2), channel_id=1, source_target_pairs={{0,2},{2,0},{4,6},{6,4},{8,10},{10,8},{12,14},{14,12},{16,18},{18,... | collective-permute-start | bytes 786440 | tf_op jit(solution)/shard_map/ppermute | solution.py:54
  41.6 4.8 %collective-permute-start.13 = (f32[4,64,128]{2,1,0:T(8,128)S(1)}, f32[4,64,128]{2,1,0:T(8,128)S(1)}, u32[]{:S(2)}, u32[]{:S(2)}) collective-permute-start(f32[4,64,128]{2,1,0:T(8,128)S(1)} %slice.114), channel_id=1, source_target_pairs={{0,4},{2,6},{4,0},{6,2},{8,12},{10,14},{12,8},{14,10},{16,20},{18,... | collective-permute-start | bytes 393224 | tf_op jit(solution)/shard_map/ppermute | solution.py:61
  46.4 10.4 %collective-permute-start.15 = (f32[4,64,128]{2,1,0:T(8,128)S(1)}, f32[4,64,128]{2,1,0:T(8,128)S(1)}, u32[]{:S(2)}, u32[]{:S(2)}) collective-permute-start(f32[4,64,128]{2,1,0:T(8,128)S(1)} %slice_add_fusion.1), channel_id=1, source_target_pairs={{0,16},{2,18},{4,20},{6,22},{8,24},{10,26},{12,28},{14,30},{16,0},... | collective-permute-start | bytes 393224 | tf_op jit(solution)/shard_map/ppermute | solution.py:70
  47.2 9.6 %collective-permute-start.16 = (f32[4,64,128]{2,1,0:T(8,128)S(1)}, f32[4,64,128]{2,1,0:T(8,128)S(1)}, u32[]{:S(2)}, u32[]{:S(2)}) collective-permute-start(f32[4,64,128]{2,1,0:T(8,128)S(1)} %slice_add_fusion.1), channel_id=1, source_target_pairs={{0,24},{2,26},{4,28},{6,30},{8,16},{10,18},{12,20},{14,22},{16,8},... | collective-permute-start | bytes 393224 | tf_op jit(solution)/shard_map/ppermute | solution.py:70
  49.7 8.5 %collective-permute-start.14 = (f32[4,64,128]{2,1,0:T(8,128)S(1)}, f32[4,64,128]{2,1,0:T(8,128)S(1)}, u32[]{:S(2)}, u32[]{:S(2)}) collective-permute-start(f32[4,64,128]{2,1,0:T(8,128)S(1)} %slice_add_fusion.1), channel_id=1, source_target_pairs={{0,8},{2,10},{4,12},{6,14},{8,0},{10,2},{12,4},{14,6},{16,24},{18,... | collective-permute-start | bytes 393224 | tf_op jit(solution)/shard_map/ppermute | solution.py:70
  58.2 3.9 %collective-permute-start.17 = (f32[4,64,128]{2,1,0:T(8,128)S(1)}, f32[4,64,128]{2,1,0:T(8,128)S(1)}, u32[]{:S(2)}, u32[]{:S(2)}) collective-permute-start(f32[4,64,128]{2,1,0:T(8,128)S(1)} %fusion.2), channel_id=1, source_target_pairs={{0,4},{2,6},{4,0},{6,2},{8,12},{10,14},{12,8},{14,10},{16,20},{18,... | collective-permute-start | bytes 393224 | tf_op jit(solution)/shard_map/ppermute | solution.py:47
  62.1 4.5 %collective-permute-start.18 = (f32[8,64,128]{2,1,0:T(8,128)S(1)}, f32[8,64,128]{2,1,0:T(8,128)S(1)}, u32[]{:S(2)}, u32[]{:S(2)}) collective-permute-start(f32[8,64,128]{2,1,0:T(8,128)S(1)} %pad_maximum_fusion.2), channel_id=1, source_target_pairs={{0,2},{2,0},{4,6},{6,4},{8,10},{10,8},{12,14},{14,12},{16,18},{18,... | collective-permute-start | bytes 786440 | tf_op jit(solution)/shard_map/ppermute | solution.py:47
  67.3 2.8 %collective-permute-start.19 = (f32[64,64]{1,0:T(8,128)S(1)}, f32[64,64]{1,0:T(8,128)S(1)}, u32[]{:S(2)}, u32[]{:S(2)}) collective-permute-start(f32[64,64]{1,0:T(8,128)S(1)} %gram.2.ga_ref), channel_id=1, source_target_pairs={{0,1},{1,0},{2,3},{3,2},{4,5},{5,4},{6,7},{7,6},{8,9},{9,8},{10,11... | collective-permute-start | bytes 49160 | tf_op jit(solution)/shard_map/ppermute | solution.py:417
  73.3 3.9 %collective-permute-start.21 = (bf16[64,1024]{1,0:T(8,128)(2,1)S(1)}, bf16[64,1024]{1,0:T(8,128)(2,1)S(1)}, u32[]{:S(2)}, u32[]{:S(2)}) collective-permute-start(bf16[64,1024]{1,0:T(8,128)(2,1)S(1)} %y_first.1.ya_ref), channel_id=1, source_target_pairs={{0,1},{1,0},{2,3},{3,2},{4,5},{5,4},{6,7},{7,6},{8,9},{9,8},{10,11... | collective-permute-start | bytes 393224 | tf_op jit(solution)/shard_map/ppermute | solution.py:417
  75.0 5.3 %collective-permute-start.20 = (bf16[64,1024]{1,0:T(8,128)(2,1)S(1)}, bf16[64,1024]{1,0:T(8,128)(2,1)S(1)}, u32[]{:S(2)}, u32[]{:S(2)}) collective-permute-start(bf16[64,1024]{1,0:T(8,128)(2,1)S(1)} %y_second.1.ya_ref), channel_id=1, source_target_pairs={{0,1},{1,0},{2,3},{3,2},{4,5},{5,4},{6,7},{7,6},{8,9},{9,8},{10,11... | collective-permute-start | bytes 393224 | tf_op jit(solution)/shard_map/ppermute | solution.py:417
  80.7 3.0 %collective-permute-start.22 = (f32[64,64]{1,0:T(8,128)S(1)}, f32[64,64]{1,0:T(8,128)S(1)}, u32[]{:S(2)}, u32[]{:S(2)}) collective-permute-start(f32[64,64]{1,0:T(8,128)S(1)} %get-tuple-element.49), channel_id=1, source_target_pairs={{0,2},{2,0},{4,6},{6,4},{8,10},{10,8},{12,14},{14,12},{16,18},{18,... | collective-permute-start | bytes 49160 | tf_op jit(solution)/shard_map/ppermute | solution.py:491
  83.7 2.8 %collective-permute-start.23 = (f32[64,64]{1,0:T(8,128)S(1)}, f32[64,64]{1,0:T(8,128)S(1)}, u32[]{:S(2)}, u32[]{:S(2)}) collective-permute-start(f32[64,64]{1,0:T(8,128)S(1)} %add.92), channel_id=1, source_target_pairs={{0,4},{2,6},{4,0},{6,2},{8,12},{10,14},{12,8},{14,10},{16,20},{18,... | collective-permute-start | bytes 49160 | tf_op jit(solution)/shard_map/ppermute | solution.py:491
  86.5 4.6 %collective-permute-start.26 = (f32[64,64]{1,0:T(8,128)S(1)}, f32[64,64]{1,0:T(8,128)S(1)}, u32[]{:S(2)}, u32[]{:S(2)}) collective-permute-start(f32[64,64]{1,0:T(8,128)S(1)} %add.93), channel_id=1, source_target_pairs={{0,24},{2,26},{4,28},{6,30},{8,16},{10,18},{12,20},{14,22},{16,8},... | collective-permute-start | bytes 49160 | tf_op jit(solution)/shard_map/ppermute | solution.py:491
  88.1 3.7 %collective-permute-start.25 = (f32[64,64]{1,0:T(8,128)S(1)}, f32[64,64]{1,0:T(8,128)S(1)}, u32[]{:S(2)}, u32[]{:S(2)}) collective-permute-start(f32[64,64]{1,0:T(8,128)S(1)} %add.93), channel_id=1, source_target_pairs={{0,16},{2,18},{4,20},{6,22},{8,24},{10,26},{12,28},{14,30},{16,0},... | collective-permute-start | bytes 49160 | tf_op jit(solution)/shard_map/ppermute | solution.py:491
  94.7 4.3 %collective-permute-start.27 = (bf16[8,64,128]{2,1,0:T(8,128)(2,1)S(1)}, bf16[8,64,128]{2,1,0:T(8,128)(2,1)S(1)}, u32[]{:S(2)}, u32[]{:S(2)}) collective-permute-start(bf16[8,64,128]{2,1,0:T(8,128)(2,1)S(1)} %z_far.3), channel_id=1, source_target_pairs={{0,2},{2,0},{4,6},{6,4},{8,10},{10,8},{12,14},{14,12},{16,18},{18,... | collective-permute-start | bytes 393224 | tf_op jit(solution)/shard_map/ppermute | solution.py:54
  99.0 3.2 %collective-permute-start.28 = (bf16[4,64,128]{2,1,0:T(8,128)(2,1)S(1)}, bf16[4,64,128]{2,1,0:T(8,128)(2,1)S(1)}, u32[]{:S(2)}, u32[]{:S(2)}) collective-permute-start(bf16[4,64,128]{2,1,0:T(8,128)(2,1)S(1)} %slice.144), channel_id=1, source_target_pairs={{0,4},{2,6},{4,0},{6,2},{8,12},{10,14},{12,8},{14,10},{16,20},{18,... | collective-permute-start | bytes 196616 | tf_op jit(solution)/shard_map/ppermute | solution.py:61
  102.2 4.8 %collective-permute-start.30 = (bf16[4,64,128]{2,1,0:T(8,128)(2,1)S(1)}, bf16[4,64,128]{2,1,0:T(8,128)(2,1)S(1)}, u32[]{:S(2)}, u32[]{:S(2)}) collective-permute-start(bf16[4,64,128]{2,1,0:T(8,128)(2,1)S(1)} %fusion), channel_id=1, source_target_pairs={{0,16},{2,18},{4,20},{6,22},{8,24},{10,26},{12,28},{14,30},{16,0},... | collective-permute-start | bytes 196616 | tf_op jit(solution)/shard_map/ppermute | solution.py:70
  103.4 5.4 %collective-permute-start.31 = (bf16[4,64,128]{2,1,0:T(8,128)(2,1)S(1)}, bf16[4,64,128]{2,1,0:T(8,128)(2,1)S(1)}, u32[]{:S(2)}, u32[]{:S(2)}) collective-permute-start(bf16[4,64,128]{2,1,0:T(8,128)(2,1)S(1)} %fusion), channel_id=1, source_target_pairs={{0,24},{2,26},{4,28},{6,30},{8,16},{10,18},{12,20},{14,22},{16,8},... | collective-permute-start | bytes 196616 | tf_op jit(solution)/shard_map/ppermute | solution.py:70
  105.0 4.1 %collective-permute-start.29 = (bf16[4,64,128]{2,1,0:T(8,128)(2,1)S(1)}, bf16[4,64,128]{2,1,0:T(8,128)(2,1)S(1)}, u32[]{:S(2)}, u32[]{:S(2)}) collective-permute-start(bf16[4,64,128]{2,1,0:T(8,128)(2,1)S(1)} %fusion), channel_id=1, source_target_pairs={{0,8},{2,10},{4,12},{6,14},{8,0},{10,2},{12,4},{14,6},{16,24},{18,... | collective-permute-start | bytes 196616 | tf_op jit(solution)/shard_map/ppermute | solution.py:70
  109.2 3.2 %collective-permute-start.32 = (bf16[4,64,128]{2,1,0:T(8,128)(2,1)S(1)}, bf16[4,64,128]{2,1,0:T(8,128)(2,1)S(1)}, u32[]{:S(2)}, u32[]{:S(2)}) collective-permute-start(bf16[4,64,128]{2,1,0:T(8,128)(2,1)S(1)} %get-tuple-element.59), channel_id=1, source_target_pairs={{0,4},{2,6},{4,0},{6,2},{8,12},{10,14},{12,8},{14,10},{16,20},{18,... | collective-permute-start | bytes 196616 | tf_op jit(solution)/shard_map/ppermute | solution.py:47
  112.4 5.1 %collective-permute-start.33 = (bf16[8,64,128]{2,1,0:T(8,128)(2,1)S(1)}, bf16[8,64,128]{2,1,0:T(8,128)(2,1)S(1)}, u32[]{:S(2)}, u32[]{:S(2)}) collective-permute-start(bf16[8,64,128]{2,1,0:T(8,128)(2,1)S(1)} %pad_maximum_fusion.4), channel_id=1, source_target_pairs={{0,2},{2,0},{4,6},{6,4},{8,10},{10,8},{12,14},{14,12},{16,18},{18,... | collective-permute-start | bytes 393224 | tf_op jit(solution)/shard_map/ppermute | solution.py:47
  117.7 2.8 %collective-permute-start.34 = (f32[64,64]{1,0:T(8,128)S(1)}, f32[64,64]{1,0:T(8,128)S(1)}, u32[]{:S(2)}, u32[]{:S(2)}) collective-permute-start(f32[64,64]{1,0:T(8,128)S(1)} %gram.3.ga_ref), channel_id=1, source_target_pairs={{0,1},{1,0},{2,3},{3,2},{4,5},{5,4},{6,7},{7,6},{8,9},{9,8},{10,11... | collective-permute-start | bytes 49160 | tf_op jit(solution)/shard_map/ppermute | solution.py:417
  (5 other events, 18.6 us)

commit v5 on v4

--- a/solution.py
+++ b/solution.py
@@ -102,7 +102,7 @@
     tile = vals_ref.shape[1]
     rank = bq_ref.shape[1] // 2
     count = slot_ref[2, 0]
-    group = math.gcd(vals_ref.shape[0], 32)
+    group = math.gcd(vals_ref.shape[0], 64)
 
     def body(i, carry):
         for j in range(group):

time: 128 us -> 128 us (level)
  waiting for transfers between devices: 50.7 us -> 52.7 us
  starting transfers between devices: 44 us -> 42.3 us
  transfers between devices with their start and end apart: 35 -> 35, of which waited for: 31 -> 32; matrix products, arithmetic and copies ran while one was open for 1% -> 1% of each run, Pallas kernels for 6% -> 6%
where the time goes in v5:
time: 128 us; the launch traced here: 127 us
  waiting for transfers between devices  52.7 us (41%)
  starting transfers between devices  42.3 us (33%)
  Pallas kernels  26.1 us (20%)
  other arithmetic  2.45 us (2%)
  between operations  1.86 us (1%)
    pallas_call x19, Pallas kernels, call(): pl.pallas_call(kernel, out_shape=outs, in_specs=[SMEM] * smem + [pl.Block...  26.1 us
    ppermute x9, starting transfers between devices, gather_blocks(): got.append(lax.ppermute(held, axis, xor_pairs(size, k << at)))  14.3 us
    ppermute x6, waiting for transfers between devices, reduce_blocks(): lax.ppermute(mine, axis, xor_pairs(size, k << at))  13.3 us
    ppermute x10, waiting for transfers between devices, over_users(): terms.append(lax.ppermute(part, 'user', xor_pairs(n_user, k << at)))  11.9 us
    ppermute x10, starting transfers between devices, over_users(): terms.append(lax.ppermute(part, 'user', xor_pairs(n_user, k << at)))  11.2 us
    ppermute x6, waiting for transfers between devices, across(): other = lax.ppermute(mine, 'item', xor_pairs(n_item, bit))  9.71 us
    ppermute x9, waiting for transfers between devices, gather_blocks(): got.append(lax.ppermute(held, axis, xor_pairs(size, k << at)))  9.69 us
    ppermute x2, waiting for transfers between devices, reduce_blocks(): lax.ppermute(pieces[k].astype(kind), axis, xor_pairs(size, k << at))  7.61 us
  transfers between devices with their start and end apart: 35, of which 32 were waited for; matrix products, arithmetic and copies ran while one was open for 1% of the time, Pallas kernels for 6%

profile of v5, /device:TPU:29, one launch (start us, length us, event | category | flops | bytes accessed | tf_op | source)
XLA Modules:
  0.0 126.6 jit_solution(17871594320749987452)
XLA Ops:
  2.7 2.2 %collective-permute-start = (bf16[1,128,128]{2,1,0:T(8,128)(2,1)S(1)}, bf16[1,128,128]{2,1,0:T(8,128)(2,1)S(1)}, u32[]{:S(2)}, u32[]{:S(2)}) collective-permute-start(bf16[1,128,128]{2,1,0:T(8,128)(2,1)S(1)} %bitcast.16), channel_id=1, source_target_pairs={{0,8},{2,10},{4,12},{6,14},{8,0},{10,2},{12,4},{14,6},{16,24},{18,... | collective-permute-start | bytes 98312 | tf_op jit(solution)/shard_map/ppermute | solution.py:47
  10.5 2.9 %collective-permute-start.4 = (bf16[8,128,128]{2,1,0:T(8,128)(2,1)S(1)}, bf16[8,128,128]{2,1,0:T(8,128)(2,1)S(1)}, u32[]{:S(2)}, u32[]{:S(2)}) collective-permute-start(bf16[8,128,128]{2,1,0:T(8,128)(2,1)S(1)} %pad_maximum_fusion.1), channel_id=1, source_target_pairs={{0,2},{2,0},{4,6},{6,4},{8,10},{10,8},{12,14},{14,12},{16,18},{18,... | collective-permute-start | bytes 786440 | tf_op jit(solution)/shard_map/ppermute | solution.py:47
  14.7 3.1 %resid_y.1 = (bf16[2048,2048]{1,0:T(8,128)(2,1)S(1)}, f32[64,512]{1,0:T(8,128)S(1)}) custom-call(s32[3,128]{1,0:T(4,128)S(1)} %add_add_fusion.2.slot_ref.slot_any, bf16[128,128,128]{2,1,0:T(8,128)(2,1)S(1)} %bitcast.12, bf16[2048,64]{1,0:T(8,128)(2,1)S(1)} %get-tuple-element.38.at_ref, ...), custom_call_target="tpu_custom_call", output_to_operand_aliasing={{0}: (4, {})} | custom-call | bytes 65536 | tf_op jit(solution)/shard_map/resid_y/pallas_call | solution.py:440
  19.0 2.0 %y_omega.1.ya_ref = f32[64,1536]{1,0:T(8,128)S(1)} custom-call(bf16[16,128,128]{2,1,0:T(8,128)(2,1)S(1)} %constant_dynamic-update-slice_fusion.bq_ref, bf16[2048,2048]{1,0:T(8,128)(2,1)S(1)} %get-tuple-element.42.r_ref), custom_call_target="tpu_custom_call" | custom-call | flops 268435456 | bytes 65536 | tf_op jit(solution)/shard_map/y_omega/pallas_call | solution.py:440
  21.1 1.5 %collective-permute-done.5.yb_ref = f32[64,512]{1,0:T(8,128)S(1)} collective-permute-done((f32[64,512]{1,0:T(8,128)S(1)}, f32[64,512]{1,0:T(8,128)S(1)}, u32[]{:S(2)}, u32[]{:S(2)}) %collective-permute-start.5) | collective-permute-done | bytes 131104 | tf_op jit(solution)/shard_map/ppermute | solution.py:417
  24.0 1.5 %collective-permute-start.6 = (f32[64,64]{1,0:T(8,128)S(1)}, f32[64,64]{1,0:T(8,128)S(1)}, u32[]{:S(2)}, u32[]{:S(2)}) collective-permute-start(f32[64,64]{1,0:T(8,128)S(1)} %get-tuple-element.45), channel_id=1, source_target_pairs={{0,2},{2,0},{4,6},{6,4},{8,10},{10,8},{12,14},{14,12},{16,18},{18,... | collective-permute-start | bytes 49160 | tf_op jit(solution)/shard_map/ppermute | solution.py:491
  26.7 2.8 %collective-permute-done.7 = f32[64,64]{1,0:T(8,128)S(1)} collective-permute-done((f32[64,64]{1,0:T(8,128)S(1)}, f32[64,64]{1,0:T(8,128)S(1)}, u32[]{:S(2)}, u32[]{:S(2)}) %collective-permute-start.7) | collective-permute-done | bytes 16416 | tf_op jit(solution)/shard_map/ppermute | solution.py:491
  30.7 1.6 %collective-permute-start.9 = (f32[64,64]{1,0:T(8,128)S(1)}, f32[64,64]{1,0:T(8,128)S(1)}, u32[]{:S(2)}, u32[]{:S(2)}) collective-permute-start(f32[64,64]{1,0:T(8,128)S(1)} %add.83), channel_id=1, source_target_pairs={{0,16},{2,18},{4,20},{6,22},{8,24},{10,26},{12,28},{14,30},{16,0},... | collective-permute-start | bytes 49160 | tf_op jit(solution)/shard_map/ppermute | solution.py:491
  35.5 1.7 %y_hat.2.y_ref = f32[64,2048]{1,0:T(8,128)S(1)} custom-call(f32[64,64]{1,0:T(8,128)S(1)} %add_add_fusion.1.g_ref, f32[64,512]{1,0:T(8,128)S(1)} %get-tuple-element.46.y_0, f32[64,1536]{1,0:T(8,128)S(1)} %y_omega.1.ya_ref, f32[64,1536]{1,0:T(8,128)S(1)} %collective-permute-done.11.yb_ref), custom_call_target="tpu_custom_call" | custom-call | bytes 65536 | tf_op jit(solution)/shard_map/y_hat/pallas_call | solution.py:440
  38.0 2.7 %collective-permute-start.12 = (f32[8,64,128]{2,1,0:T(8,128)S(1)}, f32[8,64,128]{2,1,0:T(8,128)S(1)}, u32[]{:S(2)}, u32[]{:S(2)}) collective-permute-start(f32[8,64,128]{2,1,0:T(8,128)S(1)} %z_far.2), channel_id=1, source_target_pairs={{0,2},{2,0},{4,6},{6,4},{8,10},{10,8},{12,14},{14,12},{16,18},{18,... | collective-permute-start | bytes 786440 | tf_op jit(solution)/shard_map/ppermute | solution.py:54
  42.0 4.7 %collective-permute-done.13 = f32[4,64,128]{2,1,0:T(8,128)S(1)} collective-permute-done((f32[4,64,128]{2,1,0:T(8,128)S(1)}, f32[4,64,128]{2,1,0:T(8,128)S(1)}, u32[]{:S(2)}, u32[]{:S(2)}) %collective-permute-start.13) | collective-permute-done | bytes 131104 | tf_op jit(solution)/shard_map/ppermute | solution.py:61
  47.5 2.0 %collective-permute-start.16 = (f32[4,64,128]{2,1,0:T(8,128)S(1)}, f32[4,64,128]{2,1,0:T(8,128)S(1)}, u32[]{:S(2)}, u32[]{:S(2)}) collective-permute-start(f32[4,64,128]{2,1,0:T(8,128)S(1)} %slice_add_fusion.1), channel_id=1, source_target_pairs={{0,24},{2,26},{4,28},{6,30},{8,16},{10,18},{12,20},{14,22},{16,8},... | collective-permute-start | bytes 393224 | tf_op jit(solution)/shard_map/ppermute | solution.py:70
  49.5 8.7 %collective-permute-done.15 = f32[4,64,128]{2,1,0:T(8,128)S(1)} collective-permute-done((f32[4,64,128]{2,1,0:T(8,128)S(1)}, f32[4,64,128]{2,1,0:T(8,128)S(1)}, u32[]{:S(2)}, u32[]{:S(2)}) %collective-permute-start.15) | collective-permute-done | bytes 131104 | tf_op jit(solution)/shard_map/ppermute | solution.py:70
  59.1 3.7 %collective-permute-done.17 = f32[4,64,128]{2,1,0:T(8,128)S(1)} collective-permute-done((f32[4,64,128]{2,1,0:T(8,128)S(1)}, f32[4,64,128]{2,1,0:T(8,128)S(1)}, u32[]{:S(2)}, u32[]{:S(2)}) %collective-permute-start.17) | collective-permute-done | bytes 131104 | tf_op jit(solution)/shard_map/ppermute | solution.py:47
  62.8 2.9 %collective-permute-start.18 = (f32[8,64,128]{2,1,0:T(8,128)S(1)}, f32[8,64,128]{2,1,0:T(8,128)S(1)}, u32[]{:S(2)}, u32[]{:S(2)}) collective-permute-start(f32[8,64,128]{2,1,0:T(8,128)S(1)} %pad_maximum_fusion.2), channel_id=1, source_target_pairs={{0,2},{2,0},{4,6},{6,4},{8,10},{10,8},{12,14},{14,12},{16,18},{18,... | collective-permute-start | bytes 786440 | tf_op jit(solution)/shard_map/ppermute | solution.py:47
  67.8 2.5 %collective-permute-done.19.gb_ref = f32[64,64]{1,0:T(8,128)S(1)} collective-permute-done((f32[64,64]{1,0:T(8,128)S(1)}, f32[64,64]{1,0:T(8,128)S(1)}, u32[]{:S(2)}, u32[]{:S(2)}) %collective-permute-start.19) | collective-permute-done | bytes 16416 | tf_op jit(solution)/shard_map/ppermute | solution.py:417
  70.3 1.8 %q.1.q_ref = bf16[16,64,128]{2,1,0:T(8,128)(2,1)S(1)} custom-call(f32[64,64]{1,0:T(8,128)S(1)} %gram.2.ga_ref, f32[64,64]{1,0:T(8,128)S(1)} %collective-permute-done.19.gb_ref, f32[16,64,128]{2,1,0:T(8,128)S(1)} %pad_maximum_fusion.z_ref), custom_call_target="tpu_custom_call" | custom-call | bytes 65536 | tf_op jit(solution)/shard_map/q/pallas_call | solution.py:440
  72.1 1.4 %y_first.1.ya_ref = bf16[64,1024]{1,0:T(8,128)(2,1)S(1)} custom-call(bf16[16,64,128]{2,1,0:T(8,128)(2,1)S(1)} %q.1.q_ref, bf16[2048,2048]{1,0:T(8,128)(2,1)S(1)} %get-tuple-element.42.r_ref), custom_call_target="tpu_custom_call" | custom-call | flops 268435456 | bytes 65536 | tf_op jit(solution)/shard_map/y_first/pallas_call | solution.py:440
  73.8 1.4 %y_second.1.ya_ref = bf16[64,1024]{1,0:T(8,128)(2,1)S(1)} custom-call(bf16[16,64,128]{2,1,0:T(8,128)(2,1)S(1)} %q.1.q_ref, bf16[2048,2048]{1,0:T(8,128)(2,1)S(1)} %get-tuple-element.42.r_ref), custom_call_target="tpu_custom_call" | custom-call | flops 268435456 | bytes 65536 | tf_op jit(solution)/shard_map/y_second/pallas_call | solution.py:440
  77.8 2.7 %collective-permute-done.20.yb_ref = bf16[64,1024]{1,0:T(8,128)(2,1)S(1)} collective-permute-done((bf16[64,1024]{1,0:T(8,128)(2,1)S(1)}, bf16[64,1024]{1,0:T(8,128)(2,1)S(1)}, u32[]{:S(2)}, u32[]{:S(2)}) %collective-permute-start.20) | collective-permute-done | bytes 131104 | tf_op jit(solution)/shard_map/ppermute | solution.py:417
  80.9 2.2 %collective-permute-start.22 = (f32[64,64]{1,0:T(8,128)S(1)}, f32[64,64]{1,0:T(8,128)S(1)}, u32[]{:S(2)}, u32[]{:S(2)}) collective-permute-start(f32[64,64]{1,0:T(8,128)S(1)} %get-tuple-element.49), channel_id=1, source_target_pairs={{0,2},{2,0},{4,6},{6,4},{8,10},{10,8},{12,14},{14,12},{16,18},{18,... | collective-permute-start | bytes 49160 | tf_op jit(solution)/shard_map/ppermute | solution.py:491
  84.1 2.6 %collective-permute-done.23 = f32[64,64]{1,0:T(8,128)S(1)} collective-permute-done((f32[64,64]{1,0:T(8,128)S(1)}, f32[64,64]{1,0:T(8,128)S(1)}, u32[]{:S(2)}, u32[]{:S(2)}) %collective-permute-start.23) | collective-permute-done | bytes 16416 | tf_op jit(solution)/shard_map/ppermute | solution.py:491
  87.7 1.9 %collective-permute-start.25 = (f32[64,64]{1,0:T(8,128)S(1)}, f32[64,64]{1,0:T(8,128)S(1)}, u32[]{:S(2)}, u32[]{:S(2)}) collective-permute-start(f32[64,64]{1,0:T(8,128)S(1)} %add.93), channel_id=1, source_target_pairs={{0,16},{2,18},{4,20},{6,22},{8,24},{10,26},{12,28},{14,30},{16,0},... | collective-permute-start | bytes 49160 | tf_op jit(solution)/shard_map/ppermute | solution.py:491
  92.7 1.7 %y_hat.3.y_ref = f32[64,2048]{1,0:T(8,128)S(1)} custom-call(f32[64,64]{1,0:T(8,128)S(1)} %add_add_fusion.g_ref, f32[64,1024]{1,0:T(8,128)S(1)} %get-tuple-element.50.y_0, f32[64,1024]{1,0:T(8,128)S(1)} %get-tuple-element.51.y_1), custom_call_target="tpu_custom_call" | custom-call | bytes 65536 | tf_op jit(solution)/shard_map/y_hat/pallas_call | solution.py:440
  95.2 3.0 %collective-permute-start.27 = (bf16[8,64,128]{2,1,0:T(8,128)(2,1)S(1)}, bf16[8,64,128]{2,1,0:T(8,128)(2,1)S(1)}, u32[]{:S(2)}, u32[]{:S(2)}) collective-permute-start(bf16[8,64,128]{2,1,0:T(8,128)(2,1)S(1)} %z_far.3), channel_id=1, source_target_pairs={{0,2},{2,0},{4,6},{6,4},{8,10},{10,8},{12,14},{14,12},{16,18},{18,... | collective-permute-start | bytes 393224 | tf_op jit(solution)/shard_map/ppermute | solution.py:54
  99.5 2.9 %collective-permute-done.28 = bf16[4,64,128]{2,1,0:T(8,128)(2,1)S(1)} collective-permute-done((bf16[4,64,128]{2,1,0:T(8,128)(2,1)S(1)}, bf16[4,64,128]{2,1,0:T(8,128)(2,1)S(1)}, u32[]{:S(2)}, u32[]{:S(2)}) %collective-permute-start.28) | collective-permute-done | bytes 65568 | tf_op jit(solution)/shard_map/ppermute | solution.py:61
  103.1 2.1 %collective-permute-start.31 = (bf16[4,64,128]{2,1,0:T(8,128)(2,1)S(1)}, bf16[4,64,128]{2,1,0:T(8,128)(2,1)S(1)}, u32[]{:S(2)}, u32[]{:S(2)}) collective-permute-start(bf16[4,64,128]{2,1,0:T(8,128)(2,1)S(1)} %fusion), channel_id=1, source_target_pairs={{0,24},{2,26},{4,28},{6,30},{8,16},{10,18},{12,20},{14,22},{16,8},... | collective-permute-start | bytes 196616 | tf_op jit(solution)/shard_map/ppermute | solution.py:70
  105.2 2.0 %collective-permute-done.30 = bf16[4,64,128]{2,1,0:T(8,128)(2,1)S(1)} collective-permute-done((bf16[4,64,128]{2,1,0:T(8,128)(2,1)S(1)}, bf16[4,64,128]{2,1,0:T(8,128)(2,1)S(1)}, u32[]{:S(2)}, u32[]{:S(2)}) %collective-permute-start.30) | collective-permute-done | bytes 65568 | tf_op jit(solution)/shard_map/ppermute | solution.py:70
  111.0 1.5 %collective-permute-done.32 = bf16[4,64,128]{2,1,0:T(8,128)(2,1)S(1)} collective-permute-done((bf16[4,64,128]{2,1,0:T(8,128)(2,1)S(1)}, bf16[4,64,128]{2,1,0:T(8,128)(2,1)S(1)}, u32[]{:S(2)}, u32[]{:S(2)}) %collective-permute-start.32) | collective-permute-done | bytes 65568 | tf_op jit(solution)/shard_map/ppermute | solution.py:47
  112.5 4.0 %collective-permute-start.33 = (bf16[8,64,128]{2,1,0:T(8,128)(2,1)S(1)}, bf16[8,64,128]{2,1,0:T(8,128)(2,1)S(1)}, u32[]{:S(2)}, u32[]{:S(2)}) collective-permute-start(bf16[8,64,128]{2,1,0:T(8,128)(2,1)S(1)} %pad_maximum_fusion.4), channel_id=1, source_target_pairs={{0,2},{2,0},{4,6},{6,4},{8,10},{10,8},{12,14},{14,12},{16,18},{18,... | collective-permute-start | bytes 393224 | tf_op jit(solution)/shard_map/ppermute | solution.py:47
  118.4 2.1 %collective-permute-done.34.gb_ref = f32[64,64]{1,0:T(8,128)S(1)} collective-permute-done((f32[64,64]{1,0:T(8,128)S(1)}, f32[64,64]{1,0:T(8,128)S(1)}, u32[]{:S(2)}, u32[]{:S(2)}) %collective-permute-start.34) | collective-permute-done | bytes 16416 | tf_op jit(solution)/shard_map/ppermute | solution.py:417
  120.5 5.9 %loss.1 = (f32[64,128]{1,0:T(8,128)}, f32[128,128]{1,0:T(8,128)}) custom-call(s32[3,128]{1,0:T(4,128)S(1)} %add_add_fusion.2.slot_ref.slot_any, f32[64,64]{1,0:T(8,128)S(1)} %gram.3.ga_ref, f32[64,64]{1,0:T(8,128)S(1)} %collective-permute-done.34.gb_ref, bf16[16,64,128]{2,1,0:T(8,128)(2,1)S(1)} %constant_dynamic-update-slice_fusion.2.z_ref, ...), custom_call_target="tpu_custom_call" | custom-call | bytes 65536 | tf_op jit(solution)/shard_map/loss/pallas_call | solution.py:440
  (95 shorter events, 39.1 us)
Async XLA Ops:
  1.4 4.6 %collective-permute-start.2 = (bf16[1,128,128]{2,1,0:T(8,128)(2,1)S(1)}, bf16[1,128,128]{2,1,0:T(8,128)(2,1)S(1)}, u32[]{:S(2)}, u32[]{:S(2)}) collective-permute-start(bf16[1,128,128]{2,1,0:T(8,128)(2,1)S(1)} %bitcast.14), channel_id=1, source_target_pairs={{0,24},{2,26},{4,28},{6,30},{8,16},{10,18},{12,20},{14,22},{16,8},... | collective-permute-start | bytes 98312 | tf_op jit(solution)/shard_map/ppermute | solution.py:47
  1.4 4.6 %collective-permute-start.1 = (bf16[1,128,128]{2,1,0:T(8,128)(2,1)S(1)}, bf16[1,128,128]{2,1,0:T(8,128)(2,1)S(1)}, u32[]{:S(2)}, u32[]{:S(2)}) collective-permute-start(bf16[1,128,128]{2,1,0:T(8,128)(2,1)S(1)} %bitcast.15), channel_id=1, source_target_pairs={{0,16},{2,18},{4,20},{6,22},{8,24},{10,26},{12,28},{14,30},{16,0},... | collective-permute-start | bytes 98312 | tf_op jit(solution)/shard_map/ppermute | solution.py:47
  2.7 3.9 %collective-permute-start = (bf16[1,128,128]{2,1,0:T(8,128)(2,1)S(1)}, bf16[1,128,128]{2,1,0:T(8,128)(2,1)S(1)}, u32[]{:S(2)}, u32[]{:S(2)}) collective-permute-start(bf16[1,128,128]{2,1,0:T(8,128)(2,1)S(1)} %bitcast.16), channel_id=1, source_target_pairs={{0,8},{2,10},{4,12},{6,14},{8,0},{10,2},{12,4},{14,6},{16,24},{18,... | collective-permute-start | bytes 98312 | tf_op jit(solution)/shard_map/ppermute | solution.py:47
  6.6 3.9 %collective-permute-start.3 = (bf16[4,128,128]{2,1,0:T(8,128)(2,1)S(1)}, bf16[4,128,128]{2,1,0:T(8,128)(2,1)S(1)}, u32[]{:S(2)}, u32[]{:S(2)}) collective-permute-start(bf16[4,128,128]{2,1,0:T(8,128)(2,1)S(1)} %pad_maximum_fusion.3), channel_id=1, source_target_pairs={{0,4},{2,6},{4,0},{6,2},{8,12},{10,14},{12,8},{14,10},{16,20},{18,... | collective-permute-start | bytes 393224 | tf_op jit(solution)/shard_map/ppermute | solution.py:47
  10.5 4.1 %collective-permute-start.4 = (bf16[8,128,128]{2,1,0:T(8,128)(2,1)S(1)}, bf16[8,128,128]{2,1,0:T(8,128)(2,1)S(1)}, u32[]{:S(2)}, u32[]{:S(2)}) collective-permute-start(bf16[8,128,128]{2,1,0:T(8,128)(2,1)S(1)} %pad_maximum_fusion.1), channel_id=1, source_target_pairs={{0,2},{2,0},{4,6},{6,4},{8,10},{10,8},{12,14},{14,12},{16,18},{18,... | collective-permute-start | bytes 786440 | tf_op jit(solution)/shard_map/ppermute | solution.py:47
  17.8 4.8 %collective-permute-start.5 = (f32[64,512]{1,0:T(8,128)S(1)}, f32[64,512]{1,0:T(8,128)S(1)}, u32[]{:S(2)}, u32[]{:S(2)}) collective-permute-start(f32[64,512]{1,0:T(8,128)S(1)} %get-tuple-element.43.ya_ref), channel_id=1, source_target_pairs={{0,1},{1,0},{2,3},{3,2},{4,5},{5,4},{6,7},{7,6},{8,9},{9,8},{10,11... | collective-permute-start | bytes 393224 | tf_op jit(solution)/shard_map/ppermute | solution.py:417
  22.6 12.9 %collective-permute-start.11 = (f32[64,1536]{1,0:T(8,128)S(1)}, f32[64,1536]{1,0:T(8,128)S(1)}, u32[]{:S(2)}, u32[]{:S(2)}) collective-permute-start(f32[64,1536]{1,0:T(8,128)S(1)} %y_omega.1.ya_ref), channel_id=1, source_target_pairs={{0,1},{1,0},{2,3},{3,2},{4,5},{5,4},{6,7},{7,6},{8,9},{9,8},{10,11... | collective-permute-start | bytes 1179656 | tf_op jit(solution)/shard_map/ppermute | solution.py:417
  26.4 3.1 %collective-permute-start.7 = (f32[64,64]{1,0:T(8,128)S(1)}, f32[64,64]{1,0:T(8,128)S(1)}, u32[]{:S(2)}, u32[]{:S(2)}) collective-permute-start(f32[64,64]{1,0:T(8,128)S(1)} %add.82), channel_id=1, source_target_pairs={{0,4},{2,6},{4,0},{6,2},{8,12},{10,14},{12,8},{14,10},{16,20},{18,... | collective-permute-start | bytes 49160 | tf_op jit(solution)/shard_map/ppermute | solution.py:491
  29.5 4.6 %collective-permute-start.10 = (f32[64,64]{1,0:T(8,128)S(1)}, f32[64,64]{1,0:T(8,128)S(1)}, u32[]{:S(2)}, u32[]{:S(2)}) collective-permute-start(f32[64,64]{1,0:T(8,128)S(1)} %add.83), channel_id=1, source_target_pairs={{0,24},{2,26},{4,28},{6,30},{8,16},{10,18},{12,20},{14,22},{16,8},... | collective-permute-start | bytes 49160 | tf_op jit(solution)/shard_map/ppermute | solution.py:491
  30.7 4.0 %collective-permute-start.9 = (f32[64,64]{1,0:T(8,128)S(1)}, f32[64,64]{1,0:T(8,128)S(1)}, u32[]{:S(2)}, u32[]{:S(2)}) collective-permute-start(f32[64,64]{1,0:T(8,128)S(1)} %add.83), channel_id=1, source_target_pairs={{0,16},{2,18},{4,20},{6,22},{8,24},{10,26},{12,28},{14,30},{16,0},... | collective-permute-start | bytes 49160 | tf_op jit(solution)/shard_map/ppermute | solution.py:491
  32.4 3.1 %collective-permute-start.8 = (f32[64,64]{1,0:T(8,128)S(1)}, f32[64,64]{1,0:T(8,128)S(1)}, u32[]{:S(2)}, u32[]{:S(2)}) collective-permute-start(f32[64,64]{1,0:T(8,128)S(1)} %add.83), channel_id=1, source_target_pairs={{0,8},{2,10},{4,12},{6,14},{8,0},{10,2},{12,4},{14,6},{16,24},{18,... | collective-permute-start | bytes 49160 | tf_op jit(solution)/shard_map/ppermute | solution.py:491
  38.0 3.8 %collective-permute-start.12 = (f32[8,64,128]{2,1,0:T(8,128)S(1)}, f32[8,64,128]{2,1,0:T(8,128)S(1)}, u32[]{:S(2)}, u32[]{:S(2)}) collective-permute-start(f32[8,64,128]{2,1,0:T(8,128)S(1)} %z_far.2), channel_id=1, source_target_pairs={{0,2},{2,0},{4,6},{6,4},{8,10},{10,8},{12,14},{14,12},{16,18},{18,... | collective-permute-start | bytes 786440 | tf_op jit(solution)/shard_map/ppermute | solution.py:54
  41.9 4.8 %collective-permute-start.13 = (f32[4,64,128]{2,1,0:T(8,128)S(1)}, f32[4,64,128]{2,1,0:T(8,128)S(1)}, u32[]{:S(2)}, u32[]{:S(2)}) collective-permute-start(f32[4,64,128]{2,1,0:T(8,128)S(1)} %slice.114), channel_id=1, source_target_pairs={{0,4},{2,6},{4,0},{6,2},{8,12},{10,14},{12,8},{14,10},{16,20},{18,... | collective-permute-start | bytes 393224 | tf_op jit(solution)/shard_map/ppermute | solution.py:61
  46.7 11.5 %collective-permute-start.15 = (f32[4,64,128]{2,1,0:T(8,128)S(1)}, f32[4,64,128]{2,1,0:T(8,128)S(1)}, u32[]{:S(2)}, u32[]{:S(2)}) collective-permute-start(f32[4,64,128]{2,1,0:T(8,128)S(1)} %slice_add_fusion.1), channel_id=1, source_target_pairs={{0,16},{2,18},{4,20},{6,22},{8,24},{10,26},{12,28},{14,30},{16,0},... | collective-permute-start | bytes 393224 | tf_op jit(solution)/shard_map/ppermute | solution.py:70
  47.5 10.8 %collective-permute-start.16 = (f32[4,64,128]{2,1,0:T(8,128)S(1)}, f32[4,64,128]{2,1,0:T(8,128)S(1)}, u32[]{:S(2)}, u32[]{:S(2)}) collective-permute-start(f32[4,64,128]{2,1,0:T(8,128)S(1)} %slice_add_fusion.1), channel_id=1, source_target_pairs={{0,24},{2,26},{4,28},{6,30},{8,16},{10,18},{12,20},{14,22},{16,8},... | collective-permute-start | bytes 393224 | tf_op jit(solution)/shard_map/ppermute | solution.py:70
  49.5 9.3 %collective-permute-start.14 = (f32[4,64,128]{2,1,0:T(8,128)S(1)}, f32[4,64,128]{2,1,0:T(8,128)S(1)}, u32[]{:S(2)}, u32[]{:S(2)}) collective-permute-start(f32[4,64,128]{2,1,0:T(8,128)S(1)} %slice_add_fusion.1), channel_id=1, source_target_pairs={{0,8},{2,10},{4,12},{6,14},{8,0},{10,2},{12,4},{14,6},{16,24},{18,... | collective-permute-start | bytes 393224 | tf_op jit(solution)/shard_map/ppermute | solution.py:70
  58.9 3.9 %collective-permute-start.17 = (f32[4,64,128]{2,1,0:T(8,128)S(1)}, f32[4,64,128]{2,1,0:T(8,128)S(1)}, u32[]{:S(2)}, u32[]{:S(2)}) collective-permute-start(f32[4,64,128]{2,1,0:T(8,128)S(1)} %fusion.2), channel_id=1, source_target_pairs={{0,4},{2,6},{4,0},{6,2},{8,12},{10,14},{12,8},{14,10},{16,20},{18,... | collective-permute-start | bytes 393224 | tf_op jit(solution)/shard_map/ppermute | solution.py:47
  62.8 4.1 %collective-permute-start.18 = (f32[8,64,128]{2,1,0:T(8,128)S(1)}, f32[8,64,128]{2,1,0:T(8,128)S(1)}, u32[]{:S(2)}, u32[]{:S(2)}) collective-permute-start(f32[8,64,128]{2,1,0:T(8,128)S(1)} %pad_maximum_fusion.2), channel_id=1, source_target_pairs={{0,2},{2,0},{4,6},{6,4},{8,10},{10,8},{12,14},{14,12},{16,18},{18,... | collective-permute-start | bytes 786440 | tf_op jit(solution)/shard_map/ppermute | solution.py:47
  67.5 2.8 %collective-permute-start.19 = (f32[64,64]{1,0:T(8,128)S(1)}, f32[64,64]{1,0:T(8,128)S(1)}, u32[]{:S(2)}, u32[]{:S(2)}) collective-permute-start(f32[64,64]{1,0:T(8,128)S(1)} %gram.2.ga_ref), channel_id=1, source_target_pairs={{0,1},{1,0},{2,3},{3,2},{4,5},{5,4},{6,7},{7,6},{8,9},{9,8},{10,11... | collective-permute-start | bytes 49160 | tf_op jit(solution)/shard_map/ppermute | solution.py:417
  73.5 3.9 %collective-permute-start.21 = (bf16[64,1024]{1,0:T(8,128)(2,1)S(1)}, bf16[64,1024]{1,0:T(8,128)(2,1)S(1)}, u32[]{:S(2)}, u32[]{:S(2)}) collective-permute-start(bf16[64,1024]{1,0:T(8,128)(2,1)S(1)} %y_first.1.ya_ref), channel_id=1, source_target_pairs={{0,1},{1,0},{2,3},{3,2},{4,5},{5,4},{6,7},{7,6},{8,9},{9,8},{10,11... | collective-permute-start | bytes 393224 | tf_op jit(solution)/shard_map/ppermute | solution.py:417
  75.2 5.3 %collective-permute-start.20 = (bf16[64,1024]{1,0:T(8,128)(2,1)S(1)}, bf16[64,1024]{1,0:T(8,128)(2,1)S(1)}, u32[]{:S(2)}, u32[]{:S(2)}) collective-permute-start(bf16[64,1024]{1,0:T(8,128)(2,1)S(1)} %y_second.1.ya_ref), channel_id=1, source_target_pairs={{0,1},{1,0},{2,3},{3,2},{4,5},{5,4},{6,7},{7,6},{8,9},{9,8},{10,11... | collective-permute-start | bytes 393224 | tf_op jit(solution)/shard_map/ppermute | solution.py:417
  80.9 3.0 %collective-permute-start.22 = (f32[64,64]{1,0:T(8,128)S(1)}, f32[64,64]{1,0:T(8,128)S(1)}, u32[]{:S(2)}, u32[]{:S(2)}) collective-permute-start(f32[64,64]{1,0:T(8,128)S(1)} %get-tuple-element.49), channel_id=1, source_target_pairs={{0,2},{2,0},{4,6},{6,4},{8,10},{10,8},{12,14},{14,12},{16,18},{18,... | collective-permute-start | bytes 49160 | tf_op jit(solution)/shard_map/ppermute | solution.py:491
  86.7 4.6 %collective-permute-start.26 = (f32[64,64]{1,0:T(8,128)S(1)}, f32[64,64]{1,0:T(8,128)S(1)}, u32[]{:S(2)}, u32[]{:S(2)}) collective-permute-start(f32[64,64]{1,0:T(8,128)S(1)} %add.93), channel_id=1, source_target_pairs={{0,24},{2,26},{4,28},{6,30},{8,16},{10,18},{12,20},{14,22},{16,8},... | collective-permute-start | bytes 49160 | tf_op jit(solution)/shard_map/ppermute | solution.py:491
  87.7 3.9 %collective-permute-start.25 = (f32[64,64]{1,0:T(8,128)S(1)}, f32[64,64]{1,0:T(8,128)S(1)}, u32[]{:S(2)}, u32[]{:S(2)}) collective-permute-start(f32[64,64]{1,0:T(8,128)S(1)} %add.93), channel_id=1, source_target_pairs={{0,16},{2,18},{4,20},{6,22},{8,24},{10,26},{12,28},{14,30},{16,0},... | collective-permute-start | bytes 49160 | tf_op jit(solution)/shard_map/ppermute | solution.py:491
  89.6 3.1 %collective-permute-start.24 = (f32[64,64]{1,0:T(8,128)S(1)}, f32[64,64]{1,0:T(8,128)S(1)}, u32[]{:S(2)}, u32[]{:S(2)}) collective-permute-start(f32[64,64]{1,0:T(8,128)S(1)} %add.93), channel_id=1, source_target_pairs={{0,8},{2,10},{4,12},{6,14},{8,0},{10,2},{12,4},{14,6},{16,24},{18,... | collective-permute-start | bytes 49160 | tf_op jit(solution)/shard_map/ppermute | solution.py:491
  95.2 4.0 %collective-permute-start.27 = (bf16[8,64,128]{2,1,0:T(8,128)(2,1)S(1)}, bf16[8,64,128]{2,1,0:T(8,128)(2,1)S(1)}, u32[]{:S(2)}, u32[]{:S(2)}) collective-permute-start(bf16[8,64,128]{2,1,0:T(8,128)(2,1)S(1)} %z_far.3), channel_id=1, source_target_pairs={{0,2},{2,0},{4,6},{6,4},{8,10},{10,8},{12,14},{14,12},{16,18},{18,... | collective-permute-start | bytes 393224 | tf_op jit(solution)/shard_map/ppermute | solution.py:54
  99.2 3.2 %collective-permute-start.28 = (bf16[4,64,128]{2,1,0:T(8,128)(2,1)S(1)}, bf16[4,64,128]{2,1,0:T(8,128)(2,1)S(1)}, u32[]{:S(2)}, u32[]{:S(2)}) collective-permute-start(bf16[4,64,128]{2,1,0:T(8,128)(2,1)S(1)} %slice.144), channel_id=1, source_target_pairs={{0,4},{2,6},{4,0},{6,2},{8,12},{10,14},{12,8},{14,10},{16,20},{18,... | collective-permute-start | bytes 196616 | tf_op jit(solution)/shard_map/ppermute | solution.py:61
  102.4 4.8 %collective-permute-start.30 = (bf16[4,64,128]{2,1,0:T(8,128)(2,1)S(1)}, bf16[4,64,128]{2,1,0:T(8,128)(2,1)S(1)}, u32[]{:S(2)}, u32[]{:S(2)}) collective-permute-start(bf16[4,64,128]{2,1,0:T(8,128)(2,1)S(1)} %fusion), channel_id=1, source_target_pairs={{0,16},{2,18},{4,20},{6,22},{8,24},{10,26},{12,28},{14,30},{16,0},... | collective-permute-start | bytes 196616 | tf_op jit(solution)/shard_map/ppermute | solution.py:70
  103.1 5.1 %collective-permute-start.31 = (bf16[4,64,128]{2,1,0:T(8,128)(2,1)S(1)}, bf16[4,64,128]{2,1,0:T(8,128)(2,1)S(1)}, u32[]{:S(2)}, u32[]{:S(2)}) collective-permute-start(bf16[4,64,128]{2,1,0:T(8,128)(2,1)S(1)} %fusion), channel_id=1, source_target_pairs={{0,24},{2,26},{4,28},{6,30},{8,16},{10,18},{12,20},{14,22},{16,8},... | collective-permute-start | bytes 196616 | tf_op jit(solution)/shard_map/ppermute | solution.py:70
  105.2 4.0 %collective-permute-start.29 = (bf16[4,64,128]{2,1,0:T(8,128)(2,1)S(1)}, bf16[4,64,128]{2,1,0:T(8,128)(2,1)S(1)}, u32[]{:S(2)}, u32[]{:S(2)}) collective-permute-start(bf16[4,64,128]{2,1,0:T(8,128)(2,1)S(1)} %fusion), channel_id=1, source_target_pairs={{0,8},{2,10},{4,12},{6,14},{8,0},{10,2},{12,4},{14,6},{16,24},{18,... | collective-permute-start | bytes 196616 | tf_op jit(solution)/shard_map/ppermute | solution.py:70
  109.3 3.2 %collective-permute-start.32 = (bf16[4,64,128]{2,1,0:T(8,128)(2,1)S(1)}, bf16[4,64,128]{2,1,0:T(8,128)(2,1)S(1)}, u32[]{:S(2)}, u32[]{:S(2)}) collective-permute-start(bf16[4,64,128]{2,1,0:T(8,128)(2,1)S(1)} %get-tuple-element.59), channel_id=1, source_target_pairs={{0,4},{2,6},{4,0},{6,2},{8,12},{10,14},{12,8},{14,10},{16,20},{18,... | collective-permute-start | bytes 196616 | tf_op jit(solution)/shard_map/ppermute | solution.py:47
  112.5 5.0 %collective-permute-start.33 = (bf16[8,64,128]{2,1,0:T(8,128)(2,1)S(1)}, bf16[8,64,128]{2,1,0:T(8,128)(2,1)S(1)}, u32[]{:S(2)}, u32[]{:S(2)}) collective-permute-start(bf16[8,64,128]{2,1,0:T(8,128)(2,1)S(1)} %pad_maximum_fusion.4), channel_id=1, source_target_pairs={{0,2},{2,0},{4,6},{6,4},{8,10},{10,8},{12,14},{14,12},{16,18},{18,... | collective-permute-start | bytes 393224 | tf_op jit(solution)/shard_map/ppermute | solution.py:47
  (5 other events, 18.7 us)
